TPU v7x, 32 devices: a whole 2x2x4 slice. The times are simulated.
32 devices in a mesh: ev: 2 (over y), mem: 16 (over z, x, core).
Axes of the slice: x: 2, y: 2, z: 4, core: 2. Of those that a mesh axis runs over, the one named last changes fastest.
Arguments:
- memory: bfloat16 [8192, 512], P(('ev', 'mem')), may hold values from -24 to 24
- last_time: int32 [8192], P(('ev', 'mem')), may hold values from 0 to 499
- event_time: int32 [4096], P(('ev', 'mem')), may hold values from 500 to 999
- edge_features: bfloat16 [4096, 48], P(('ev', 'mem')), may hold values from -6 to 6
- update_slot: int32 [4096, 2], P(('ev', 'mem')), may hold values from 0 to 511, as said below
- update_serve: int32 [32, 512], P(('ev', 'mem')), may hold values from -1 to 255, as said below
- lookup_slot: int32 [4096, 7], P(('ev', 'mem')), may hold values from 0 to 1791, as said below
- lookup_serve: int32 [32, 1792], P(('ev', 'mem')), may hold values from -1 to 255, as said below
- neighbour_gap: int32 [4096, 10], P(('ev', 'mem')), may hold values from 0 to 999
- hub_node: int32 [32], P(('ev', 'mem')), may hold values from 0 to 255
- hub_choice: int32 [4096, 4], P(('ev', 'mem')), may hold values from 0 to 31
- time_freq: float32 [100], replicated, may hold values from 0.001 to 0.3
- time_phase: float32 [100], replicated, may hold values from -3.140625 to 3.140625
- gru_weight: bfloat16 [1684, 1536], P(None, 'ev'), may hold values from -0.1875 to 0.1875
- gru_bias: float32 [2, 1536], replicated, may hold values from -3 to 3
- query_weight: bfloat16 [612, 256], replicated, may hold values from -0.25 to 0.25
- keyval_weight: bfloat16 [612, 512], replicated, may hold values from -0.25 to 0.25
- output_weight: bfloat16 [768, 512], replicated, may hold values from -0.21875 to 0.21875
Outputs:
- new_memory: bfloat16 [8192, 512], P(('ev', 'mem'))
- embedding: bfloat16 [4096, 512], P(('ev', 'mem'))
Inputs may be any that keep to these rules, and one draw needn't show every extreme that they name: Within one device's events the values of update_slot are distinct; at most 16 of one device's endpoints go to one owner, and one owner, drawn from the seed, gets exactly 16 from every device. update_serve holds a local node exactly in the slots named by update_slot, -1 elsewhere; several slots may name the same node. Within one device's queries the values of lookup_slot are distinct; at most 56 of one device's lookups go to one owner, and one owner gets exactly 56 from every device. lookup_serve holds a local node exactly in the slots named by lookup_slot, -1 elsewhere.
All inputs are finite; a program needn't handle non-finite values.
Results may differ from a plain program's by a relative error of at most 0.011.
Values may be sent and summed in bfloat16 or wider, within the bound.
No kernel may reach another device: no remote copies, remote signals or barrier semaphores. Data moves between devices by JAX's collectives and lax.ppermute only.
A program may use at most 64 MiB of HBM per device.

v0:
```python
import jax
import jax.numpy as jnp
from jax import lax
from jax.sharding import PartitionSpec as P

HEADS = 2


def encode(gap, time_freq, time_phase):
    return jnp.cos(gap.astype(jnp.float32)[..., None] * time_freq + time_phase).astype(jnp.bfloat16)


def gru_update(pre_in, pre_hid, previous_mem, counts):
    mem_width = previous_mem.shape[1]
    reset_gate = jax.nn.sigmoid(pre_in[:, :mem_width] + pre_hid[:, :mem_width])
    update_gate = jax.nn.sigmoid(
        pre_in[:, mem_width : 2 * mem_width] + pre_hid[:, mem_width : 2 * mem_width]
    )
    candidate = jnp.tanh(pre_in[:, 2 * mem_width :] + reset_gate * pre_hid[:, 2 * mem_width :])
    previous = previous_mem.astype(jnp.float32)
    fresh = (1.0 - update_gate) * candidate + update_gate * previous
    return jnp.where(counts[:, None] > 0, fresh, previous).astype(jnp.bfloat16)


def local(
    memory,
    last_time,
    event_time,
    edge_features,
    update_slot,
    update_serve,
    lookup_slot,
    lookup_serve,
    neighbour_gap,
    hub_node,
    hub_choice,
    time_freq,
    time_phase,
    gru_weight,
    gru_bias,
    query_weight,
    keyval_weight,
    output_weight,
):
    ev_size = lax.axis_size("ev")
    mem_size = lax.axis_size("mem")
    node_count, mem_width = memory.shape
    event_count = event_time.shape[0]
    slots_update = update_serve[0]
    slot_total = slots_update.shape[0]
    cap_update = slot_total // (ev_size * mem_size)
    valid_update = slots_update >= 0
    safe_update = jnp.maximum(slots_update, 0)
    own_rows = jnp.where(valid_update[:, None], memory[safe_update], jnp.zeros((), jnp.bfloat16))
    own_times = last_time[safe_update]
    fetched_rows, fetched_times = (
        lax.all_to_all(
            lax.all_to_all(
                own_rows.reshape(ev_size, mem_size, cap_update, mem_width),
                "ev",
                split_axis=0,
                concat_axis=0,
                tiled=True,
            ),
            "mem",
            split_axis=1,
            concat_axis=1,
            tiled=True,
        ),
        lax.all_to_all(
            lax.all_to_all(
                own_times.reshape(ev_size, mem_size, cap_update),
                "ev",
                split_axis=0,
                concat_axis=0,
                tiled=True,
            ),
            "mem",
            split_axis=1,
            concat_axis=1,
            tiled=True,
        ),
    )
    flat_slots = update_slot.reshape(-1)
    endpoints = fetched_rows.reshape(slot_total, mem_width)[flat_slots].reshape(
        event_count, 2, mem_width
    )
    edge_pair = jnp.broadcast_to(
        edge_features[:, None, :], (event_count, 2, edge_features.shape[1])
    )
    partner = jnp.concatenate([endpoints[:, ::-1], edge_pair], axis=2)
    part_width = partner.shape[2]
    stamps = jnp.broadcast_to(event_time[:, None], (event_count, 2))
    out_rows = (
        jnp.zeros((slot_total, part_width), jnp.bfloat16)
        .at[flat_slots]
        .set(partner.reshape(-1, part_width))
    )
    out_stamps = jnp.zeros((slot_total,), jnp.int32).at[flat_slots].set(stamps.reshape(-1))
    arrived_rows, arrived_stamps = (
        lax.all_to_all(
            lax.all_to_all(
                out_rows.reshape(ev_size, mem_size, cap_update, part_width),
                "ev",
                split_axis=0,
                concat_axis=0,
                tiled=True,
            ),
            "mem",
            split_axis=1,
            concat_axis=1,
            tiled=True,
        ),
        lax.all_to_all(
            lax.all_to_all(
                out_stamps.reshape(ev_size, mem_size, cap_update),
                "ev",
                split_axis=0,
                concat_axis=0,
                tiled=True,
            ),
            "mem",
            split_axis=1,
            concat_axis=1,
            tiled=True,
        ),
    )
    partner_got = arrived_rows.reshape(slot_total, part_width)
    encoded = encode(arrived_stamps.reshape(slot_total) - own_times, time_freq, time_phase)
    received = jnp.concatenate(
        [own_rows, partner_got[:, :mem_width], encoded, partner_got[:, mem_width:]], axis=1
    )
    msg_width = received.shape[1]
    matches = jnp.arange(node_count, dtype=jnp.int32)[:, None] == slots_update[None, :]
    summed = jnp.dot(matches.astype(jnp.bfloat16), received, preferred_element_type=jnp.float32)
    counts = jnp.sum(matches.astype(jnp.float32), axis=1)
    averaged = (summed / jnp.maximum(counts, 1.0)[:, None]).astype(jnp.bfloat16)
    column_block = lax.all_gather(gru_weight, "ev", axis=1, tiled=True)
    from_message = jnp.dot(averaged, column_block[:msg_width], preferred_element_type=jnp.float32)
    from_memory = jnp.dot(memory, column_block[msg_width:], preferred_element_type=jnp.float32)
    pre_acts = jnp.stack([from_message, from_memory])
    new_memory = gru_update(pre_acts[0] + gru_bias[0], pre_acts[1] + gru_bias[1], memory, counts)
    hub_table = lax.all_gather(new_memory[hub_node], ("ev", "mem"), axis=0, tiled=True)
    slots_lookup = lookup_serve[0]
    lookup_total = slots_lookup.shape[0]
    cap_lookup = lookup_total // (ev_size * mem_size)
    valid_lookup = slots_lookup >= 0
    served_rows = jnp.where(
        valid_lookup[:, None], new_memory[jnp.maximum(slots_lookup, 0)], jnp.zeros((), jnp.bfloat16)
    )
    looked = lax.all_to_all(
        lax.all_to_all(
            served_rows.reshape(ev_size, mem_size, cap_lookup, mem_width),
            "ev",
            split_axis=0,
            concat_axis=0,
            tiled=True,
        ),
        "mem",
        split_axis=1,
        concat_axis=1,
        tiled=True,
    )
    routed = looked.reshape(lookup_total, mem_width)[lookup_slot.reshape(-1)].reshape(
        event_count, -1, mem_width
    )
    hub_count = hub_table.shape[0]
    pick_table = (
        hub_choice.reshape(-1)[:, None] == jnp.arange(hub_count, dtype=jnp.int32)[None, :]
    ).astype(jnp.bfloat16)
    hub_near = (
        jnp.dot(pick_table, hub_table, preferred_element_type=jnp.float32)
        .astype(jnp.bfloat16)
        .reshape(event_count, -1, mem_width)
    )
    self_row = routed[:, 0]
    neighbours = jnp.concatenate([routed[:, 1:], hub_near], axis=1)
    near_count = neighbours.shape[1]
    key_input = jnp.concatenate(
        [neighbours, encode(neighbour_gap, time_freq, time_phase)], axis=2
    ).reshape(event_count * near_count, -1)
    keyval = (
        jnp.dot(key_input, keyval_weight, preferred_element_type=jnp.float32)
        .astype(jnp.bfloat16)
        .reshape(event_count, near_count, -1)
    )
    att_width = query_weight.shape[1]
    head_size = att_width // HEADS
    self_enc = encode(jnp.zeros((event_count,), jnp.int32), time_freq, time_phase)
    queries = jnp.dot(
        jnp.concatenate([self_row, self_enc], axis=1),
        query_weight,
        preferred_element_type=jnp.float32,
    ).astype(jnp.bfloat16)
    query_heads = queries.reshape(event_count, HEADS, head_size)
    key_heads = keyval[:, :, :att_width].reshape(event_count, near_count, HEADS, head_size)
    value_heads = keyval[:, :, att_width:].reshape(event_count, near_count, HEADS, head_size)
    scores = jnp.einsum(
        "ehd,ekhd->ehk", query_heads, key_heads, preferred_element_type=jnp.float32
    ) * head_size ** (-0.5)
    scores = scores - jnp.max(scores, axis=2, keepdims=True)
    expo = jnp.exp(scores)
    prob = (expo / jnp.sum(expo, axis=2, keepdims=True)).astype(jnp.bfloat16)
    mixed = (
        jnp.einsum("ehk,ekhd->ehd", prob, value_heads, preferred_element_type=jnp.float32)
        .astype(jnp.bfloat16)
        .reshape(event_count, att_width)
    )
    embedding = jnp.dot(
        jnp.concatenate([mixed, self_row], axis=1),
        output_weight,
        preferred_element_type=jnp.float32,
    ).astype(jnp.bfloat16)
    return (new_memory, embedding)


def solution(mesh):
    return jax.shard_map(
        local,
        mesh=mesh,
        in_specs=(
            P(("ev", "mem"), None),
            P(("ev", "mem")),
            P(("ev", "mem")),
            P(("ev", "mem"), None),
            P(("ev", "mem"), None),
            P(("ev", "mem"), None),
            P(("ev", "mem"), None),
            P(("ev", "mem"), None),
            P(("ev", "mem"), None),
            P(("ev", "mem")),
            P(("ev", "mem"), None),
            P(),
            P(),
            P(None, "ev"),
            P(),
            P(),
            P(),
            P(),
        ),
        out_specs=(P(("ev", "mem"), None), P(("ev", "mem"), None)),
        check_vma=False,
    )
```

profile of v0, /device:TPU:0, one launch (start us, length us, event | category | flops | bytes accessed | tf_op | source)
XLA Modules:
  0.0 254.6 jit_solution(17817721390695751498)
XLA Ops:
  7.2 0.7 all-gather.3.cloned.1.call-update
  8.2 2.0 gather_fusion
  10.4 12.1 %all_to_all.40 = bf16[2,16,16,512]{3,2,1,0:T(8,128)(2,1)S(1)} all-to-all(bf16[2,16,16,512]{3,2,1,0:T(8,128)(2,1)S(1)} %broadcast_select_fusion.2), channel_id=1, replica_groups=mesh['ev'=2,'mem'=16] {'ev'}, dimensions={0} | all-to-all | bytes 1048576 | tf_op jit(solution)/shard_map/all_to_all | solution.py:58
  22.5 0.8 copy.75
  23.3 6.0 %all-to-all-start.1 = ((bf16[2,16,16,512]{3,2,0,1:T(8,128)(2,1)}), bf16[2,16,16,512]{3,2,0,1:T(8,128)(2,1)S(1)}, u32[]{:S(2)}, u32[]{:S(2)}) async-start(bf16[2,16,16,512]{3,2,0,1:T(8,128)(2,1)} %copy.75), calls=%async_computation.1 | async-start | bytes 1048576 | tf_op jit(solution)/shard_map/all_to_all | solution.py:57
  30.0 1.4 scatter_custom_fusion.1
  31.5 0.7 reshape.311
  32.3 11.5 %all-to-all-done.1 = bf16[2,16,16,512]{3,2,0,1:T(8,128)(2,1)S(1)} async-done(((bf16[2,16,16,512]{3,2,0,1:T(8,128)(2,1)}), bf16[2,16,16,512]{3,2,0,1:T(8,128)(2,1)S(1)}, u32[]{:S(2)}, u32[]{:S(2)}) %all-to-all-start.1) | async-done | bytes 524320 | tf_op jit(solution)/shard_map/all_to_all | solution.py:57
  43.8 3.2 %all-to-all-start.4 = ((s32[2,1,256]{2,1,0:T(1,128)}), s32[2,1,256]{2,1,0:T(1,128)S(1)}, u32[]{:S(2)}, u32[]{:S(2)}) async-start(s32[2,1,256]{2,1,0:T(1,128)} %reshape.311), calls=%async_computation.4 | async-start | bytes 4096 | tf_op jit(solution)/shard_map/all_to_all | solution.py:115
  47.1 1.2 gather_fusion.1
  48.4 1.4 rev.3
  50.4 2.5 scatter_custom_fusion
  52.9 3.5 %all-to-all-start.2 = ((bf16[2,16,16,560]{3,2,1,0:T(8,128)(2,1)}), bf16[2,16,16,560]{3,2,1,0:T(8,128)(2,1)S(1)}, u32[]{:S(2)}, u32[]{:S(2)}) async-start(bf16[2,16,16,560]{3,2,1,0:T(8,128)(2,1)} %bitcast.7), calls=%async_computation.2 | async-start | bytes 1310720 | tf_op jit(solution)/shard_map/all_to_all | solution.py:102
  56.5 0.5 broadcast.170
  57.0 0.7 reduce.16
  57.8 0.6 copy.80
  58.4 15.5 %all-to-all-done.2 = bf16[2,16,16,560]{3,2,1,0:T(8,128)(2,1)S(1)} async-done(((bf16[2,16,16,560]{3,2,1,0:T(8,128)(2,1)}), bf16[2,16,16,560]{3,2,1,0:T(8,128)(2,1)S(1)}, u32[]{:S(2)}, u32[]{:S(2)}) %all-to-all-start.2) | async-done | bytes 573472 | tf_op jit(solution)/shard_map/all_to_all | solution.py:102
  73.9 4.2 %all-to-all-start.5 = ((s32[2,16,16]{2,0,1:T(2,128)}), s32[2,16,16]{2,0,1:T(2,128)S(1)}, u32[]{:S(2)}, u32[]{:S(2)}) async-start(s32[2,16,16]{2,0,1:T(2,128)} %copy.80), calls=%async_computation.5 | async-start | bytes 32768 | tf_op jit(solution)/shard_map/all_to_all | solution.py:114
  78.1 0.9 copy.78
  79.1 5.5 %all-to-all-done.5 = s32[2,16,16]{2,0,1:T(2,128)S(1)} async-done(((s32[2,16,16]{2,0,1:T(2,128)}), s32[2,16,16]{2,0,1:T(2,128)S(1)}, u32[]{:S(2)}, u32[]{:S(2)}) %all-to-all-start.5) | async-done | bytes 2080 | tf_op jit(solution)/shard_map/all_to_all | solution.py:114
  84.6 3.8 %all-to-all-start.3 = ((bf16[2,16,16,560]{3,2,0,1:T(8,128)(2,1)}), bf16[2,16,16,560]{3,2,0,1:T(8,128)(2,1)S(1)}, u32[]{:S(2)}, u32[]{:S(2)}) async-start(bf16[2,16,16,560]{3,2,0,1:T(8,128)(2,1)} %copy.78), calls=%async_computation.3 | async-start | bytes 1310720 | tf_op jit(solution)/shard_map/all_to_all | solution.py:101
  88.4 3.5 %gather_fusion.2 = s32[512]{0:T(512)S(1)} fusion(s32[256]{0:T(256)S(1)} %copy-done.1, s32[1024]{0:T(1024)S(1)} %pad_clamp_fusion.3), kind=kCustom, calls=%fused_computation.2 | custom fusion | bytes 6144 | tf_op jit(solution)/shard_map/gather | solution.py:55
  92.4 0.9 cosine_convert_fusion.1
  93.3 11.5 %all-to-all-done.3 = bf16[2,16,16,560]{3,2,0,1:T(8,128)(2,1)S(1)} async-done(((bf16[2,16,16,560]{3,2,0,1:T(8,128)(2,1)}), bf16[2,16,16,560]{3,2,0,1:T(8,128)(2,1)S(1)}, u32[]{:S(2)}, u32[]{:S(2)}) %all-to-all-start.3) | async-done | bytes 573472 | tf_op jit(solution)/shard_map/all_to_all | solution.py:101
  104.9 2.0 concatenate.22
  106.9 2.0 convolution_add_fusion
  108.9 5.8 %fusion.2 = f32[256,1536]{1,0:T(8,128)} fusion(bf16[1684,1536]{1,0:T(8,128)(2,1)} %all-gather.3.cloned.1.call-done, f32[1536]{0:T(1024)S(1)} %get-tuple-element.13, bf16[512,1172]{1,0:T(8,128)(2,1)} %concatenate.22, f32[256]{0:T(256)S(1)} %broadcast_maximum_fusion.1, s32[512]{0:T(512)S(1)} %bitcast.49), kind=kOutput, calls=%fused_computation.12 | convolution fusion | flops 1230055424 | bytes 6505472 | tf_op jit(solution)/shard_map/dot_general | solution.py:139
  114.7 1.7 fusion.12
  116.5 5.5 %gather_fusion.3 = bf16[1792,512]{1,0:T(8,128)(2,1)S(1)} fusion(bf16[256,512]{1,0:T(8,128)(2,1)S(1)} %fusion.12, s32[2048]{0:T(1024)S(1)} %pad_clamp_fusion), kind=kCustom, calls=%fused_computation.3 | custom fusion | bytes 3677184 | tf_op jit(solution)/shard_map/gather | solution.py:149
  122.3 25.0 %all_to_all.41 = bf16[2,16,56,512]{3,2,1,0:T(8,128)(2,1)S(1)} all-to-all(bf16[2,16,56,512]{3,2,1,0:T(8,128)(2,1)S(1)} %broadcast_select_fusion), channel_id=1, replica_groups=mesh['ev'=2,'mem'=16] {'ev'}, dimensions={0} | all-to-all | bytes 3670016 | tf_op jit(solution)/shard_map/all_to_all | solution.py:152
  147.4 1.5 copy.82
  148.9 5.1 %all-to-all-start.7 = ((bf16[2,16,56,512]{3,2,0,1:T(8,128)(2,1)}), bf16[2,16,56,512]{3,2,0,1:T(8,128)(2,1)}, u32[]{:S(2)}, u32[]{:S(2)}) async-start(bf16[2,16,56,512]{3,2,0,1:T(8,128)(2,1)} %copy.82), calls=%async_computation.7 | async-start | bytes 3670016 | tf_op jit(solution)/shard_map/all_to_all | solution.py:151
  155.6 3.1 %cosine_convert_fusion = bf16[1280,100]{1,0:T(8,128)(2,1)} fusion(f32[100]{0:T(128)S(1)} %copy-done.13, f32[100]{0:T(128)S(1)} %copy-done.14, f32[1280]{0:T(1024)S(1)} %mul.62), kind=kLoop, calls=%fused_computation.27 | loop fusion | flops 384000 | bytes 261920 | tf_op jit(solution)/shard_map/convert_element_type | solution.py:10
  158.7 65.2 %all-gather = bf16[32,1,512]{2,1,0:T(2,128)(2,1)S(1)} all-gather(bf16[1,1,512]{2,1,0:T(2,128)(2,1)S(1)} %dynamic-slice_bitcast_fusion), channel_id=1, replica_groups=mesh['ev'=2,'mem'=16] {'ev','mem'}, dimensions={0}, use_global_device_ids=true | all-gather | bytes 33792 | tf_op jit(solution)/shard_map/all_gather | solution.py:143
  223.9 0.3 convolution_convert_fusion.1
  224.3 0.9 reshape.210
  225.2 1.6 copy.83
  226.9 4.0 %gather_fusion.4 = bf16[896,512]{1,0:T(8,128)(2,1)} fusion(bf16[1792,512]{1,0:T(8,128)(2,1)S(1)} %bitcast.36, s32[1024]{0:T(1024)S(1)} %pad_clamp_fusion.1), kind=kCustom, calls=%fused_computation.4 | custom fusion | bytes 1838592 | tf_op jit(solution)/shard_map/gather | solution.py:164
  230.9 1.4 reshape.208
  232.7 0.6 copy-done.5
  233.3 0.8 pad_maximum_fusion
  234.1 1.3 concatenate.25
  235.4 3.8 %convolution_convert_fusion = bf16[1280,512]{1,0:T(8,128)(2,1)} fusion(bf16[612,512]{1,0:T(8,128)(2,1)} %param.34, bf16[1280,100]{1,0:T(8,128)(2,1)} %cosine_convert_fusion, bf16[1280,512]{1,0:T(8,128)(2,1)} %concatenate.25), kind=kOutput, calls=%fused_computation.9 | convolution fusion | flops 805949440 | bytes 3504128 | tf_op jit(solution)/shard_map/dot_general | solution.py:183
  239.3 2.4 reshape.211
  241.6 1.5 fusion.45
  243.2 1.8 copy.101
  245.6 0.9 copy.102
  246.8 0.9 convolution_convert_fusion.2
  (100 shorter events, 5.2 us)
Async XLA Ops:
  7.2 239.6 %copy-start = (bf16[768,512]{1,0:T(8,128)(2,1)S(1)}, bf16[768,512]{1,0:T(8,128)(2,1)}, u32[]{:S(2)}) copy-start(bf16[768,512]{1,0:T(8,128)(2,1)} %param.35) | copy-start | bytes 2359300
  7.2 0.8 copy-start.7
  7.2 1.0 copy-start.3
  7.2 99.7 %all-gather.3.cloned.1.call-start = ((), (), s32[]{:S(2)}) async-start(), calls=%async_computation.8 | async-start | bytes 7778304 | tf_op jit(solution)/shard_map/all_gather | solution.py:138
  10.3 19.0 %copy-start.16 = (s32[128,2]{0,1:T(2,128)S(1)}, s32[128,2]{0,1:T(2,128)}, u32[]{:S(2)}) copy-start(s32[128,2]{0,1:T(2,128)} %param.22) | copy-start | bytes 3076
  10.3 19.3 %copy-start.10 = (bf16[128,48]{0,1:T(8,128)(2,1)S(1)}, bf16[128,48]{0,1:T(8,128)(2,1)}, u32[]{:S(2)}) copy-start(bf16[128,48]{0,1:T(8,128)(2,1)} %param.21) | copy-start | bytes 36868
  10.4 19.4 %copy-start.17 = (s32[128]{0:T(128)S(1)}, s32[128]{0:T(128)}, u32[]{:S(2)}) copy-start(s32[128]{0:T(128)} %param.20) | copy-start | bytes 1540
  23.3 20.5 %all-to-all-start.1 = ((bf16[2,16,16,512]{3,2,0,1:T(8,128)(2,1)}), bf16[2,16,16,512]{3,2,0,1:T(8,128)(2,1)S(1)}, u32[]{:S(2)}, u32[]{:S(2)}) async-start(bf16[2,16,16,512]{3,2,0,1:T(8,128)(2,1)} %copy.75), calls=%async_computation.1 | async-start | bytes 1048576 | tf_op jit(solution)/shard_map/all_to_all | solution.py:57
  43.8 9.1 %all-to-all-start.4 = ((s32[2,1,256]{2,1,0:T(1,128)}), s32[2,1,256]{2,1,0:T(1,128)S(1)}, u32[]{:S(2)}, u32[]{:S(2)}) async-start(s32[2,1,256]{2,1,0:T(1,128)} %reshape.311), calls=%async_computation.4 | async-start | bytes 4096 | tf_op jit(solution)/shard_map/all_to_all | solution.py:115
  49.8 6.6 %copy-start.8 = (s32[1,1792]{1,0:T(1,128)S(1)}, s32[1,1792]{1,0:T(1,128)}, u32[]{:S(2)}) copy-start(s32[1,1792]{1,0:T(1,128)} %param.25) | copy-start | bytes 21508
  52.9 21.0 %all-to-all-start.2 = ((bf16[2,16,16,560]{3,2,1,0:T(8,128)(2,1)}), bf16[2,16,16,560]{3,2,1,0:T(8,128)(2,1)S(1)}, u32[]{:S(2)}, u32[]{:S(2)}) async-start(bf16[2,16,16,560]{3,2,1,0:T(8,128)(2,1)} %bitcast.7), calls=%async_computation.2 | async-start | bytes 1310720 | tf_op jit(solution)/shard_map/all_to_all | solution.py:102
  56.5 32.0 %copy-start.1 = (s32[256]{0:T(256)S(1)}, s32[256]{0:T(256)}, u32[]{:S(2)}) copy-start(s32[256]{0:T(256)} %param.19) | copy-start | bytes 3076
  73.9 10.7 %all-to-all-start.5 = ((s32[2,16,16]{2,0,1:T(2,128)}), s32[2,16,16]{2,0,1:T(2,128)S(1)}, u32[]{:S(2)}, u32[]{:S(2)}) async-start(s32[2,16,16]{2,0,1:T(2,128)} %copy.80), calls=%async_computation.5 | async-start | bytes 32768 | tf_op jit(solution)/shard_map/all_to_all | solution.py:114
  79.1 13.0 %copy-start.9 = (f32[2,1536]{1,0:T(2,128)S(1)}, f32[2,1536]{1,0:T(2,128)}, u32[]{:S(2)}) copy-start(f32[2,1536]{1,0:T(2,128)} %param.32) | copy-start | bytes 36868
  84.6 20.2 %all-to-all-start.3 = ((bf16[2,16,16,560]{3,2,0,1:T(8,128)(2,1)}), bf16[2,16,16,560]{3,2,0,1:T(8,128)(2,1)S(1)}, u32[]{:S(2)}, u32[]{:S(2)}) async-start(bf16[2,16,16,560]{3,2,0,1:T(8,128)(2,1)} %copy.78), calls=%async_computation.3 | async-start | bytes 1310720 | tf_op jit(solution)/shard_map/all_to_all | solution.py:101
  88.4 4.0 %copy-start.13 = (f32[100]{0:T(128)S(1)}, f32[100]{0:T(128)}, u32[]{:S(2)}) copy-start(f32[100]{0:T(128)} %param.30) | copy-start | bytes 1204
  88.4 4.0 %copy-start.14 = (f32[100]{0:T(128)S(1)}, f32[100]{0:T(128)}, u32[]{:S(2)}) copy-start(f32[100]{0:T(128)} %param.29) | copy-start | bytes 1204
  116.5 42.2 %copy-start.2 = (bf16[256,512]{1,0:T(8,128)(2,1)}, bf16[256,512]{1,0:T(8,128)(2,1)S(1)}, u32[]{:S(2)}) copy-start(bf16[256,512]{1,0:T(8,128)(2,1)S(1)} %fusion.12) | copy-start | bytes 786436
  148.8 5.8 %copy-start.15 = (s32[128,4]{0,1:T(4,128)S(1)}, s32[128,4]{0,1:T(4,128)}, u32[]{:S(2)}) copy-start(s32[128,4]{0,1:T(4,128)} %param.28) | copy-start | bytes 6148
  148.8 6.0 %copy-start.12 = (s32[128,7]{0,1:T(8,128)S(1)}, s32[128,7]{0,1:T(8,128)}, u32[]{:S(2)}) copy-start(s32[128,7]{0,1:T(8,128)} %param.24) | copy-start | bytes 10756
  148.9 6.4 %copy-start.11 = (s32[128,10]{0,1:T(8,128)S(1)}, s32[128,10]{0,1:T(8,128)}, u32[]{:S(2)}) copy-start(s32[128,10]{0,1:T(8,128)} %param.26) | copy-start | bytes 15364
  148.9 76.4 %all-to-all-start.7 = ((bf16[2,16,56,512]{3,2,0,1:T(8,128)(2,1)}), bf16[2,16,56,512]{3,2,0,1:T(8,128)(2,1)}, u32[]{:S(2)}, u32[]{:S(2)}) async-start(bf16[2,16,56,512]{3,2,0,1:T(8,128)(2,1)} %copy.82), calls=%async_computation.7 | async-start | bytes 3670016 | tf_op jit(solution)/shard_map/all_to_all | solution.py:151
  232.3 1.0 copy-start.5
  243.2 1.8 copy-start.6
  243.2 2.5 copy-start.4
Sparse Core Ops, SparseCore 0:
  9.6 77.6 all-gather.2
where the time goes:
time: 256 us; the launch traced here: 255 us
  blocking collectives  102 us (40%)
  waiting for transfers between devices  44.7 us (17%)
  local copies, waits for them, and re-layouts  44.2 us (17%)
  starting transfers between devices  25.9 us (10%)
  between operations  15.3 us (6%)
  matrix products  13.2 us (5%)
  other arithmetic  8.83 us (3%)
    all_gather x1, blocking collectives, local(): lax.all_gather(new_memory[hub_node], ('ev', 'mem'), axis=0, tiled=True)  65.2 us
    all_to_all x1, blocking collectives, local(): lax.all_to_all(served_rows.reshape(ev_size, mem_size, cap_lookup, mem_wid...  25 us
    all_to_all x1, waiting for transfers between devices, local(): lax.all_to_all(out_rows.reshape(ev_size, mem_size, cap_update, part_width...  15.5 us
    all_to_all x1, blocking collectives, local(): lax.all_to_all(own_rows.reshape(ev_size, mem_size, cap_update, mem_width)...  12.1 us
    all_to_all x1, waiting for transfers between devices, local(): lax.all_to_all(lax.all_to_all(own_rows.reshape(ev_size, mem_size, cap_upd...  11.5 us
    all_to_all x1, waiting for transfers between devices, local(): lax.all_to_all(lax.all_to_all(out_rows.reshape(ev_size, mem_size, cap_upd...  11.5 us
    all_to_all x1, starting transfers between devices, local(): lax.all_to_all(lax.all_to_all(own_rows.reshape(ev_size, mem_size, cap_upd...  6.01 us
    dot_general x1, matrix products, local(): jnp.dot(averaged, column_block[:msg_width], preferred_element_type=jnp.fl...  5.83 us
  transfers between devices with their start and end apart: 7, of which 4 were waited for; matrix products, arithmetic and copies ran while one was open for 11% of the time, Pallas kernels for 0%

commit v1 on v0

v1 whole, which is shorter than its diff:
```python
import functools

import jax
import jax.numpy as jnp
from jax import lax
from jax.experimental import pallas as pl
from jax.experimental.pallas import tpu as pltpu
from jax.sharding import PartitionSpec as P

HEADS = 2
LANES = 128
BF = jnp.bfloat16
F32 = jnp.float32
BOTH = ("ev", "mem")
VMEM = pl.BlockSpec(memory_space=pltpu.VMEM)
SMEM = pl.BlockSpec(memory_space=pltpu.SMEM)
PARAMS = pltpu.CompilerParams(vmem_limit_bytes=48 * 1024 * 1024)


def dot(a, b):
    return jnp.dot(a, b, preferred_element_type=F32)


def columns(row):
    parts = []
    for start in range(0, row.shape[1], LANES):
        part = jnp.broadcast_to(row[:, start : start + LANES], (LANES, LANES))
        parts.append(part.T)
    return jnp.concatenate(parts, axis=0)


def one_hot(column, width):
    lane = lax.broadcasted_iota(jnp.int32, column.shape, 1).astype(F32)
    parts = [(column - start == lane).astype(F32).astype(BF) for start in range(0, width, LANES)]
    return jnp.concatenate(parts, axis=1)


def one_hot_rows(row, height):
    line = lax.broadcasted_iota(jnp.int32, (height, row.shape[1]), 0).astype(F32)
    return (line == row).astype(F32)


def serve_kernel(serve_ref, time_ref, memory_ref, rows_ref, tau_ref):
    picks = one_hot(columns(serve_ref[...]), memory_ref.shape[0])
    rows_ref[...] = dot(picks, memory_ref[...]).astype(BF)
    tau = jnp.sum(picks.astype(F32) * time_ref[...], axis=1, keepdims=True)
    tau_ref[...] = jnp.broadcast_to(tau, tau_ref.shape)


def partner_kernel(slot_ref, extra_ref, fetched_ref, out_ref):
    total = fetched_ref.shape[0]
    fetched = fetched_ref[...]
    ends = [
        dot(one_hot(columns(slot_ref[c : c + 1, :]), total), fetched).astype(BF) for c in range(2)
    ]
    spread = jnp.concatenate(
        [one_hot_rows(slot_ref[c : c + 1, :], total).astype(BF) for c in range(2)], axis=1
    )
    extra = extra_ref[...]
    table = jnp.concatenate(
        [
            jnp.concatenate([ends[1], extra], axis=1),
            jnp.concatenate([ends[0], extra], axis=1),
        ],
        axis=0,
    )
    out_ref[...] = dot(spread, table).astype(BF)


def update_kernel(
    enc_width,
    edge_width,
    place_ref,
    serve_ref,
    lookup_ref,
    freq_ref,
    phase_ref,
    bias_ref,
    tau_ref,
    message_ref,
    memory_ref,
    shifted_ref,
    *refs,
):
    weight_refs, (new_ref, served_ref, in_ref, hid_ref) = refs[:-4], refs[-4:]
    nodes, width = memory_ref.shape
    lane = lax.broadcasted_iota(jnp.int32, tau_ref.shape, 1)
    rest = enc_width + edge_width - LANES
    match = one_hot_rows(serve_ref[...], nodes)
    counts = jnp.sum(match, axis=1, keepdims=True)
    extra = message_ref[:, width:].astype(F32)
    stamp = extra[:, rest : rest + 1] * 8.0 + extra[:, rest + 1 : rest + 2]
    gap = stamp - tau_ref[...]
    enc = jnp.cos(gap * freq_ref[...] + phase_ref[...])
    mixed = jnp.where(lane < enc_width, enc, extra).astype(BF)
    tail = jnp.where(lane < rest, extra, 0.0).astype(BF)
    messages = jnp.concatenate([message_ref[:, :width], mixed, tail], axis=1)
    summed = dot(match.astype(BF), messages)
    averaged = (summed / jnp.maximum(counts, 1.0)).astype(BF)
    memory = memory_ref[...]
    msg_width = 2 * width + enc_width + edge_width
    base = 2 * width + LANES
    left = jnp.concatenate([memory, averaged], axis=1)[:, :msg_width]
    hid_left = shifted_ref[:, : rest + width]
    piece = in_ref.shape[2]
    number = 0
    for weight_ref in weight_refs:
        for start in range(0, weight_ref.shape[1], piece):
            cols = slice(start, start + piece)
            where = place_ref[number]
            in_ref[where] = dot(left, weight_ref[:msg_width, cols])
            hid_ref[where] = dot(hid_left, weight_ref[base : msg_width + width, cols])
            number += 1

    def third(ref, row, index):
        parts = []
        at, end = index * width, (index + 1) * width
        while at < end:
            inside = at % piece
            size = min(piece - inside, end - at)
            parts.append(ref[at // piece, :, inside : inside + size])
            at += size
        joined = parts[0] if len(parts) == 1 else jnp.concatenate(parts, axis=1)
        return joined + bias_ref[row : row + 1, index * width : end]

    reset = jax.nn.sigmoid(third(in_ref, 0, 0) + third(hid_ref, 1, 0))
    keep = jax.nn.sigmoid(third(in_ref, 0, 1) + third(hid_ref, 1, 1))
    fresh = jnp.tanh(third(in_ref, 0, 2) + reset * third(hid_ref, 1, 2))
    previous = memory.astype(F32)
    fresh = (1.0 - keep) * fresh + keep * previous
    new = jnp.where(counts > 0.0, fresh, previous).astype(BF)
    new_ref[...] = new
    served_ref[...] = dot(one_hot(columns(lookup_ref[...]), nodes), new).astype(BF)


def attend_kernel(
    index_ref,
    hub_ref,
    gap_ref,
    freq_ref,
    phase_ref,
    looked_ref,
    query_ref,
    keyval_ref,
    output_ref,
    out_ref,
):
    owners, block, width = looked_ref.shape
    routes, events = index_ref.shape
    hubs, near = hub_ref.shape[0], gap_ref.shape[0]
    att = query_ref.shape[1]
    head = att // HEADS
    key_width = query_ref.shape[0]
    hub_from = max(block - 16, 0)
    hub_block = block - hub_from
    looked = looked_ref[...].reshape(owners * block, width)
    hub_rows = looked_ref[:, hub_from:, :].reshape(owners * hub_block, width)
    picks = jnp.concatenate(
        [one_hot(columns(index_ref[k : k + 1, :]), owners * block) for k in range(routes)], axis=0
    )
    rows = dot(picks, looked).astype(BF)
    hub_picks = jnp.concatenate(
        [one_hot(columns(hub_ref[k : k + 1, :]), owners * hub_block) for k in range(hubs)], axis=0
    )
    hub_near = dot(hub_picks, hub_rows).astype(BF)
    freq, phase = freq_ref[...], phase_ref[...]
    enc = jnp.concatenate(
        [jnp.cos(columns(gap_ref[k : k + 1, :]) * freq + phase) for k in range(near)], axis=0
    ).astype(BF)
    own = rows[:events]
    near_rows = jnp.concatenate([rows[events:], hub_near], axis=0)
    key_input = jnp.concatenate([near_rows, enc], axis=1)[:, :key_width]
    keyval = dot(key_input, keyval_ref[...]).astype(BF).astype(F32)
    own_enc = jnp.broadcast_to(jnp.cos(phase), (events, LANES)).astype(BF)
    query_input = jnp.concatenate([own, own_enc], axis=1)[:, :key_width]
    query = dot(query_input, query_ref[...]).astype(BF).astype(F32)
    mixed = []
    for h in range(HEADS):
        cols = slice(h * head, (h + 1) * head)
        vals = slice(att + h * head, att + (h + 1) * head)
        slabs = [slice(k * events, (k + 1) * events) for k in range(near)]
        scores = [
            jnp.sum(query[:, cols] * keyval[s, cols], axis=1, keepdims=True) * head**-0.5
            for s in slabs
        ]
        top = functools.reduce(jnp.maximum, scores)
        expo = [jnp.exp(s - top) for s in scores]
        total = functools.reduce(jnp.add, expo)
        prob = [(e / total).astype(BF).astype(F32) for e in expo]
        mixed.append(sum(p * keyval[s, vals] for p, s in zip(prob, slabs)))
    joined = jnp.concatenate([m.astype(BF) for m in mixed] + [own], axis=1)
    out_ref[...] = dot(joined, output_ref[...]).astype(BF)


def exchange(x):
    return lax.all_to_all(x, BOTH, split_axis=0, concat_axis=0, tiled=True)


def lanes(row):
    return jnp.pad(row, (0, LANES - row.shape[0]))[None, :]


def weight_pieces(gru_weight, ev_size, mem_size):
    half = gru_weight.shape[1] // 2
    if ev_size != 2 or mem_size % 2 or half % LANES:
        whole = lax.all_gather(gru_weight, "ev", axis=1, tiled=True)
        return [whole], whole.shape[1], jnp.zeros((1,), jnp.int32)
    ev, core = lax.axis_index("ev"), lax.axis_index("mem") % 2
    mine = lax.dynamic_slice_in_dim(gru_weight, core * half, half, axis=1)
    first = lax.ppermute(mine, "ev", [(0, 1), (1, 0)])
    second = lax.ppermute(first, "mem", [(i, i ^ 1) for i in range(mem_size)])
    other = 2 * (1 - ev)
    place = jnp.stack([2 * ev, 2 * ev + 1, other + core, other + 1 - core]).astype(jnp.int32)
    return [gru_weight, first, second], half, place


def local(
    memory,
    last_time,
    event_time,
    edge_features,
    update_slot,
    update_serve,
    lookup_slot,
    lookup_serve,
    neighbour_gap,
    hub_node,
    hub_choice,
    time_freq,
    time_phase,
    gru_weight,
    gru_bias,
    query_weight,
    keyval_weight,
    output_weight,
):
    ev_size = lax.axis_size("ev")
    mem_size = lax.axis_size("mem")
    devices = ev_size * mem_size
    nodes, width = memory.shape
    events = event_time.shape[0]
    slots = update_serve.shape[1]
    cap = slots // devices
    lookups = lookup_serve.shape[1]
    cap_lookup = lookups // devices
    enc_width = time_freq.shape[0]
    edge_width = edge_features.shape[1]
    freq, phase = lanes(time_freq), lanes(time_phase)

    pieces, piece, place = weight_pieces(gru_weight, ev_size, mem_size)

    serve_row = update_serve.astype(F32)
    rows, tau = pl.pallas_call(
        serve_kernel,
        out_shape=(
            jax.ShapeDtypeStruct((slots, width), BF),
            jax.ShapeDtypeStruct((slots, LANES), F32),
        ),
        in_specs=[VMEM] * 3,
        out_specs=(VMEM, VMEM),
        compiler_params=PARAMS,
        name="serve_endpoints",
    )(serve_row, last_time.astype(F32)[None, :], memory)
    fetched = exchange(rows.reshape(devices, cap, width)).reshape(slots, width)

    first_edges = LANES - enc_width
    rest = edge_width - first_edges
    stamps = jnp.stack([event_time // 8, event_time % 8], axis=1).astype(BF)
    extra = jnp.concatenate(
        [
            edge_features[:, first_edges:],
            stamps,
            jnp.zeros((events, LANES - edge_width - 2), BF),
            edge_features[:, :first_edges],
        ],
        axis=1,
    )
    message = pl.pallas_call(
        partner_kernel,
        out_shape=jax.ShapeDtypeStruct((slots, width + LANES), BF),
        in_specs=[VMEM] * 3,
        out_specs=VMEM,
        compiler_params=PARAMS,
        name="partner_rows",
    )(update_slot.T.astype(F32), extra, fetched)
    message = exchange(message.reshape(devices, cap, width + LANES)).reshape(slots, width + LANES)

    block = -(-(cap_lookup + 1) // 8) * 8
    lookup_row = jnp.concatenate(
        [
            lookup_serve.reshape(devices, cap_lookup),
            jnp.broadcast_to(hub_node[None, :], (devices, 1)),
            jnp.full((devices, block - cap_lookup - 1), -1, jnp.int32),
        ],
        axis=1,
    ).reshape(1, devices * block)
    shifted = jnp.pad(memory, ((0, 0), (rest, LANES - rest)))
    new_memory, served = pl.pallas_call(
        functools.partial(update_kernel, enc_width, edge_width),
        out_shape=(
            jax.ShapeDtypeStruct((nodes, width), BF),
            jax.ShapeDtypeStruct((devices * block, width), BF),
        ),
        in_specs=[SMEM] + [VMEM] * (9 + len(pieces)),
        out_specs=(VMEM, VMEM),
        scratch_shapes=[
            pltpu.VMEM((3 * width // piece, nodes, piece), F32),
            pltpu.VMEM((3 * width // piece, nodes, piece), F32),
        ],
        compiler_params=PARAMS,
        name="update_memory",
    )(
        place,
        serve_row,
        lookup_row.astype(F32),
        freq,
        phase,
        gru_bias,
        tau,
        message,
        memory,
        shifted,
        *pieces,
    )
    looked = exchange(served.reshape(devices, block, width))

    owner = lookup_slot // cap_lookup
    index = (owner * block + lookup_slot % cap_lookup).T.astype(F32)
    hub_from = max(block - 16, 0)
    hub_index = (hub_choice * (block - hub_from) + cap_lookup - hub_from).T.astype(F32)
    embedding = pl.pallas_call(
        attend_kernel,
        out_shape=jax.ShapeDtypeStruct((events, width), BF),
        in_specs=[VMEM] * 9,
        out_specs=VMEM,
        compiler_params=PARAMS,
        name="attend",
    )(
        index,
        hub_index,
        neighbour_gap.T.astype(F32),
        freq,
        phase,
        looked,
        query_weight,
        keyval_weight,
        output_weight,
    )
    return (new_memory, embedding)


def solution(mesh):
    both = P(BOTH)
    rows = P(BOTH, None)
    return jax.shard_map(
        local,
        mesh=mesh,
        in_specs=(
            rows,
            both,
            both,
            rows,
            rows,
            rows,
            rows,
            rows,
            rows,
            both,
            rows,
            P(),
            P(),
            P(None, "ev"),
            P(),
            P(),
            P(),
            P(),
        ),
        out_specs=(rows, rows),
        check_vma=False,
    )
```

time: 256 us -> 136 us (0.53)
  blocking collectives: 102 us -> 0 us
  waiting for transfers between devices: 44.7 us -> 94.7 us
  local copies, waits for them, and re-layouts: 44.2 us -> 4.78 us
  Pallas kernels: 0 us -> 17.4 us
  between operations: 15.3 us -> 1.58 us
  matrix products: 13.2 us -> 0 us
  starting transfers between devices: 25.9 us -> 17.1 us
  other arithmetic: 8.83 us -> 0.16 us
    all_gather x1 -> x0, blocking collectives: 65.2 us -> none  [local(): lax.all_gather(new_memory[hub_node], ('ev', 'mem'), axis=0, tiled=True)]
    all_to_all x2 -> x0, blocking collectives: 37.2 us -> none  [the longest x1 25 us: local(): lax.all_to_all(served_rows.reshape(ev_size, mem_size, cap_lookup, mem_wid...]
    ppermute x0 -> x2, waiting for transfers between devices: none -> 27.8 us  [the longest x1 27.8 us: weight_pieces(): first = lax.ppermute(mine, 'ev', [(0, 1), (1, 0)])]
    all_to_all x6 -> x3, waiting for transfers between devices: 44 us -> 66.9 us  [exchange(): return lax.all_to_all(x, BOTH, split_axis=0, concat_axis=0, tiled=True)]
    pallas_call x0 -> x4, Pallas kernels: none -> 17.4 us  [the longest x1 7.99 us: local(): pl.pallas_call(functools.partial(update_kernel, enc_width, edge_width), o...]
    gather x5 -> x0, local copies, waits for them, and re-layouts: 16.1 us -> none  [the longest x1 5.52 us: local(): new_memory[jnp.maximum(slots_lookup, 0)]]
    dot_general x6 -> x0, matrix products: 13.2 us -> none  [the longest x1 5.83 us: local(): jnp.dot(averaged, column_block[:msg_width], preferred_element_type=jnp.fl...]
    all_to_all x6 -> x3, starting transfers between devices: 25.9 us -> 14.1 us  [exchange(): return lax.all_to_all(x, BOTH, split_axis=0, concat_axis=0, tiled=True)]
  transfers between devices with their start and end apart: 7 -> 5, of which waited for: 4 -> 3; matrix products, arithmetic and copies ran while one was open for 11% -> 1% of each run, Pallas kernels for 0% -> 2%
where the time goes in v1:
time: 136 us
  waiting for transfers between devices  94.7 us (70%)
  Pallas kernels  17.4 us (13%)
  starting transfers between devices  17.1 us (13%)
  local copies, waits for them, and re-layouts  4.78 us (4%)
  between operations  1.58 us (1%)
    all_to_all x3, waiting for transfers between devices, exchange(): return lax.all_to_all(x, BOTH, split_axis=0, concat_axis=0, tiled=True)  66.9 us
    ppermute x1, waiting for transfers between devices, weight_pieces(): first = lax.ppermute(mine, 'ev', [(0, 1), (1, 0)])  27.8 us
    all_to_all x3, starting transfers between devices, exchange(): return lax.all_to_all(x, BOTH, split_axis=0, concat_axis=0, tiled=True)  14.1 us
    pallas_call x1, Pallas kernels, local(): pl.pallas_call(functools.partial(update_kernel, enc_width, edge_width), o...  7.99 us
    pallas_call x1, Pallas kernels, local(): pl.pallas_call(attend_kernel, out_shape=jax.ShapeDtypeStruct((events, wid...  6.71 us
    ppermute x1, starting transfers between devices, weight_pieces(): first = lax.ppermute(mine, 'ev', [(0, 1), (1, 0)])  2.97 us
  transfers between devices with their start and end apart: 5, of which 3 were waited for; matrix products, arithmetic and copies ran while one was open for 1% of the time, Pallas kernels for 2%

profile of v1, /device:TPU:0, one launch (start us, length us, event | category | flops | bytes accessed | tf_op | source)
XLA Modules:
  0.0 135.7 jit_solution(15133376916073431412)
XLA Ops:
  0.6 0.0 copy-start.9
  0.6 0.0 copy-start.11
  0.7 0.0 copy-start
  0.7 0.0 copy-start.12
  0.7 0.0 copy-start.15
  0.7 0.0 copy-start.5
  0.7 0.0 slice-start
  0.7 2.6 %constant_dynamic-slice_fusion = bf16[1684,384]{1,0:T(8,128)(2,1)} fusion(bf16[1684,768]{1,0:T(8,128)(2,1)} %refs_0_.1, s32[]{:T(128)S(6)} %select_n.35), kind=kLoop, calls=%fused_computation.24 | loop fusion | bytes 2586628 | tf_op jit(solution)/shard_map/dynamic_slice | solution.py:209
  3.3 3.0 %collective-permute-start = (bf16[1684,384]{1,0:T(8,128)(2,1)}, bf16[1684,384]{1,0:T(8,128)(2,1)S(1)}, u32[]{:S(2)}, u32[]{:S(2)}) collective-permute-start(bf16[1684,384]{1,0:T(8,128)(2,1)} %constant_dynamic-slice_fusion), channel_id=1, source_target_pairs={{0,16},{16,0},{1,17},{17,1},{2,18},{18,2},{3,19},{19,3},{4,20},{20... | collective-permute-start | bytes 3879944 | tf_op jit(solution)/shard_map/ppermute | solution.py:210
  6.3 0.0 copy-done.9
  6.3 0.0 copy-done.11
  6.3 0.0 copy-done
  6.3 1.2 serve_endpoints.1
  7.5 4.9 %all-to-all-start = ((bf16[32,16,512]{2,1,0:T(8,128)(2,1)}), bf16[32,16,512]{2,1,0:T(8,128)(2,1)S(1)}, u32[]{:S(2)}, u32[]{:S(2)}) async-start(bf16[32,16,512]{2,1,0:T(8,128)(2,1)} %bitcast.11), calls=%async_computation | async-start | bytes 1048576 | tf_op jit(solution)/shard_map/all_to_all | solution.py:196
  12.4 0.0 copy-done.12
  12.4 0.0 copy-start.4
  12.4 27.8 %collective-permute-done.refs_1_ = bf16[1684,384]{1,0:T(8,128)(2,1)S(1)} collective-permute-done((bf16[1684,384]{1,0:T(8,128)(2,1)}, bf16[1684,384]{1,0:T(8,128)(2,1)S(1)}, u32[]{:S(2)}, u32[]{:S(2)}) %collective-permute-start) | collective-permute-done | bytes 1293344 | tf_op jit(solution)/shard_map/ppermute | solution.py:210
  40.2 0.0 collective-permute-start.1
  40.2 0.0 copy-done.15
  40.2 0.0 copy-done.5
  40.3 0.1 copy.22
  40.4 0.1 copy.23
  40.5 0.0 slice-done
  40.5 0.1 copy.25
  40.7 0.1 copy.24
  40.8 0.1 concatenate.8.extra_ref
  40.9 0.0 all-to-all-done
  41.0 1.6 %partner_rows.1 = bf16[512,640]{1,0:T(8,128)(2,1)} custom-call(f32[2,128]{1,0:T(2,128)S(1)} %convert_bitcast_fusion.2.slot_ref, bf16[128,128]{1,0:T(8,128)(2,1)S(1)} %concatenate.8.extra_ref, bf16[512,512]{1,0:T(8,128)(2,1)S(1)} %bitcast.28), custom_call_target="tpu_custom_call" | custom-call | tf_op jit(solution)/shard_map/partner_rows/pallas_call | solution.py:278
  42.5 6.2 %all-to-all-start.1 = ((bf16[32,16,640]{2,1,0:T(8,128)(2,1)}), bf16[32,16,640]{2,1,0:T(8,128)(2,1)S(1)}, u32[]{:S(2)}, u32[]{:S(2)}) async-start(bf16[32,16,640]{2,1,0:T(8,128)(2,1)} %bitcast.13), calls=%async_computation.1 | async-start | bytes 1310720 | tf_op jit(solution)/shard_map/all_to_all | solution.py:196
  48.7 0.2 pad.13.shifted_ref
  48.9 0.0 copy-done.7
  48.9 0.1 reshape.39
  49.7 0.1 pad.15.clone
  49.7 0.1 pad.16.clone
  49.8 0.1 convert_element_type.39.lookup_ref
  49.9 0.1 pad_add_fusion.place_ref
  50.0 0.0 copy-done.13
  50.0 17.4 %all-to-all-done.1 = bf16[32,16,640]{2,1,0:T(8,128)(2,1)S(1)} async-done(((bf16[32,16,640]{2,1,0:T(8,128)(2,1)}), bf16[32,16,640]{2,1,0:T(8,128)(2,1)S(1)}, u32[]{:S(2)}, u32[]{:S(2)}) %all-to-all-start.1) | async-done | bytes 655392 | tf_op jit(solution)/shard_map/all_to_all | solution.py:196
  67.4 0.0 collective-permute-done.1.refs_2_
  67.4 8.0 %update_memory.1 = (bf16[256,512]{1,0:T(8,128)(2,1)}, bf16[2048,512]{1,0:T(8,128)(2,1)}) custom-call(s32[4]{0:T(128)S(1)} %pad_add_fusion.place_ref, f32[1,512]{1,0:T(1,128)S(1)} %convert_element_type.37.serve_ref, f32[1,2048]{1,0:T(1,128)S(1)} %convert_element_type.39.lookup_ref, f32[1,128]{1,0:T(1,128)S(1)} %get-tuple-element.13.freq_ref, ...), custom_call_target="tpu_custom_call" | custom-call | tf_op jit(solution)/shard_map/update_memory/pallas_call | solution.py:298
  75.4 0.0 copy-start.1
  75.5 0.0 copy-start.2
  75.5 3.1 %all-to-all-start.2 = ((bf16[32,64,512]{2,1,0:T(8,128)(2,1)}), bf16[32,64,512]{2,1,0:T(8,128)(2,1)S(1)}, u32[]{:S(2)}, u32[]{:S(2)}) async-start(bf16[32,64,512]{2,1,0:T(8,128)(2,1)} %bitcast.30), calls=%async_computation.2 | async-start | bytes 4194304 | tf_op jit(solution)/shard_map/all_to_all | solution.py:196
  78.5 0.0 copy-done.10
  78.6 49.5 %all-to-all-done.2.looked_ref = bf16[32,64,512]{2,1,0:T(8,128)(2,1)S(1)} async-done(((bf16[32,64,512]{2,1,0:T(8,128)(2,1)}), bf16[32,64,512]{2,1,0:T(8,128)(2,1)S(1)}, u32[]{:S(2)}, u32[]{:S(2)}) %all-to-all-start.2) | async-done | bytes 2097184 | tf_op jit(solution)/shard_map/all_to_all | solution.py:196
  128.1 0.0 copy-done.2
  128.1 1.0 copy-done.3
  129.0 6.7 %attend.1 = bf16[128,512]{1,0:T(8,128)(2,1)} custom-call(f32[7,128]{1,0:T(8,128)S(1)} %fusion.3.index_ref, f32[4,128]{1,0:T(4,128)S(1)} %convert_bitcast_fusion.1.hub_ref, f32[10,128]{1,0:T(8,128)S(1)} %convert_bitcast_fusion.gap_ref, f32[1,128]{1,0:T(1,128)S(1)} %get-tuple-element.13.freq_ref, f32[1,128]{1,0:T(1,128)S(1)} %get-tuple-element.12.phase_ref, ...), custom_call_target="tpu_custom_call" | custom-call | tf_op jit(solution)/shard_map/attend/pallas_call | solution.py:331
  (25 shorter events, 0.1 us)
Async XLA Ops:
  0.6 5.7 %copy-start.9 = (s32[1,512]{1,0:T(1,128)S(1)}, s32[1,512]{1,0:T(1,128)}, u32[]{:S(2)}) copy-start(s32[1,512]{1,0:T(1,128)} %param.23) | copy-start | bytes 6148
  0.6 5.6 %copy-start.11 = (s32[256]{0:T(256)S(1)}, s32[256]{0:T(256)}, u32[]{:S(2)}) copy-start(s32[256]{0:T(256)} %param.19) | copy-start | bytes 3076
  0.7 5.7 %copy-start = (bf16[256,512]{1,0:T(8,128)(2,1)S(1)}, bf16[256,512]{1,0:T(8,128)(2,1)}, u32[]{:S(2)}) copy-start(bf16[256,512]{1,0:T(8,128)(2,1)} %memory_ref.3) | copy-start | bytes 786436
  0.7 11.7 %copy-start.12 = (s32[128,2]{0,1:T(2,128)S(1)}, s32[128,2]{0,1:T(2,128)}, u32[]{:S(2)}) copy-start(s32[128,2]{0,1:T(2,128)} %param.22) | copy-start | bytes 3076
  0.7 39.6 %copy-start.15 = (s32[128]{0:T(128)S(1)}, s32[128]{0:T(128)}, u32[]{:S(2)}) copy-start(s32[128]{0:T(128)} %param.20) | copy-start | bytes 1540
  0.7 39.6 %copy-start.5 = (bf16[128,48]{0,1:T(8,128)(2,1)S(1)}, bf16[128,48]{0,1:T(8,128)(2,1)}, u32[]{:S(2)}) copy-start(bf16[128,48]{0,1:T(8,128)(2,1)} %param.21) | copy-start | bytes 36868
  0.7 39.9 %slice-start = ((bf16[128,48]{0,1:T(8,128)(2,1)}), bf16[128,28]{0,1:T(8,128)(2,1)S(1)}, s32[]{:S(2)}) async-start(bf16[128,48]{0,1:T(8,128)(2,1)} %param.21), calls=%async_computation.3 | async-start | bytes 16384 | tf_op jit(solution)/shard_map/slice | solution.py:274
  3.3 36.9 %collective-permute-start = (bf16[1684,384]{1,0:T(8,128)(2,1)}, bf16[1684,384]{1,0:T(8,128)(2,1)S(1)}, u32[]{:S(2)}, u32[]{:S(2)}) collective-permute-start(bf16[1684,384]{1,0:T(8,128)(2,1)} %constant_dynamic-slice_fusion), channel_id=1, source_target_pairs={{0,16},{16,0},{1,17},{17,1},{2,18},{18,2},{3,19},{19,3},{4,20},{20... | collective-permute-start | bytes 3879944 | tf_op jit(solution)/shard_map/ppermute | solution.py:210
  7.5 41.4 %copy-start.7 = (s32[1,1792]{1,0:T(1,128)S(1)}, s32[1,1792]{1,0:T(1,128)}, u32[]{:S(2)}) copy-start(s32[1,1792]{1,0:T(1,128)} %param.25) | copy-start | bytes 21508
  7.5 42.5 %copy-start.13 = (f32[100]{0:T(128)S(1)}, f32[100]{0:T(128)}, u32[]{:S(2)}) copy-start(f32[100]{0:T(128)} %param.30) | copy-start | bytes 1204
  7.5 42.5 %copy-start.14 = (f32[100]{0:T(128)S(1)}, f32[100]{0:T(128)}, u32[]{:S(2)}) copy-start(f32[100]{0:T(128)} %param.29) | copy-start | bytes 1204
  7.5 33.5 %all-to-all-start = ((bf16[32,16,512]{2,1,0:T(8,128)(2,1)}), bf16[32,16,512]{2,1,0:T(8,128)(2,1)S(1)}, u32[]{:S(2)}, u32[]{:S(2)}) async-start(bf16[32,16,512]{2,1,0:T(8,128)(2,1)} %bitcast.11), calls=%async_computation | async-start | bytes 1048576 | tf_op jit(solution)/shard_map/all_to_all | solution.py:196
  12.4 55.1 %copy-start.4 = (f32[2,1536]{1,0:T(2,128)S(1)}, f32[2,1536]{1,0:T(2,128)}, u32[]{:S(2)}) copy-start(f32[2,1536]{1,0:T(2,128)} %bias_ref.1) | copy-start | bytes 36868
  40.2 27.2 %collective-permute-start.1 = (bf16[1684,384]{1,0:T(8,128)(2,1)S(1)}, bf16[1684,384]{1,0:T(8,128)(2,1)}, u32[]{:S(2)}, u32[]{:S(2)}) collective-permute-start(bf16[1684,384]{1,0:T(8,128)(2,1)S(1)} %collective-permute-done.refs_1_), channel_id=1, source_target_pairs={{0,1},{1,0},{2,3},{3,2},{4,5},{5,4},{6,7},{7,6},{8,9},{9,8},{10,11... | collective-permute-start | bytes 3879944 | tf_op jit(solution)/shard_map/ppermute | solution.py:211
  42.5 24.9 %all-to-all-start.1 = ((bf16[32,16,640]{2,1,0:T(8,128)(2,1)}), bf16[32,16,640]{2,1,0:T(8,128)(2,1)S(1)}, u32[]{:S(2)}, u32[]{:S(2)}) async-start(bf16[32,16,640]{2,1,0:T(8,128)(2,1)} %bitcast.13), calls=%async_computation.1 | async-start | bytes 1310720 | tf_op jit(solution)/shard_map/all_to_all | solution.py:196
  75.4 3.1 %copy-start.10 = (s32[128,4]{0,1:T(4,128)S(1)}, s32[128,4]{0,1:T(4,128)}, u32[]{:S(2)}) copy-start(s32[128,4]{0,1:T(4,128)} %param.28) | copy-start | bytes 6148
  75.4 3.1 %copy-start.8 = (s32[128,7]{0,1:T(8,128)S(1)}, s32[128,7]{0,1:T(8,128)}, u32[]{:S(2)}) copy-start(s32[128,7]{0,1:T(8,128)} %param.24) | copy-start | bytes 10756
  75.4 3.1 %copy-start.6 = (s32[128,10]{0,1:T(8,128)S(1)}, s32[128,10]{0,1:T(8,128)}, u32[]{:S(2)}) copy-start(s32[128,10]{0,1:T(8,128)} %param.26) | copy-start | bytes 15364
  75.4 52.6 %copy-start.1 = (bf16[768,512]{1,0:T(8,128)(2,1)S(1)}, bf16[768,512]{1,0:T(8,128)(2,1)}, u32[]{:S(2)}) copy-start(bf16[768,512]{1,0:T(8,128)(2,1)} %output_ref.1) | copy-start | bytes 2359300
  75.5 52.6 %copy-start.2 = (bf16[612,512]{1,0:T(8,128)(2,1)S(1)}, bf16[612,512]{1,0:T(8,128)(2,1)}, u32[]{:S(2)}) copy-start(bf16[612,512]{1,0:T(8,128)(2,1)} %keyval_ref.1) | copy-start | bytes 1880068
  75.5 52.6 %all-to-all-start.2 = ((bf16[32,64,512]{2,1,0:T(8,128)(2,1)}), bf16[32,64,512]{2,1,0:T(8,128)(2,1)S(1)}, u32[]{:S(2)}, u32[]{:S(2)}) async-start(bf16[32,64,512]{2,1,0:T(8,128)(2,1)} %bitcast.30), calls=%async_computation.2 | async-start | bytes 4194304 | tf_op jit(solution)/shard_map/all_to_all | solution.py:196
  128.1 1.0 copy-start.3

commit v2 on v1

v2 whole, which is shorter than its diff:
```python
import functools
import math

import jax
import jax.numpy as jnp
from jax import lax
from jax.experimental import pallas as pl
from jax.experimental.pallas import tpu as pltpu
from jax.sharding import PartitionSpec as P

HEADS = 2
LANES = 128
SPLIT = 896
BF = jnp.bfloat16
F32 = jnp.float32
BOTH = ("ev", "hi", "lo")
NEAR = ("ev", "lo")
VMEM = pl.BlockSpec(memory_space=pltpu.VMEM)
SMEM = pl.BlockSpec(memory_space=pltpu.SMEM)
HBM = pl.BlockSpec(memory_space=pltpu.HBM)
MIB = 1024 * 1024


def dot(a, b):
    return jnp.dot(a, b, preferred_element_type=F32)


def dot_t(a, b):
    return lax.dot_general(a, b, (((1,), (1,)), ((), ())), preferred_element_type=F32)


def cosine(x):
    turns = jnp.floor(x * (0.5 / math.pi) + 0.5)
    rest = (x - turns * 6.28125) - turns * (2.0 * math.pi - 6.28125)
    square = rest * rest
    value = jnp.full_like(square, 1.0 / math.factorial(16))
    for order in range(14, -2, -2):
        sign = 1.0 if order % 4 == 0 else -1.0
        value = value * square + sign / math.factorial(order)
    return value


def sigmoid(x):
    return 0.5 * jnp.tanh(0.5 * x) + 0.5


def floor_div(x, n):
    return jnp.floor((x + 0.5) * (1.0 / n))


def columns(row):
    parts = []
    for start in range(0, row.shape[1], LANES):
        part = jnp.broadcast_to(row[:, start : start + LANES], (LANES, LANES))
        parts.append(part.T)
    return jnp.concatenate(parts, axis=0)


def one_hot(column, width):
    lane = lax.broadcasted_iota(jnp.int32, column.shape, 1).astype(F32)
    parts = [(column - start == lane).astype(F32).astype(BF) for start in range(0, width, LANES)]
    return jnp.concatenate(parts, axis=1)


def one_hot_rows(row, height):
    line = lax.broadcasted_iota(jnp.int32, (height, row.shape[1]), 0).astype(F32)
    return (line == row).astype(F32)


def lanes(row):
    return jnp.concatenate([row, jnp.zeros((1, LANES - row.shape[1]), row.dtype)], axis=1)


def fetch(pairs, sems):
    copies = [pltpu.make_async_copy(a, b, sems.at[i]) for i, (a, b) in enumerate(pairs)]
    for copy in copies:
        copy.start()
    return copies


def serve_kernel(serve_hbm, memory_hbm, rows_ref, serve, memory, sems):
    copies = fetch([(serve_hbm, serve), (memory_hbm, memory)], sems)
    copies[0].wait()
    picks = one_hot(columns(serve[...].astype(F32)), memory.shape[0])
    copies[1].wait()
    rows_ref[...] = dot(picks, memory[...]).astype(BF)


def prepare_kernel(
    enc_width,
    group,
    scalar_ref,
    serve_hbm,
    time_hbm,
    stamp_hbm,
    edge_hbm,
    slot_hbm,
    gap_hbm,
    lookup_hbm,
    freq_hbm,
    phase_hbm,
    tau_ref,
    enc_ref,
    swap_ref,
    sent_ref,
    near_ref,
    serve,
    time,
    stamp,
    edge,
    slot,
    gaps,
    lookup,
    freq,
    phase,
    column,
    sems,
):
    copies = fetch(
        [
            (serve_hbm, serve),
            (time_hbm, time),
            (stamp_hbm, stamp),
            (edge_hbm, edge),
            (slot_hbm, slot),
            (gap_hbm, gaps),
            (lookup_hbm, lookup),
            (freq_hbm, freq),
            (phase_hbm, phase),
        ],
        sems,
    )
    for copy in copies:
        copy.wait()
    picks = one_hot(columns(serve[...].astype(F32)), time.shape[1]).astype(F32)
    tau = jnp.sum(picks * time[...].astype(F32), axis=1, keepdims=True)
    tau_ref[...] = jnp.broadcast_to(tau, tau_ref.shape)
    events = gaps.shape[1]
    freq_row, phase_row = lanes(freq[...]), lanes(phase[...])
    for k in range(gaps.shape[0]):
        angle = columns(gaps[k : k + 1, :].astype(F32)) * freq_row + phase_row
        enc_ref[k * events : (k + 1) * events, :] = cosine(angle).astype(BF)
    first, second = (
        one_hot_rows(slot[c : c + 1, :].astype(F32), swap_ref.shape[0]) for c in range(2)
    )
    ends = jnp.concatenate([first, second], axis=1).astype(BF)
    others = jnp.concatenate([second, first], axis=1).astype(BF)
    swap_ref[...] = dot_t(ends, others).astype(BF)
    edges = edge.shape[0]
    first_edges = LANES - enc_width
    rest = edges - first_edges
    line = lax.broadcasted_iota(jnp.int32, (LANES, edges), 0)
    entry = lax.broadcasted_iota(jnp.int32, (LANES, edges), 1)
    wanted = jnp.where(line >= enc_width, line - enc_width, line + first_edges)
    shown = (line >= enc_width) | (line < rest)
    spread = ((wanted == entry) & shown).astype(F32).astype(BF)
    extra = dot(spread, edge[...])
    stamps = stamp[...].astype(F32)
    high = floor_div(stamps, 8)
    line = lax.broadcasted_iota(jnp.int32, extra.shape, 0)
    extra = jnp.where(line == rest, high, extra)
    extra = jnp.where(line == rest + 1, stamps - 8.0 * high, extra)
    sent_ref[...] = dot_t((first + second).astype(BF), extra.astype(BF)).astype(BF)
    column[...] = columns(lookup[...].astype(F32))
    own_half(scalar_ref[0], column, near_ref, group)


def own_half(hi, column, near_ref, group):
    for e in range(near_ref.shape[0] // group):
        start = pl.multiple_of((2 * e + hi) * group, 8)
        near_ref[e * group : (e + 1) * group, :] = column[pl.ds(start, group), :]


def partner_kernel(swap_ref, sent_ref, fetched_ref, out_ref):
    width = fetched_ref.shape[1]
    out_ref[:, :width] = dot(swap_ref[...], fetched_ref[...]).astype(BF)
    out_ref[:, width:] = sent_ref[...]


def update_kernel(
    enc_width,
    edge_width,
    shared,
    scalar_ref,
    hub_ref,
    serve_hbm,
    freq_hbm,
    phase_hbm,
    bias_hbm,
    memory_hbm,
    own_weight_hbm,
    tau_ref,
    near_ref,
    message_ref,
    *refs,
):
    count = 4 if shared else 1
    weight_refs, refs = refs[:count], refs[count:]
    new_ref, extended_ref, rows_ref, serve, freq, phase, bias, memory_ref, own_weight, pre, hid, sems = refs
    copies = fetch(
        [
            (serve_hbm, serve),
            (freq_hbm, freq),
            (phase_hbm, phase),
            (bias_hbm, bias),
            (memory_hbm, memory_ref),
        ]
        + ([(own_weight_hbm, own_weight)] if shared else []),
        sems,
    )
    for copy in copies[:5]:
        copy.wait()
    nodes, width = memory_ref.shape
    lane = lax.broadcasted_iota(jnp.int32, tau_ref.shape, 1)
    rest = enc_width + edge_width - LANES
    match = one_hot_rows(serve[...].astype(F32), nodes)
    counts = jnp.sum(match, axis=1, keepdims=True)
    extra = message_ref[:, width:].astype(F32)
    stamp = extra[:, rest : rest + 1] * 8.0 + extra[:, rest + 1 : rest + 2]
    gap = stamp - tau_ref[...]
    enc = cosine(gap * lanes(freq[...]) + lanes(phase[...]))
    mixed = jnp.where(lane < enc_width, enc, extra).astype(BF)
    tail = jnp.where(lane < rest, extra, 0.0).astype(BF)
    messages = jnp.concatenate([message_ref[:, :width], mixed, tail], axis=1)
    summed = dot(match.astype(BF), messages)
    averaged = (summed / jnp.maximum(counts, 1.0)).astype(BF)
    memory = memory_ref[...]
    msg_width = 2 * width + enc_width + edge_width
    left = jnp.concatenate([memory, averaged], axis=1)[:, :msg_width]
    hid_left = jnp.concatenate([jnp.zeros((nodes, rest), BF), memory], axis=1)
    piece = pre.shape[2]
    if shared:
        copies[5].wait()
        arrays = [(own_weight, own_weight, 0)]
        arrays += [(weight_refs[i], weight_refs[i + 1], SPLIT) for i in (0, 2)]
    else:
        arrays = [(weight_refs[0], weight_refs[0], 0)]
    number = 1
    for upper_ref, lower_ref, at in arrays:
        base = 2 * width + LANES - at
        for start in range(0, upper_ref.shape[1], piece):
            cols = slice(start, start + piece)
            where = scalar_ref[number]
            pre[where] = dot(left[:, :SPLIT], upper_ref[:SPLIT, cols]) + dot(
                left[:, SPLIT:], lower_ref[SPLIT - at : msg_width - at, cols]
            )
            hid[where] = dot(hid_left, lower_ref[base : base + rest + width, cols])
            number += 1

    def third(ref, row, index):
        parts = []
        at, end = index * width, (index + 1) * width
        while at < end:
            inside = at % piece
            size = min(piece - inside, end - at)
            parts.append(ref[at // piece, :, inside : inside + size])
            at += size
        joined = parts[0] if len(parts) == 1 else jnp.concatenate(parts, axis=1)
        return joined + bias[row : row + 1, index * width : end]

    reset = sigmoid(third(pre, 0, 0) + third(hid, 1, 0))
    keep = sigmoid(third(pre, 0, 1) + third(hid, 1, 1))
    fresh = jnp.tanh(third(pre, 0, 2) + reset * third(hid, 1, 2))
    previous = memory.astype(F32)
    fresh = (1.0 - keep) * fresh + keep * previous
    new = jnp.where(counts > 0.0, fresh, previous).astype(BF)
    new_ref[...] = new
    extended_ref[:nodes, :] = new
    line = lax.broadcasted_iota(jnp.int32, (16, nodes), 0)
    entry = lax.broadcasted_iota(jnp.int32, (16, nodes), 1)
    hub = ((entry == hub_ref[0]) & (line == 0)).astype(F32).astype(BF)
    extended_ref[nodes:, :] = dot(hub, new).astype(BF)
    rows_ref[...] = dot(one_hot(near_ref[...], nodes), new).astype(BF)


def far_kernel(group, scalar_ref, lookup_hbm, own_hbm, other_ref, out_ref, lookup, hub, column, far, sems):
    nodes = other_ref.shape[0] - 16
    copies = fetch([(lookup_hbm, lookup), (own_hbm.at[nodes:, :], hub)], sems)
    for copy in copies:
        copy.wait()
    column[...] = columns(lookup[...].astype(F32))
    own_half(scalar_ref[0], column, far, group)
    rows = dot(one_hot(far[...], nodes), other_ref[:nodes, :])
    near, block, width = out_ref.shape
    out_ref[:, : block - 8, :] = rows.reshape(near, block - 8, width).astype(BF)
    hubs = jnp.concatenate(
        [other_ref[nodes : nodes + 1, :], hub[0:1, :], jnp.zeros((6, width), BF)], axis=0
    )
    out_ref[:, block - 8 :, :] = jnp.broadcast_to(hubs[None], (near, 8, width))


def places(slot, hi, cap, lo_size):
    owner = floor_div(slot, cap)
    group = floor_div(owner, lo_size)
    ev = floor_div(group, 2)
    relay = ev * lo_size + owner - group * lo_size
    return relay, group - 2.0 * ev == hi, slot - cap * owner


def picks_of(index, width):
    return jnp.concatenate(
        [one_hot(columns(index[k : k + 1, :]), width) for k in range(index.shape[0])], axis=0
    )


def pick_kernel(cap, lo_size, scalar_ref, slot_ref, looked_ref, out_ref):
    owners, block, width = looked_ref.shape
    relay, near, place = places(slot_ref[...].astype(F32), scalar_ref[0].astype(F32), cap, lo_size)
    index = jnp.where(near, relay * block + place, -1.0)
    looked = looked_ref[...].reshape(owners * block, width)
    out_ref[...] = dot(picks_of(index, owners * block), looked).astype(BF)


def attend_kernel(
    cap,
    lo_size,
    scalar_ref,
    slot_hbm,
    hub_hbm,
    phase_hbm,
    query_hbm,
    keyval_hbm,
    output_hbm,
    enc_ref,
    picked_ref,
    looked_ref,
    out_ref,
    slot,
    hub,
    phase,
    query_ref,
    keyval_ref,
    output_ref,
    sems,
):
    copies = fetch(
        [
            (slot_hbm, slot),
            (hub_hbm, hub),
            (phase_hbm, phase),
            (keyval_hbm, keyval_ref),
            (query_hbm, query_ref),
            (output_hbm, output_ref),
        ],
        sems,
    )
    owners, block, width = looked_ref.shape
    routes, events = slot.shape
    near = routes - 1 + hub.shape[0]
    att = query_ref.shape[1]
    head = att // HEADS
    key_width = query_ref.shape[0]
    for copy in copies[:3]:
        copy.wait()
    hi = scalar_ref[0].astype(F32)
    relay, is_near, place = places(slot[...].astype(F32), hi, cap, lo_size)
    index = jnp.where(is_near, -1.0, relay * block + place)
    looked = looked_ref[...].reshape(owners * block, width)
    rows = (dot(picks_of(index, owners * block), looked) + picked_ref[...].astype(F32)).astype(BF)
    relay, is_near, place = places(hub[...].astype(F32), hi, 1, lo_size)
    hub_index = relay * 8.0 + jnp.where(is_near, 1.0, 0.0)
    hub_rows = looked_ref[:, block - 8 :, :].reshape(owners * 8, width)
    hub_near = dot(picks_of(hub_index, owners * 8), hub_rows).astype(BF)
    own = rows[:events]
    near_rows = jnp.concatenate([rows[events:], hub_near], axis=0)
    key_input = jnp.concatenate([near_rows, enc_ref[...]], axis=1)[:, :key_width]
    copies[3].wait()
    keyval = dot(key_input, keyval_ref[...]).astype(BF).astype(F32)
    own_enc = jnp.broadcast_to(cosine(lanes(phase[...])), (events, LANES)).astype(BF)
    query_input = jnp.concatenate([own, own_enc], axis=1)[:, :key_width]
    copies[4].wait()
    query = dot(query_input, query_ref[...]).astype(BF).astype(F32)
    mixed = []
    for h in range(HEADS):
        cols = slice(h * head, (h + 1) * head)
        vals = slice(att + h * head, att + (h + 1) * head)
        slabs = [slice(k * events, (k + 1) * events) for k in range(near)]
        scores = [
            jnp.sum(query[:, cols] * keyval[s, cols], axis=1, keepdims=True) * head**-0.5
            for s in slabs
        ]
        top = functools.reduce(jnp.maximum, scores)
        expo = [jnp.exp(s - top) for s in scores]
        total = functools.reduce(jnp.add, expo)
        prob = [(e / total).astype(BF).astype(F32) for e in expo]
        mixed.append(sum(p * keyval[s, vals] for p, s in zip(prob, slabs)))
    joined = jnp.concatenate([m.astype(BF) for m in mixed] + [own], axis=1)
    copies[5].wait()
    out_ref[...] = dot(joined, output_ref[...]).astype(BF)


def exchange(x, axes):
    return lax.all_to_all(x, axes, split_axis=0, concat_axis=0, tiled=True)


def after(x, *earlier):
    return lax.optimization_barrier((x, *earlier))[0]


def call(kernel, name, out_shape, smem, hbm, vmem, fetched=(), scratch=(), limit=20):
    many = isinstance(out_shape, tuple)
    copies = [pltpu.VMEM(x.shape, x.dtype) for x in fetched]
    sems = [pltpu.SemaphoreType.DMA((len(fetched),))] if fetched else []
    return pl.pallas_call(
        kernel,
        out_shape=out_shape,
        in_specs=[SMEM] * len(smem) + [HBM] * len(hbm) + [VMEM] * len(vmem),
        out_specs=(VMEM,) * len(out_shape) if many else VMEM,
        scratch_shapes=copies + list(scratch) + sems,
        compiler_params=pltpu.CompilerParams(vmem_limit_bytes=limit * MIB),
        name=name,
    )(*smem, *[pltpu.with_memory_space_constraint(x, pltpu.HBM) for x in hbm], *vmem)


def cores_share(gru_weight):
    half = gru_weight.shape[1] // 2
    return lax.axis_size("ev") == 2 and lax.axis_size("lo") % 2 == 0 and half % LANES == 0


def weight_rows(gru_weight, begin, end):
    half = gru_weight.shape[1] // 2
    core = lax.axis_index("lo") % 2
    mine = lax.dynamic_slice(gru_weight, (begin, core * half), (end - begin, half))
    return lax.ppermute(mine, "ev", [(0, 1), (1, 0)])


def other_core(x):
    return lax.ppermute(x, "lo", [(i, i ^ 1) for i in range(lax.axis_size("lo"))])


def other_half(x):
    return lax.ppermute(x, "hi", [(0, 1), (1, 0)])


def local(
    memory,
    last_time,
    event_time,
    edge_features,
    update_slot,
    update_serve,
    lookup_slot,
    lookup_serve,
    neighbour_gap,
    hub_node,
    hub_choice,
    time_freq,
    time_phase,
    gru_weight,
    gru_bias,
    query_weight,
    keyval_weight,
    output_weight,
):
    ev_size, hi_size, lo_size = (lax.axis_size(a) for a in BOTH)
    ev, hi, lo = (lax.axis_index(a) for a in BOTH)
    devices = ev_size * hi_size * lo_size
    near = ev_size * lo_size
    nodes, width = memory.shape
    events = event_time.shape[0]
    slots = update_serve.shape[1]
    cap = slots // devices
    cap_lookup = lookup_serve.shape[1] // devices
    block = -(-cap_lookup // 8) * 8
    group = lo_size * block
    enc_width = time_freq.shape[0]
    edge_width = edge_features.shape[1]
    freq, phase = time_freq[None, :], time_phase[None, :]
    shape, sent_shape = jax.ShapeDtypeStruct, pltpu.HBM

    rows = call(
        serve_kernel,
        "serve_endpoints",
        sent_shape((slots, width), BF),
        (),
        (update_serve, memory),
        (),
        fetched=(update_serve, memory),
    )
    shared = cores_share(gru_weight)
    if shared:
        late_weight = after(gru_weight, rows)
        upper = weight_rows(late_weight, 0, SPLIT)
        lower = weight_rows(late_weight, SPLIT, gru_weight.shape[0])
        piece = upper.shape[1]
        core, other = lo % 2, 2 * (1 - ev)
        place = [2 * ev, 2 * ev + 1, other + core, other + 1 - core]
    else:
        whole = lax.all_gather(gru_weight, "ev", axis=1, tiled=True)
        piece, place = whole.shape[1], [jnp.int32(0)]
    scalars = jnp.stack([hi] + place).astype(jnp.int32)
    fetched = exchange(rows.reshape(devices, cap, width), BOTH).reshape(slots, width)

    lookup_row = lookup_serve
    if block != cap_lookup:
        lookup_row = jnp.pad(
            lookup_serve.reshape(devices, cap_lookup),
            ((0, 0), (0, block - cap_lookup)),
            constant_values=-1,
        ).reshape(1, devices * block)
    late_lookup = after(lookup_row, rows)
    other_lookup = other_half(late_lookup)
    raw = (
        update_serve,
        last_time[None, :],
        event_time[None, :],
        edge_features.T,
        update_slot.T,
        neighbour_gap.T,
        late_lookup,
        freq,
        phase,
    )
    column = pltpu.VMEM((devices * block, LANES), F32)
    tau, enc, swap, sent, near_column = call(
        functools.partial(prepare_kernel, enc_width, group),
        "prepare",
        (
            shape((slots, LANES), F32),
            shape((events * neighbour_gap.shape[1], LANES), BF),
            shape((slots, slots), BF),
            shape((slots, LANES), BF),
            shape((near * block, LANES), F32),
        ),
        (scalars,),
        raw,
        (),
        fetched=raw,
        scratch=(column,),
    )
    message = call(
        partner_kernel,
        "partner_rows",
        sent_shape((slots, width + LANES), BF),
        (),
        (),
        (swap, sent, fetched),
    )
    if shared:
        upper, lower = after(upper, message), after(lower, message)
        pieces = [upper, lower, other_core(upper), other_core(lower)]
    else:
        pieces = [whole]
    message = exchange(message.reshape(devices, cap, width + LANES), BOTH)
    raw = (update_serve, freq, phase, gru_bias, memory, gru_weight)
    parts = pltpu.VMEM((3 * width // piece, nodes, piece), F32)
    new_memory, extended, near_rows = call(
        functools.partial(update_kernel, enc_width, edge_width, shared),
        "update_memory",
        (
            sent_shape((nodes, width), BF),
            sent_shape((nodes + 16, width), BF),
            sent_shape((near * block, width), BF),
        ),
        (scalars, hub_node),
        raw,
        (tau, near_column, message.reshape(slots, width + LANES), *pieces),
        fetched=raw,
        scratch=(parts, parts),
        limit=28,
    )
    other_extended = other_half(extended)
    near_looked = exchange(near_rows.reshape(near, block, width), NEAR)
    far_rows = call(
        functools.partial(far_kernel, group),
        "far_rows",
        sent_shape((near, block + 8, width), BF),
        (scalars,),
        (other_lookup, extended),
        (other_extended,),
        fetched=(other_lookup, shape((16, width), BF)),
        scratch=(column, pltpu.VMEM((near * block, LANES), F32)),
    )
    far_looked = exchange(far_rows, NEAR)
    slot_row = lookup_slot.T
    picked = call(
        functools.partial(pick_kernel, cap_lookup, lo_size),
        "pick_near",
        shape((lookup_slot.shape[1] * events, width), BF),
        (scalars,),
        (),
        (slot_row, near_looked),
    )
    raw = (slot_row, hub_choice.T, phase, query_weight, keyval_weight, output_weight)
    embedding = call(
        functools.partial(attend_kernel, cap_lookup, lo_size),
        "attend",
        sent_shape((events, width), BF),
        (scalars,),
        raw,
        (enc, picked, far_looked),
        fetched=raw,
    )
    return (new_memory, embedding)


def solution(mesh):
    ev_size, mem_size = mesh.devices.shape
    split = jax.sharding.Mesh(mesh.devices.reshape(ev_size, 2, mem_size // 2), BOTH)
    both = P(BOTH)
    rows = P(BOTH, None)
    return jax.shard_map(
        local,
        mesh=split,
        in_specs=(
            rows,
            both,
            both,
            rows,
            rows,
            rows,
            rows,
            rows,
            rows,
            both,
            rows,
            P(),
            P(),
            P(None, "ev"),
            P(),
            P(),
            P(),
            P(),
        ),
        out_specs=(rows, rows),
        check_vma=False,
    )
```

time: 136 us -> 118 us (0.87)
  waiting for transfers between devices: 94.7 us -> 59.4 us
  starting transfers between devices: 17.1 us -> 27.2 us
  Pallas kernels: 17.4 us -> 23.1 us
  local copies, waits for them, and re-layouts: 4.78 us -> 6.37 us
    all_to_all x3 -> x4, waiting for transfers between devices: 66.9 us -> 22.8 us  [exchange(): return lax.all_to_all(x, axes, split_axis=0, concat_axis=0, tiled=True)]
    ppermute x2 -> x6, waiting for transfers between devices: 27.8 us -> 36.6 us  [the longest x2 21.2 us: weight_rows(): return lax.ppermute(mine, 'ev', [(0, 1), (1, 0)])]
    all_to_all x3 -> x4, starting transfers between devices: 14.1 us -> 20.8 us  [exchange(): return lax.all_to_all(x, axes, split_axis=0, concat_axis=0, tiled=True)]
    pallas_call x4 -> x7, Pallas kernels: 17.4 us -> 23.1 us  [call(): pl.pallas_call(kernel, out_shape=out_shape, in_specs=[SMEM] * len(smem) +...]
    ppermute x2 -> x6, starting transfers between devices: 2.97 us -> 6.48 us  [the longest x2 3.49 us: weight_rows(): return lax.ppermute(mine, 'ev', [(0, 1), (1, 0)])]
    unnamed x34 -> x14, local copies, waits for them, and re-layouts: 1.3 us -> 3.1 us
    dynamic_slice x1 -> x2, local copies, waits for them, and re-layouts: 2.59 us -> 3.19 us  [weight_rows(): lax.dynamic_slice(gru_weight, (begin, core * half), (end - begin, half))]
  transfers between devices with their start and end apart: 5 -> 10, of which waited for: 3 -> 7; matrix products, arithmetic and copies ran while one was open for 1% -> 3% of each run, Pallas kernels for 2% -> 7%
where the time goes in v2:
time: 118 us; the launch traced here: 117 us
  waiting for transfers between devices  59.4 us (50%)
  starting transfers between devices  27.2 us (23%)
  Pallas kernels  23.1 us (20%)
  local copies, waits for them, and re-layouts  6.37 us (5%)
  between operations  1.42 us (1%)
    pallas_call x7, Pallas kernels, call(): pl.pallas_call(kernel, out_shape=out_shape, in_specs=[SMEM] * len(smem) +...  23.1 us
    all_to_all x4, waiting for transfers between devices, exchange(): return lax.all_to_all(x, axes, split_axis=0, concat_axis=0, tiled=True)  22.8 us
    ppermute x2, waiting for transfers between devices, weight_rows(): return lax.ppermute(mine, 'ev', [(0, 1), (1, 0)])  21.2 us
    all_to_all x4, starting transfers between devices, exchange(): return lax.all_to_all(x, axes, split_axis=0, concat_axis=0, tiled=True)  20.8 us
    ppermute x2, waiting for transfers between devices, other_half(): return lax.ppermute(x, 'hi', [(0, 1), (1, 0)])  14 us
    ppermute x2, starting transfers between devices, weight_rows(): return lax.ppermute(mine, 'ev', [(0, 1), (1, 0)])  3.49 us
    dynamic_slice x2, local copies, waits for them, and re-layouts, weight_rows(): lax.dynamic_slice(gru_weight, (begin, core * half), (end - begin, half))  3.19 us
    unnamed x14, local copies, waits for them, and re-layouts  3.1 us
  transfers between devices with their start and end apart: 10, of which 7 were waited for; matrix products, arithmetic and copies ran while one was open for 3% of the time, Pallas kernels for 7%

profile of v2, /device:TPU:0, one launch (start us, length us, event | category | flops | bytes accessed | tf_op | source)
XLA Modules:
  0.0 117.4 jit_solution(3539600715129691943)
XLA Ops:
  0.6 2.1 %serve_endpoints.1 = bf16[512,512]{1,0:T(8,128)(2,1)} custom-call(s32[1,512]{1,0:T(1,128)} %serve_hbm.5, bf16[256,512]{1,0:T(8,128)(2,1)} %memory_hbm.3), custom_call_target="tpu_custom_call" | custom-call | tf_op jit(solution)/shard_map/serve_endpoints/pallas_call | solution.py:404
  2.7 7.3 %all-to-all-start = ((bf16[32,16,512]{2,1,0:T(8,128)(2,1)}), bf16[32,16,512]{2,1,0:T(8,128)(2,1)S(1)}, u32[]{:S(2)}, u32[]{:S(2)}) async-start(bf16[32,16,512]{2,1,0:T(8,128)(2,1)} %bitcast.24), calls=%async_computation | async-start | bytes 1048576 | tf_op jit(solution)/shard_map/all_to_all | solution.py:393
  10.1 2.0 %constant_dynamic-slice_fusion.1 = bf16[896,384]{1,0:T(8,128)(2,1)} fusion(bf16[1684,768]{1,0:T(8,128)(2,1)} %own_weight_hbm.1, s32[]{:T(128)S(6)} %select_n.16), kind=kLoop, calls=%fused_computation.1 | loop fusion | bytes 1376260 | tf_op jit(solution)/shard_map/dynamic_slice | solution.py:423
  12.1 1.8 %collective-permute-start = (bf16[896,384]{1,0:T(8,128)(2,1)}, bf16[896,384]{1,0:T(8,128)(2,1)S(1)}, u32[]{:S(2)}, u32[]{:S(2)}) collective-permute-start(bf16[896,384]{1,0:T(8,128)(2,1)} %constant_dynamic-slice_fusion.1), channel_id=1, source_target_pairs={{0,16},{16,0},{1,17},{17,1},{2,18},{18,2},{3,19},{19,3},{4,20},{20... | collective-permute-start | bytes 2064392 | tf_op jit(solution)/shard_map/ppermute | solution.py:424
  13.9 0.1 stack.23.scalar_ref
  14.0 2.5 %prepare.1 = (f32[512,128]{1,0:T(8,128)S(1)}, bf16[1280,128]{1,0:T(8,128)(2,1)S(1)}, bf16[512,512]{1,0:T(8,128)(2,1)S(1)}, bf16[512,128]{1,0:T(8,128)(2,1)S(1)}, f32[896,128]{1,0:T(8,128)S(1)}) custom-call(s32[5]{0:T(128)S(1)} %stack.23.scalar_ref, s32[1,512]{1,0:T(1,128)} %serve_hbm.5, s32[1,256]{1,0:T(1,128)} %bitcast.34, s32[1,128]{1,0:T(1,128)} %bitcast.36, ...), custom_call_target="tpu_custom_call" | custom-call | tf_op jit(solution)/shard_map/prepare/pallas_call | solution.py:404
  16.5 0.0 copy-start
  16.5 0.8 copy-done
  17.2 0.0 copy-start.2
  17.2 0.7 copy-done.2
  18.0 8.0 %all-to-all-done = bf16[32,16,512]{2,1,0:T(8,128)(2,1)S(1)} async-done(((bf16[32,16,512]{2,1,0:T(8,128)(2,1)}), bf16[32,16,512]{2,1,0:T(8,128)(2,1)S(1)}, u32[]{:S(2)}, u32[]{:S(2)}) %all-to-all-start) | async-done | bytes 524320 | tf_op jit(solution)/shard_map/all_to_all | solution.py:393
  26.0 1.3 %partner_rows.1 = bf16[512,640]{1,0:T(8,128)(2,1)} custom-call(bf16[512,512]{1,0:T(8,128)(2,1)S(1)} %get-tuple-element.17.swap_ref, bf16[512,128]{1,0:T(8,128)(2,1)S(1)} %get-tuple-element.18.sent_ref, bf16[512,512]{1,0:T(8,128)(2,1)S(1)} %bitcast.20), custom_call_target="tpu_custom_call" | custom-call | tf_op jit(solution)/shard_map/partner_rows/pallas_call | solution.py:404
  27.3 2.6 %all-to-all-start.1 = ((bf16[32,16,640]{2,1,0:T(8,128)(2,1)}), bf16[32,16,640]{2,1,0:T(8,128)(2,1)S(1)}, u32[]{:S(2)}, u32[]{:S(2)}) async-start(bf16[32,16,640]{2,1,0:T(8,128)(2,1)} %bitcast.23), calls=%async_computation.1 | async-start | bytes 1310720 | tf_op jit(solution)/shard_map/all_to_all | solution.py:393
  29.9 1.1 constant_dynamic-slice_fusion
  31.0 1.7 %collective-permute-start.1 = (bf16[788,384]{1,0:T(8,128)(2,1)S(1)}, bf16[788,384]{1,0:T(8,128)(2,1)S(1)}, u32[]{:S(2)}, u32[]{:S(2)}) collective-permute-start(bf16[788,384]{1,0:T(8,128)(2,1)S(1)} %constant_dynamic-slice_fusion), channel_id=1, source_target_pairs={{0,16},{16,0},{1,17},{17,1},{2,18},{18,2},{3,19},{19,3},{4,20},{20... | collective-permute-start | bytes 1815560 | tf_op jit(solution)/shard_map/ppermute | solution.py:424
  32.7 2.6 %collective-permute-done.refs_0_ = bf16[896,384]{1,0:T(8,128)(2,1)S(1)} collective-permute-done((bf16[896,384]{1,0:T(8,128)(2,1)}, bf16[896,384]{1,0:T(8,128)(2,1)S(1)}, u32[]{:S(2)}, u32[]{:S(2)}) %collective-permute-start) | collective-permute-done | bytes 688160 | tf_op jit(solution)/shard_map/ppermute | solution.py:424
  35.4 0.0 collective-permute-start.2
  35.4 18.6 %collective-permute-done.1.refs_1_ = bf16[788,384]{1,0:T(8,128)(2,1)S(1)} collective-permute-done((bf16[788,384]{1,0:T(8,128)(2,1)S(1)}, bf16[788,384]{1,0:T(8,128)(2,1)S(1)}, u32[]{:S(2)}, u32[]{:S(2)}) %collective-permute-start.1) | collective-permute-done | bytes 605216 | tf_op jit(solution)/shard_map/ppermute | solution.py:424
  54.0 0.0 collective-permute-start.3
  54.6 1.4 %collective-permute-done.3.refs_3_ = bf16[788,384]{1,0:T(8,128)(2,1)S(1)} collective-permute-done((bf16[788,384]{1,0:T(8,128)(2,1)S(1)}, bf16[788,384]{1,0:T(8,128)(2,1)S(1)}, u32[]{:S(2)}, u32[]{:S(2)}) %collective-permute-start.3) | collective-permute-done | bytes 605216 | tf_op jit(solution)/shard_map/ppermute | solution.py:428
  56.0 0.0 collective-permute-done.2.refs_2_
  56.0 0.0 all-to-all-done.1
  56.0 0.0 copy-start.1
  56.0 1.0 copy-done.1
  57.0 0.0 copy-start.5
  57.0 6.8 %update_memory.1 = (bf16[256,512]{1,0:T(8,128)(2,1)}, bf16[272,512]{1,0:T(8,128)(2,1)}, bf16[896,512]{1,0:T(8,128)(2,1)}) custom-call(s32[5]{0:T(128)S(1)} %stack.23.scalar_ref, s32[1]{0:T(128)S(6)} %copy.20.hub_ref, s32[1,512]{1,0:T(1,128)} %serve_hbm.5, f32[1,100]{1,0:T(1,128)} %bitcast.33, f32[1,100]{1,0:T(1,128)} %bitcast.29, f32[2,1536]{1,0:T(2,128)} %bias_hbm.1, ...), custom_call_target="tpu_custom_call" | custom-call | tf_op jit(solution)/shard_map/update_memory/pallas_call | solution.py:404
  63.8 0.0 copy-start.4
  63.8 4.0 %all-to-all-start.2 = ((bf16[16,56,512]{2,1,0:T(8,128)(2,1)}), bf16[16,56,512]{2,1,0:T(8,128)(2,1)S(1)}, u32[]{:S(2)}, u32[]{:S(2)}) async-start(bf16[16,56,512]{2,1,0:T(8,128)(2,1)} %bitcast.25), calls=%async_computation.2 | async-start | bytes 1835008 | tf_op jit(solution)/shard_map/all_to_all | solution.py:393
  67.8 0.0 copy-start.3
  67.8 2.0 %collective-permute-start.5 = (bf16[272,512]{1,0:T(8,128)(2,1)}, bf16[272,512]{1,0:T(8,128)(2,1)S(1)}, u32[]{:S(2)}, u32[]{:S(2)}) collective-permute-start(bf16[272,512]{1,0:T(8,128)(2,1)} %get-tuple-element.25.own_hbm), channel_id=1, source_target_pairs={{0,8},{8,0},{1,9},{9,1},{2,10},{10,2},{3,11},{11,3},{4,12},{12,4},... | collective-permute-start | bytes 835592 | tf_op jit(solution)/shard_map/ppermute | solution.py:432
  69.8 0.0 copy-done.5
  69.8 1.0 collective-permute-start.4
  70.8 14.0 %collective-permute-done.4.lookup_hbm = s32[1,1792]{1,0:T(1,128)S(1)} collective-permute-done((s32[1,1792]{1,0:T(1,128)S(1)}, s32[1,1792]{1,0:T(1,128)S(1)}, u32[]{:S(2)}, u32[]{:S(2)}) %collective-permute-start.4) | collective-permute-done | bytes 7200 | tf_op jit(solution)/shard_map/ppermute | solution.py:432
  84.8 0.0 copy-start.6
  84.8 0.0 collective-permute-done.5.other_ref
  84.8 0.6 copy-done.6
  85.4 3.0 %far_rows.1 = bf16[16,64,512]{2,1,0:T(8,128)(2,1)} custom-call(s32[5]{0:T(128)S(1)} %stack.23.scalar_ref, s32[1,1792]{1,0:T(1,128)} %copy-done.6, bf16[272,512]{1,0:T(8,128)(2,1)} %get-tuple-element.25.own_hbm, bf16[272,512]{1,0:T(8,128)(2,1)S(1)} %collective-permute-done.5.other_ref), custom_call_target="tpu_custom_call" | custom-call | tf_op jit(solution)/shard_map/far_rows/pallas_call | solution.py:404
  88.4 0.3 all-to-all-done.2.looked_ref
  88.7 6.8 %all-to-all-start.3 = ((bf16[16,64,512]{2,1,0:T(8,128)(2,1)}), bf16[16,64,512]{2,1,0:T(8,128)(2,1)S(1)}, u32[]{:S(2)}, u32[]{:S(2)}) async-start(bf16[16,64,512]{2,1,0:T(8,128)(2,1)} %far_rows.1), calls=%async_computation.3 | async-start | bytes 2097152 | tf_op jit(solution)/shard_map/all_to_all | solution.py:393
  95.6 0.0 copy-done.4
  95.6 1.7 %pick_near.1.picked_ref = bf16[896,512]{1,0:T(8,128)(2,1)S(1)} custom-call(s32[5]{0:T(128)S(1)} %stack.23.scalar_ref, s32[7,128]{1,0:T(8,128)S(1)} %bitcast.22, bf16[16,56,512]{2,1,0:T(8,128)(2,1)S(1)} %all-to-all-done.2.looked_ref), custom_call_target="tpu_custom_call" | custom-call | tf_op jit(solution)/shard_map/pick_near/pallas_call | solution.py:404
  97.3 14.5 %all-to-all-done.3.looked_ref = bf16[16,64,512]{2,1,0:T(8,128)(2,1)S(1)} async-done(((bf16[16,64,512]{2,1,0:T(8,128)(2,1)}), bf16[16,64,512]{2,1,0:T(8,128)(2,1)S(1)}, u32[]{:S(2)}, u32[]{:S(2)}) %all-to-all-start.3) | async-done | bytes 1048608 | tf_op jit(solution)/shard_map/all_to_all | solution.py:393
  111.7 0.0 copy-done.3
  111.7 5.7 %attend.1 = bf16[128,512]{1,0:T(8,128)(2,1)} custom-call(s32[5]{0:T(128)S(1)} %stack.23.scalar_ref, s32[7,128]{1,0:T(8,128)} %bitcast.21, s32[4,128]{1,0:T(4,128)} %bitcast.31, f32[1,100]{1,0:T(1,128)} %bitcast.30, bf16[612,256]{1,0:T(8,128)(2,1)} %query_hbm.1, bf16[612,512]{1,0:T(8,128)(2,1)} %keyval_hbm.1, bf16[768,512]{1,0:T(8,128)(2,1)} %output_hbm.1, ...), custom_call_target="tpu_custom_call" | custom-call | tf_op jit(solution)/shard_map/attend/pallas_call | solution.py:404
Async XLA Ops:
  2.7 23.2 %all-to-all-start = ((bf16[32,16,512]{2,1,0:T(8,128)(2,1)}), bf16[32,16,512]{2,1,0:T(8,128)(2,1)S(1)}, u32[]{:S(2)}, u32[]{:S(2)}) async-start(bf16[32,16,512]{2,1,0:T(8,128)(2,1)} %bitcast.24), calls=%async_computation | async-start | bytes 1048576 | tf_op jit(solution)/shard_map/all_to_all | solution.py:393
  12.1 23.3 %collective-permute-start = (bf16[896,384]{1,0:T(8,128)(2,1)}, bf16[896,384]{1,0:T(8,128)(2,1)S(1)}, u32[]{:S(2)}, u32[]{:S(2)}) collective-permute-start(bf16[896,384]{1,0:T(8,128)(2,1)} %constant_dynamic-slice_fusion.1), channel_id=1, source_target_pairs={{0,16},{16,0},{1,17},{17,1},{2,18},{18,2},{3,19},{19,3},{4,20},{20... | collective-permute-start | bytes 2064392 | tf_op jit(solution)/shard_map/ppermute | solution.py:424
  16.5 0.8 copy-start
  17.2 0.7 copy-start.2
  27.3 28.7 %all-to-all-start.1 = ((bf16[32,16,640]{2,1,0:T(8,128)(2,1)}), bf16[32,16,640]{2,1,0:T(8,128)(2,1)S(1)}, u32[]{:S(2)}, u32[]{:S(2)}) async-start(bf16[32,16,640]{2,1,0:T(8,128)(2,1)} %bitcast.23), calls=%async_computation.1 | async-start | bytes 1310720 | tf_op jit(solution)/shard_map/all_to_all | solution.py:393
  31.0 22.9 %collective-permute-start.1 = (bf16[788,384]{1,0:T(8,128)(2,1)S(1)}, bf16[788,384]{1,0:T(8,128)(2,1)S(1)}, u32[]{:S(2)}, u32[]{:S(2)}) collective-permute-start(bf16[788,384]{1,0:T(8,128)(2,1)S(1)} %constant_dynamic-slice_fusion), channel_id=1, source_target_pairs={{0,16},{16,0},{1,17},{17,1},{2,18},{18,2},{3,19},{19,3},{4,20},{20... | collective-permute-start | bytes 1815560 | tf_op jit(solution)/shard_map/ppermute | solution.py:424
  35.4 20.6 %collective-permute-start.2 = (bf16[896,384]{1,0:T(8,128)(2,1)S(1)}, bf16[896,384]{1,0:T(8,128)(2,1)S(1)}, u32[]{:S(2)}, u32[]{:S(2)}) collective-permute-start(bf16[896,384]{1,0:T(8,128)(2,1)S(1)} %collective-permute-done.refs_0_), channel_id=1, source_target_pairs={{0,1},{1,0},{2,3},{3,2},{4,5},{5,4},{6,7},{7,6},{8,9},{9,8},{10,11... | collective-permute-start | bytes 2064392 | tf_op jit(solution)/shard_map/ppermute | solution.py:428
  54.0 2.0 %collective-permute-start.3 = (bf16[788,384]{1,0:T(8,128)(2,1)S(1)}, bf16[788,384]{1,0:T(8,128)(2,1)S(1)}, u32[]{:S(2)}, u32[]{:S(2)}) collective-permute-start(bf16[788,384]{1,0:T(8,128)(2,1)S(1)} %collective-permute-done.1.refs_1_), channel_id=1, source_target_pairs={{0,1},{1,0},{2,3},{3,2},{4,5},{5,4},{6,7},{7,6},{8,9},{9,8},{10,11... | collective-permute-start | bytes 1815560 | tf_op jit(solution)/shard_map/ppermute | solution.py:428
  56.0 1.0 copy-start.1
  57.0 12.8 %copy-start.5 = (s32[1,1792]{1,0:T(1,128)S(1)}, s32[1,1792]{1,0:T(1,128)}, u32[]{:S(2)}) copy-start(s32[1,1792]{1,0:T(1,128)} %lookup_hbm) | copy-start | bytes 21508
  63.8 31.7 %copy-start.4 = (s32[128,7]{0,1:T(8,128)S(1)}, s32[128,7]{0,1:T(8,128)}, u32[]{:S(2)}) copy-start(s32[128,7]{0,1:T(8,128)} %param.24) | copy-start | bytes 10756
  63.8 24.9 %all-to-all-start.2 = ((bf16[16,56,512]{2,1,0:T(8,128)(2,1)}), bf16[16,56,512]{2,1,0:T(8,128)(2,1)S(1)}, u32[]{:S(2)}, u32[]{:S(2)}) async-start(bf16[16,56,512]{2,1,0:T(8,128)(2,1)} %bitcast.25), calls=%async_computation.2 | async-start | bytes 1835008 | tf_op jit(solution)/shard_map/all_to_all | solution.py:393
  67.8 43.9 %copy-start.3 = (bf16[1280,128]{1,0:T(8,128)(2,1)S(1)}, bf16[1280,128]{1,0:T(8,128)(2,1)}, u32[]{:S(2)}) copy-start(bf16[1280,128]{1,0:T(8,128)(2,1)} %copy-done.2) | copy-start | bytes 983044
  67.8 17.0 %collective-permute-start.5 = (bf16[272,512]{1,0:T(8,128)(2,1)}, bf16[272,512]{1,0:T(8,128)(2,1)S(1)}, u32[]{:S(2)}, u32[]{:S(2)}) collective-permute-start(bf16[272,512]{1,0:T(8,128)(2,1)} %get-tuple-element.25.own_hbm), channel_id=1, source_target_pairs={{0,8},{8,0},{1,9},{9,1},{2,10},{10,2},{3,11},{11,3},{4,12},{12,4},... | collective-permute-start | bytes 835592 | tf_op jit(solution)/shard_map/ppermute | solution.py:432
  69.8 15.0 %collective-permute-start.4 = (s32[1,1792]{1,0:T(1,128)S(1)}, s32[1,1792]{1,0:T(1,128)S(1)}, u32[]{:S(2)}, u32[]{:S(2)}) collective-permute-start(s32[1,1792]{1,0:T(1,128)S(1)} %copy-done.5), channel_id=1, source_target_pairs={{0,8},{8,0},{1,9},{9,1},{2,10},{10,2},{3,11},{11,3},{4,12},{12,4},... | collective-permute-start | bytes 21512 | tf_op jit(solution)/shard_map/ppermute | solution.py:432
  84.8 0.6 copy-start.6
  88.7 23.0 %all-to-all-start.3 = ((bf16[16,64,512]{2,1,0:T(8,128)(2,1)}), bf16[16,64,512]{2,1,0:T(8,128)(2,1)S(1)}, u32[]{:S(2)}, u32[]{:S(2)}) async-start(bf16[16,64,512]{2,1,0:T(8,128)(2,1)} %far_rows.1), calls=%async_computation.3 | async-start | bytes 2097152 | tf_op jit(solution)/shard_map/all_to_all | solution.py:393

commit v3 on v2

--- a/solution.py
+++ b/solution.py
@@ -10,7 +10,8 @@
 
 HEADS = 2
 LANES = 128
-SPLIT = 896
+SHARED = 384
+DIRECT = 2 * SHARED
 BF = jnp.bfloat16
 F32 = jnp.float32
 BOTH = ("ev", "hi", "lo")
@@ -95,25 +96,23 @@
     stamp_hbm,
     edge_hbm,
     slot_hbm,
-    gap_hbm,
     lookup_hbm,
     freq_hbm,
     phase_hbm,
     tau_ref,
-    enc_ref,
     swap_ref,
     sent_ref,
-    near_ref,
+    near_hbm,
     serve,
     time,
     stamp,
     edge,
     slot,
-    gaps,
     lookup,
     freq,
     phase,
     column,
+    near,
     sems,
 ):
     copies = fetch(
@@ -123,7 +122,6 @@
             (stamp_hbm, stamp),
             (edge_hbm, edge),
             (slot_hbm, slot),
-            (gap_hbm, gaps),
             (lookup_hbm, lookup),
             (freq_hbm, freq),
             (phase_hbm, phase),
@@ -132,14 +130,16 @@
     )
     for copy in copies:
         copy.wait()
+    column[...] = columns(lookup[...].astype(F32))
+    own_half(scalar_ref[0], column, near, group)
+    out = pltpu.make_async_copy(near, near_hbm, sems.at[0])
+    out.start()
     picks = one_hot(columns(serve[...].astype(F32)), time.shape[1]).astype(F32)
     tau = jnp.sum(picks * time[...].astype(F32), axis=1, keepdims=True)
-    tau_ref[...] = jnp.broadcast_to(tau, tau_ref.shape)
-    events = gaps.shape[1]
-    freq_row, phase_row = lanes(freq[...]), lanes(phase[...])
-    for k in range(gaps.shape[0]):
-        angle = columns(gaps[k : k + 1, :].astype(F32)) * freq_row + phase_row
-        enc_ref[k * events : (k + 1) * events, :] = cosine(angle).astype(BF)
+    slots = serve.shape[1]
+    tau_ref[:slots, :] = jnp.broadcast_to(tau, (slots, LANES))
+    tau_ref[slots : slots + 8, :] = jnp.broadcast_to(lanes(freq[...]), (8, LANES))
+    tau_ref[slots + 8 : slots + 16, :] = jnp.broadcast_to(lanes(phase[...]), (8, LANES))
     first, second = (
         one_hot_rows(slot[c : c + 1, :].astype(F32), swap_ref.shape[0]) for c in range(2)
     )
@@ -161,8 +161,7 @@
     extra = jnp.where(line == rest, high, extra)
     extra = jnp.where(line == rest + 1, stamps - 8.0 * high, extra)
     sent_ref[...] = dot_t((first + second).astype(BF), extra.astype(BF)).astype(BF)
-    column[...] = columns(lookup[...].astype(F32))
-    own_half(scalar_ref[0], column, near_ref, group)
+    out.wait()
 
 
 def own_half(hi, column, near_ref, group):
@@ -184,68 +183,71 @@
     scalar_ref,
     hub_ref,
     serve_hbm,
-    freq_hbm,
-    phase_hbm,
+    memory_hbm,
     bias_hbm,
-    memory_hbm,
+    near_hbm,
     own_weight_hbm,
     tau_ref,
-    near_ref,
     message_ref,
     *refs,
 ):
-    count = 4 if shared else 1
+    count = 6 if shared else 1
     weight_refs, refs = refs[:count], refs[count:]
-    new_ref, extended_ref, rows_ref, serve, freq, phase, bias, memory_ref, own_weight, pre, hid, sems = refs
-    copies = fetch(
-        [
-            (serve_hbm, serve),
-            (freq_hbm, freq),
-            (phase_hbm, phase),
-            (bias_hbm, bias),
-            (memory_hbm, memory_ref),
-        ]
-        + ([(own_weight_hbm, own_weight)] if shared else []),
-        sems,
-    )
-    for copy in copies[:5]:
-        copy.wait()
+    new_hbm, extended_hbm, rows_hbm, serve, memory_ref, bias, near_ref, own_weight = refs[:8]
+    pre, hid, out, rows_out, sems = refs[8:]
+    pairs = [(serve_hbm, serve), (memory_hbm, memory_ref), (bias_hbm, bias), (near_hbm, near_ref)]
+    pairs += [(own_weight_hbm, own_weight)] if shared else []
+    copies = fetch(pairs, sems)
     nodes, width = memory_ref.shape
-    lane = lax.broadcasted_iota(jnp.int32, tau_ref.shape, 1)
+    slots = message_ref.shape[0]
+    lane = lax.broadcasted_iota(jnp.int32, (slots, LANES), 1)
     rest = enc_width + edge_width - LANES
-    match = one_hot_rows(serve[...].astype(F32), nodes)
-    counts = jnp.sum(match, axis=1, keepdims=True)
     extra = message_ref[:, width:].astype(F32)
     stamp = extra[:, rest : rest + 1] * 8.0 + extra[:, rest + 1 : rest + 2]
-    gap = stamp - tau_ref[...]
-    enc = cosine(gap * lanes(freq[...]) + lanes(phase[...]))
+    gap = stamp - tau_ref[:slots, :]
+    enc = cosine(gap * tau_ref[slots : slots + 1, :] + tau_ref[slots + 8 : slots + 9, :])
     mixed = jnp.where(lane < enc_width, enc, extra).astype(BF)
     tail = jnp.where(lane < rest, extra, 0.0).astype(BF)
     messages = jnp.concatenate([message_ref[:, :width], mixed, tail], axis=1)
+    copies[0].wait()
+    match = one_hot_rows(serve[...].astype(F32), nodes)
+    counts = jnp.sum(match, axis=1, keepdims=True)
     summed = dot(match.astype(BF), messages)
     averaged = (summed / jnp.maximum(counts, 1.0)).astype(BF)
+    copies[1].wait()
     memory = memory_ref[...]
     msg_width = 2 * width + enc_width + edge_width
+    base = 2 * width + LANES
     left = jnp.concatenate([memory, averaged], axis=1)[:, :msg_width]
     hid_left = jnp.concatenate([jnp.zeros((nodes, rest), BF), memory], axis=1)
     piece = pre.shape[2]
-    if shared:
-        copies[5].wait()
-        arrays = [(own_weight, own_weight, 0)]
-        arrays += [(weight_refs[i], weight_refs[i + 1], SPLIT) for i in (0, 2)]
-    else:
-        arrays = [(weight_refs[0], weight_refs[0], 0)]
-    number = 1
-    for upper_ref, lower_ref, at in arrays:
-        base = 2 * width + LANES - at
-        for start in range(0, upper_ref.shape[1], piece):
+
+    def whole(number, weight_ref):
+        for start in range(0, weight_ref.shape[1], piece):
             cols = slice(start, start + piece)
             where = scalar_ref[number]
-            pre[where] = dot(left[:, :SPLIT], upper_ref[:SPLIT, cols]) + dot(
-                left[:, SPLIT:], lower_ref[SPLIT - at : msg_width - at, cols]
+            pre[where] = dot(left, weight_ref[:msg_width, cols])
+            hid[where] = dot(hid_left, weight_ref[base : base + rest + width, cols])
+            number += 1
+
+    if shared:
+        for number, (mine, other, lower) in ((3, weight_refs[:3]), (4, weight_refs[3:])):
+            where = scalar_ref[number]
+            side = scalar_ref[5]
+            halves = [left[:, :SHARED], left[:, SHARED:DIRECT]]
+            first = jnp.where(side == 0, halves[0], halves[1])
+            second = jnp.where(side == 0, halves[1], halves[0])
+            pre[where] = (
+                dot(first, mine[...])
+                + dot(second, other[...])
+                + dot(left[:, DIRECT:], lower[: msg_width - DIRECT, :])
             )
-            hid[where] = dot(hid_left, lower_ref[base : base + rest + width, cols])
-            number += 1
+            hid[where] = dot(hid_left, lower[base - DIRECT :, :])
+        copies[4].wait()
+        whole(1, own_weight)
+    else:
+        whole(1, weight_refs[0])
+    copies[2].wait()
 
     def third(ref, row, index):
         parts = []
@@ -264,13 +266,27 @@
     previous = memory.astype(F32)
     fresh = (1.0 - keep) * fresh + keep * previous
     new = jnp.where(counts > 0.0, fresh, previous).astype(BF)
-    new_ref[...] = new
-    extended_ref[:nodes, :] = new
+    out[:nodes, :] = new
     line = lax.broadcasted_iota(jnp.int32, (16, nodes), 0)
     entry = lax.broadcasted_iota(jnp.int32, (16, nodes), 1)
     hub = ((entry == hub_ref[0]) & (line == 0)).astype(F32).astype(BF)
-    extended_ref[nodes:, :] = dot(hub, new).astype(BF)
-    rows_ref[...] = dot(one_hot(near_ref[...], nodes), new).astype(BF)
+    out[nodes:, :] = dot(hub, new).astype(BF)
+    sends = [
+        pltpu.make_async_copy(out, extended_hbm, sems.at[0]),
+        pltpu.make_async_copy(out.at[:nodes, :], new_hbm, sems.at[1]),
+    ]
+    for send in sends:
+        send.start()
+    copies[3].wait()
+    total = near_ref.shape[0]
+    part = total // 2
+    for i in range(2):
+        some = slice(i * part, (i + 1) * part)
+        rows_out[some, :] = dot(one_hot(near_ref[some, :], nodes), new).astype(BF)
+        sends.append(pltpu.make_async_copy(rows_out.at[some, :], rows_hbm.at[some, :], sems.at[2 + i]))
+        sends[-1].start()
+    for send in sends:
+        send.wait()
 
 
 def far_kernel(group, scalar_ref, lookup_hbm, own_hbm, other_ref, out_ref, lookup, hub, column, far, sems):
@@ -303,72 +319,98 @@
     )
 
 
-def pick_kernel(cap, lo_size, scalar_ref, slot_ref, looked_ref, out_ref):
-    owners, block, width = looked_ref.shape
-    relay, near, place = places(slot_ref[...].astype(F32), scalar_ref[0].astype(F32), cap, lo_size)
-    index = jnp.where(near, relay * block + place, -1.0)
-    looked = looked_ref[...].reshape(owners * block, width)
-    out_ref[...] = dot(picks_of(index, owners * block), looked).astype(BF)
-
-
-def attend_kernel(
+def pick_kernel(
     cap,
     lo_size,
     scalar_ref,
     slot_hbm,
     hub_hbm,
+    gap_hbm,
+    freq_hbm,
     phase_hbm,
+    looked_ref,
+    picked_ref,
+    far_ref,
+    hub_ref,
+    enc_ref,
+    own_ref,
+    slot,
+    hub,
+    gaps,
+    freq,
+    phase,
+    sems,
+):
+    copies = fetch(
+        [(slot_hbm, slot), (hub_hbm, hub), (gap_hbm, gaps), (freq_hbm, freq), (phase_hbm, phase)],
+        sems,
+    )
+    for copy in copies:
+        copy.wait()
+    owners, block, width = looked_ref.shape
+    hi = scalar_ref[0].astype(F32)
+    relay, near, place = places(slot[...].astype(F32), hi, cap, lo_size)
+    index = jnp.where(near, relay * block + place, -1.0)
+    looked = looked_ref[...].reshape(owners * block, width)
+    events = gaps.shape[1]
+    picks = [one_hot(columns(index[k : k + 1, :]), owners * block) for k in range(slot.shape[0])]
+    picked_ref[...] = dot(jnp.concatenate(picks, axis=0), looked).astype(BF)
+    far_ref[...] = jnp.where(near, -1.0, relay * (block + 8) + place)
+    relay, near, place = places(hub[...].astype(F32), hi, 1, lo_size)
+    hub_ref[...] = relay * 8.0 + jnp.where(near, 1.0, 0.0)
+    freq_row, phase_row = lanes(freq[...]), lanes(phase[...])
+    for k in range(gaps.shape[0]):
+        angle = columns(gaps[k : k + 1, :].astype(F32)) * freq_row + phase_row
+        enc_ref[k * events : (k + 1) * events, :] = cosine(angle).astype(BF)
+    own_ref[...] = jnp.broadcast_to(cosine(phase_row), (8, LANES)).astype(BF)
+
+
+def attend_kernel(
+    keyval_hbm,
+    enc_hbm,
     query_hbm,
-    keyval_hbm,
     output_hbm,
-    enc_ref,
     picked_ref,
+    far_ref,
+    hub_ref,
+    own_enc_ref,
     looked_ref,
     out_ref,
-    slot,
-    hub,
-    phase,
+    keyval_ref,
+    enc_ref,
     query_ref,
-    keyval_ref,
     output_ref,
     sems,
 ):
     copies = fetch(
         [
-            (slot_hbm, slot),
-            (hub_hbm, hub),
-            (phase_hbm, phase),
             (keyval_hbm, keyval_ref),
+            (enc_hbm, enc_ref),
             (query_hbm, query_ref),
             (output_hbm, output_ref),
         ],
         sems,
     )
     owners, block, width = looked_ref.shape
-    routes, events = slot.shape
-    near = routes - 1 + hub.shape[0]
+    events = out_ref.shape[0]
+    near = enc_ref.shape[0] // events
     att = query_ref.shape[1]
     head = att // HEADS
-    key_width = query_ref.shape[0]
-    for copy in copies[:3]:
-        copy.wait()
-    hi = scalar_ref[0].astype(F32)
-    relay, is_near, place = places(slot[...].astype(F32), hi, cap, lo_size)
-    index = jnp.where(is_near, -1.0, relay * block + place)
     looked = looked_ref[...].reshape(owners * block, width)
-    rows = (dot(picks_of(index, owners * block), looked) + picked_ref[...].astype(F32)).astype(BF)
-    relay, is_near, place = places(hub[...].astype(F32), hi, 1, lo_size)
-    hub_index = relay * 8.0 + jnp.where(is_near, 1.0, 0.0)
     hub_rows = looked_ref[:, block - 8 :, :].reshape(owners * 8, width)
-    hub_near = dot(picks_of(hub_index, owners * 8), hub_rows).astype(BF)
+    hub_near = dot(picks_of(hub_ref[...], owners * 8), hub_rows).astype(BF)
+    picks = picks_of(far_ref[...], owners * block)
+    rows = (dot(picks, looked) + picked_ref[...].astype(F32)).astype(BF)
     own = rows[:events]
     near_rows = jnp.concatenate([rows[events:], hub_near], axis=0)
+    copies[0].wait()
+    copies[1].wait()
+    key_width = keyval_ref.shape[0]
     key_input = jnp.concatenate([near_rows, enc_ref[...]], axis=1)[:, :key_width]
-    copies[3].wait()
     keyval = dot(key_input, keyval_ref[...]).astype(BF).astype(F32)
-    own_enc = jnp.broadcast_to(cosine(lanes(phase[...])), (events, LANES)).astype(BF)
+    copies[2].wait()
+    own_enc = jnp.broadcast_to(own_enc_ref[0:1, :], (events, LANES))
     query_input = jnp.concatenate([own, own_enc], axis=1)[:, :key_width]
-    copies[4].wait()
     query = dot(query_input, query_ref[...]).astype(BF).astype(F32)
     mixed = []
     for h in range(HEADS):
@@ -385,7 +427,7 @@
         prob = [(e / total).astype(BF).astype(F32) for e in expo]
         mixed.append(sum(p * keyval[s, vals] for p, s in zip(prob, slabs)))
     joined = jnp.concatenate([m.astype(BF) for m in mixed] + [own], axis=1)
-    copies[5].wait()
+    copies[3].wait()
     out_ref[...] = dot(joined, output_ref[...]).astype(BF)
 
 
@@ -397,31 +439,33 @@
     return lax.optimization_barrier((x, *earlier))[0]
 
 
-def call(kernel, name, out_shape, smem, hbm, vmem, fetched=(), scratch=(), limit=20):
+def call(kernel, name, out_shape, smem, hbm, vmem, fetched=(), scratch=(), left=(), kept=(), limit=20, extra_sems=0):
     many = isinstance(out_shape, tuple)
+    specs = tuple(HBM if x in left else VMEM for x in range(len(out_shape))) if many else VMEM
     copies = [pltpu.VMEM(x.shape, x.dtype) for x in fetched]
-    sems = [pltpu.SemaphoreType.DMA((len(fetched),))] if fetched else []
+    sems = [pltpu.SemaphoreType.DMA((len(fetched) + extra_sems,))] if fetched else []
     return pl.pallas_call(
         kernel,
         out_shape=out_shape,
-        in_specs=[SMEM] * len(smem) + [HBM] * len(hbm) + [VMEM] * len(vmem),
-        out_specs=(VMEM,) * len(out_shape) if many else VMEM,
+        in_specs=[SMEM] * len(smem) + [HBM] * len(hbm) + [VMEM] * (len(kept) + len(vmem)),
+        out_specs=specs,
         scratch_shapes=copies + list(scratch) + sems,
         compiler_params=pltpu.CompilerParams(vmem_limit_bytes=limit * MIB),
         name=name,
-    )(*smem, *[pltpu.with_memory_space_constraint(x, pltpu.HBM) for x in hbm], *vmem)
+    )(*smem, *[pltpu.with_memory_space_constraint(x, pltpu.HBM) for x in hbm], *[pltpu.with_memory_space_constraint(x, pltpu.VMEM) for x in kept], *vmem)
 
 
 def cores_share(gru_weight):
     half = gru_weight.shape[1] // 2
-    return lax.axis_size("ev") == 2 and lax.axis_size("lo") % 2 == 0 and half % LANES == 0
-
-
-def weight_rows(gru_weight, begin, end):
-    half = gru_weight.shape[1] // 2
-    core = lax.axis_index("lo") % 2
-    mine = lax.dynamic_slice(gru_weight, (begin, core * half), (end - begin, half))
-    return lax.ppermute(mine, "ev", [(0, 1), (1, 0)])
+    return lax.axis_size("ev") == 2 and lax.axis_size("lo") % 4 == 0 and half % LANES == 0
+
+
+def other_ev(x):
+    return lax.ppermute(x, "ev", [(0, 1), (1, 0)])
+
+
+def other_x(x):
+    return lax.ppermute(x, "lo", [(i, i ^ 2) for i in range(lax.axis_size("lo"))])
 
 
 def other_core(x):
@@ -468,6 +512,8 @@
     freq, phase = time_freq[None, :], time_phase[None, :]
     shape, sent_shape = jax.ShapeDtypeStruct, pltpu.HBM
 
+    shared = cores_share(gru_weight)
+    total, half = gru_weight.shape[0], gru_weight.shape[1] // 2
     rows = call(
         serve_kernel,
         "serve_endpoints",
@@ -477,18 +523,19 @@
         (),
         fetched=(update_serve, memory),
     )
-    shared = cores_share(gru_weight)
     if shared:
         late_weight = after(gru_weight, rows)
-        upper = weight_rows(late_weight, 0, SPLIT)
-        lower = weight_rows(late_weight, SPLIT, gru_weight.shape[0])
-        piece = upper.shape[1]
+        side, column_at = lo // 2 % 2, lo % 2 * half
+        first = other_ev(
+            lax.dynamic_slice(late_weight, (side * SHARED, column_at), (SHARED, half))
+        )
+        piece = half
         core, other = lo % 2, 2 * (1 - ev)
         place = [2 * ev, 2 * ev + 1, other + core, other + 1 - core]
     else:
         whole = lax.all_gather(gru_weight, "ev", axis=1, tiled=True)
         piece, place = whole.shape[1], [jnp.int32(0)]
-    scalars = jnp.stack([hi] + place).astype(jnp.int32)
+    scalars = jnp.stack([hi] + place + [lo // 2 % 2]).astype(jnp.int32)
     fetched = exchange(rows.reshape(devices, cap, width), BOTH).reshape(slots, width)
 
     lookup_row = lookup_serve
@@ -498,51 +545,57 @@
             ((0, 0), (0, block - cap_lookup)),
             constant_values=-1,
         ).reshape(1, devices * block)
-    late_lookup = after(lookup_row, rows)
-    other_lookup = other_half(late_lookup)
     raw = (
-        update_serve,
+        after(update_serve, rows),
         last_time[None, :],
         event_time[None, :],
         edge_features.T,
         update_slot.T,
-        neighbour_gap.T,
-        late_lookup,
+        lookup_row,
         freq,
         phase,
     )
-    column = pltpu.VMEM((devices * block, LANES), F32)
-    tau, enc, swap, sent, near_column = call(
+    tau, swap, sent, near_column = call(
         functools.partial(prepare_kernel, enc_width, group),
         "prepare",
         (
-            shape((slots, LANES), F32),
-            shape((events * neighbour_gap.shape[1], LANES), BF),
-            shape((slots, slots), BF),
-            shape((slots, LANES), BF),
-            shape((near * block, LANES), F32),
+            pltpu.VMEM((slots + 16, LANES), F32),
+            pltpu.VMEM((slots, slots), BF),
+            pltpu.VMEM((slots, LANES), BF),
+            sent_shape((near * block, LANES), F32),
         ),
         (scalars,),
         raw,
         (),
         fetched=raw,
-        scratch=(column,),
-    )
+        scratch=(
+            pltpu.VMEM((devices * block, LANES), F32),
+            pltpu.VMEM((near * block, LANES), F32),
+        ),
+        left=(3,),
+    )
+    if shared:
+        sent = after(sent, first)
     message = call(
         partner_kernel,
         "partner_rows",
         sent_shape((slots, width + LANES), BF),
         (),
         (),
-        (swap, sent, fetched),
+        (fetched,),
+        kept=(swap, sent),
     )
     if shared:
-        upper, lower = after(upper, message), after(lower, message)
-        pieces = [upper, lower, other_core(upper), other_core(lower)]
+        late_weight = after(gru_weight, rows)
+        lower = other_ev(lax.dynamic_slice(late_weight, (DIRECT, column_at), (total - DIRECT, half)))
+        first = after(first, message)
+        second = other_x(first)
+        pieces = [first, second, after(lower, second)]
+        pieces += [other_core(x) for x in pieces]
     else:
         pieces = [whole]
     message = exchange(message.reshape(devices, cap, width + LANES), BOTH)
-    raw = (update_serve, freq, phase, gru_bias, memory, gru_weight)
+    raw = (update_serve, memory, gru_bias, near_column, gru_weight)
     parts = pltpu.VMEM((3 * width // piece, nodes, piece), F32)
     new_memory, extended, near_rows = call(
         functools.partial(update_kernel, enc_width, edge_width, shared),
@@ -554,13 +607,21 @@
         ),
         (scalars, hub_node),
         raw,
-        (tau, near_column, message.reshape(slots, width + LANES), *pieces),
+        (message.reshape(slots, width + LANES), *pieces),
+        kept=(tau,),
         fetched=raw,
-        scratch=(parts, parts),
+        scratch=(
+            parts,
+            parts,
+            pltpu.VMEM((nodes + 16, width), BF),
+            pltpu.VMEM((near * block, width), BF),
+        ),
+        left=(0, 1, 2),
         limit=28,
     )
     other_extended = other_half(extended)
     near_looked = exchange(near_rows.reshape(near, block, width), NEAR)
+    other_lookup = other_half(after(lookup_row, message))
     far_rows = call(
         functools.partial(far_kernel, group),
         "far_rows",
@@ -569,26 +630,38 @@
         (other_lookup, extended),
         (other_extended,),
         fetched=(other_lookup, shape((16, width), BF)),
-        scratch=(column, pltpu.VMEM((near * block, LANES), F32)),
+        scratch=(
+            pltpu.VMEM((devices * block, LANES), F32),
+            pltpu.VMEM((near * block, LANES), F32),
+        ),
     )
     far_looked = exchange(far_rows, NEAR)
-    slot_row = lookup_slot.T
-    picked = call(
+    raw = (lookup_slot.T, hub_choice.T, neighbour_gap.T, freq, phase)
+    routes, near_count = lookup_slot.shape[1] * events, neighbour_gap.shape[1] * events
+    picked, far_index, hub_index, enc, own_enc = call(
         functools.partial(pick_kernel, cap_lookup, lo_size),
         "pick_near",
-        shape((lookup_slot.shape[1] * events, width), BF),
+        (
+            pltpu.VMEM((routes, width), BF),
+            pltpu.VMEM(lookup_slot.T.shape, F32),
+            pltpu.VMEM(hub_choice.T.shape, F32),
+            sent_shape((near_count, LANES), BF),
+            pltpu.VMEM((8, LANES), BF),
+        ),
         (scalars,),
-        (),
-        (slot_row, near_looked),
-    )
-    raw = (slot_row, hub_choice.T, phase, query_weight, keyval_weight, output_weight)
+        raw,
+        (near_looked,),
+        fetched=raw,
+    )
+    raw = (keyval_weight, enc, query_weight, output_weight)
     embedding = call(
-        functools.partial(attend_kernel, cap_lookup, lo_size),
+        attend_kernel,
         "attend",
         sent_shape((events, width), BF),
-        (scalars,),
+        (),
         raw,
-        (enc, picked, far_looked),
+        (far_looked,),
+        kept=(picked, far_index, hub_index, own_enc),
         fetched=raw,
     )
     return (new_memory, embedding)

time: 118 us -> 110 us (0.932)
  waiting for transfers between devices: 59.4 us -> 50.6 us
  starting transfers between devices: 27.2 us -> 29.9 us
  local copies, waits for them, and re-layouts: 6.37 us -> 3.88 us
    all_to_all x4, waiting for transfers between devices: 22.8 us -> 14.9 us  [exchange(): return lax.all_to_all(x, axes, split_axis=0, concat_axis=0, tiled=True)]
    unnamed x14 -> x4, local copies, waits for them, and re-layouts: 3.1 us -> 0.59 us
    all_to_all x4, starting transfers between devices: 20.8 us -> 22.4 us  [exchange(): return lax.all_to_all(x, axes, split_axis=0, concat_axis=0, tiled=True)]
    ppermute x2 -> x3, waiting for transfers between devices: 21.2 us -> 19.9 us  [the longest x2 19.3 us: other_ev(): return lax.ppermute(x, 'ev', [(0, 1), (1, 0)])]
    ppermute x2 -> x3, starting transfers between devices: 3.49 us -> 3.92 us  [the longest x2 2.09 us: other_ev(): return lax.ppermute(x, 'ev', [(0, 1), (1, 0)])]
  transfers between devices with their start and end apart: 10 -> 12, of which waited for: 7 -> 10; matrix products, arithmetic and copies ran while one was open for 3% -> 3% of each run, Pallas kernels for 7% -> 9%
where the time goes in v3:
time: 110 us
  waiting for transfers between devices  50.6 us (46%)
  starting transfers between devices  29.9 us (27%)
  Pallas kernels  23.7 us (22%)
  local copies, waits for them, and re-layouts  3.88 us (4%)
  between operations  1.42 us (1%)
    pallas_call x7, Pallas kernels, call(): pl.pallas_call(kernel, out_shape=out_shape, in_specs=[SMEM] * len(smem) +...  23.7 us
    all_to_all x4, starting transfers between devices, exchange(): return lax.all_to_all(x, axes, split_axis=0, concat_axis=0, tiled=True)  22.4 us
    ppermute x2, waiting for transfers between devices, other_ev(): return lax.ppermute(x, 'ev', [(0, 1), (1, 0)])  19.3 us
    all_to_all x4, waiting for transfers between devices, exchange(): return lax.all_to_all(x, axes, split_axis=0, concat_axis=0, tiled=True)  14.9 us
    ppermute x2, waiting for transfers between devices, other_half(): return lax.ppermute(x, 'hi', [(0, 1), (1, 0)])  14 us
    ppermute x2, starting transfers between devices, other_half(): return lax.ppermute(x, 'hi', [(0, 1), (1, 0)])  2.99 us
  transfers between devices with their start and end apart: 12, of which 10 were waited for; matrix products, arithmetic and copies ran while one was open for 3% of the time, Pallas kernels for 9%

profile of v3, /device:TPU:0, one launch (start us, length us, event | category | flops | bytes accessed | tf_op | source)
XLA Modules:
  0.0 109.5 jit_solution(4781068770927948193)
XLA Ops:
  0.6 2.1 %serve_endpoints.1 = bf16[512,512]{1,0:T(8,128)(2,1)} custom-call(s32[1,512]{1,0:T(1,128)} %serve_hbm.4, bf16[256,512]{1,0:T(8,128)(2,1)} %memory_hbm.3), custom_call_target="tpu_custom_call" | custom-call | tf_op jit(solution)/shard_map/serve_endpoints/pallas_call | solution.py:447
  2.7 7.3 %all-to-all-start = ((bf16[32,16,512]{2,1,0:T(8,128)(2,1)}), bf16[32,16,512]{2,1,0:T(8,128)(2,1)S(1)}, u32[]{:S(2)}, u32[]{:S(2)}) async-start(bf16[32,16,512]{2,1,0:T(8,128)(2,1)} %bitcast.23), calls=%async_computation | async-start | bytes 1048576 | tf_op jit(solution)/shard_map/all_to_all | solution.py:435
  10.1 1.1 %dynamic_slice.6 = bf16[384,384]{1,0:T(8,128)(2,1)S(1)} dynamic-slice(bf16[1684,768]{1,0:T(8,128)(2,1)} %own_weight_hbm.1, s32[]{:T(128)S(6)} %select_n.30, s32[]{:T(128)S(6)} %select_n.31), dynamic_slice_sizes={384,384} | dynamic-slice | bytes 589828 | tf_op jit(solution)/shard_map/dynamic_slice | solution.py:530
  11.2 1.8 %collective-permute-start = (bf16[384,384]{1,0:T(8,128)(2,1)S(1)}, bf16[384,384]{1,0:T(8,128)(2,1)S(1)}, u32[]{:S(2)}, u32[]{:S(2)}) collective-permute-start(bf16[384,384]{1,0:T(8,128)(2,1)S(1)} %dynamic_slice.6), channel_id=1, source_target_pairs={{0,16},{16,0},{1,17},{17,1},{2,18},{18,2},{3,19},{19,3},{4,20},{20... | collective-permute-start | bytes 884744 | tf_op jit(solution)/shard_map/ppermute | solution.py:464
  13.1 2.1 %constant_dynamic-slice_fusion = bf16[916,384]{1,0:T(8,128)(2,1)} fusion(bf16[1684,768]{1,0:T(8,128)(2,1)} %own_weight_hbm.1, s32[]{:T(128)S(6)} %select_n.31), kind=kLoop, calls=%fused_computation | loop fusion | bytes 1406980 | tf_op jit(solution)/shard_map/dynamic_slice | solution.py:590
  15.1 0.3 collective-permute-start.2
  15.4 0.1 stack.27.scalar_ref
  15.5 2.5 %prepare.1 = (f32[528,128]{1,0:T(8,128)S(1)}, bf16[512,512]{1,0:T(8,128)(2,1)S(1)}, bf16[512,128]{1,0:T(8,128)(2,1)S(1)}, f32[896,128]{1,0:T(8,128)}) custom-call(s32[6]{0:T(128)S(1)} %stack.27.scalar_ref, s32[1,512]{1,0:T(1,128)} %serve_hbm.4, s32[1,256]{1,0:T(1,128)} %bitcast.33, s32[1,128]{1,0:T(1,128)} %bitcast.35, bf16[48,128]{1,0:T(8,128)(2,1)} %bitcast.25, ...), custom_call_target="tpu_custom_call" | custom-call | tf_op jit(solution)/shard_map/prepare/pallas_call | solution.py:447
  18.0 6.6 %collective-permute-done.refs_0_ = bf16[384,384]{1,0:T(8,128)(2,1)S(1)} collective-permute-done((bf16[384,384]{1,0:T(8,128)(2,1)S(1)}, bf16[384,384]{1,0:T(8,128)(2,1)S(1)}, u32[]{:S(2)}, u32[]{:S(2)}) %collective-permute-start) | collective-permute-done | bytes 294944 | tf_op jit(solution)/shard_map/ppermute | solution.py:464
  24.6 1.4 %all-to-all-done = bf16[32,16,512]{2,1,0:T(8,128)(2,1)S(1)} async-done(((bf16[32,16,512]{2,1,0:T(8,128)(2,1)}), bf16[32,16,512]{2,1,0:T(8,128)(2,1)S(1)}, u32[]{:S(2)}, u32[]{:S(2)}) %all-to-all-start) | async-done | bytes 524320 | tf_op jit(solution)/shard_map/all_to_all | solution.py:435
  26.0 1.3 %partner_rows.1 = bf16[512,640]{1,0:T(8,128)(2,1)} custom-call(bf16[512,512]{1,0:T(8,128)(2,1)S(1)} %get-tuple-element.23.swap_ref, bf16[512,128]{1,0:T(8,128)(2,1)S(1)} %get-tuple-element.26.sent_ref, bf16[512,512]{1,0:T(8,128)(2,1)S(1)} %bitcast.21), custom_call_target="tpu_custom_call" | custom-call | tf_op jit(solution)/shard_map/partner_rows/pallas_call | solution.py:447
  27.3 3.5 %all-to-all-start.1 = ((bf16[32,16,640]{2,1,0:T(8,128)(2,1)}), bf16[32,16,640]{2,1,0:T(8,128)(2,1)S(1)}, u32[]{:S(2)}, u32[]{:S(2)}) async-start(bf16[32,16,640]{2,1,0:T(8,128)(2,1)} %bitcast.22), calls=%async_computation.1 | async-start | bytes 1310720 | tf_op jit(solution)/shard_map/all_to_all | solution.py:435
  30.8 1.8 %collective-permute-start.1 = (bf16[384,384]{1,0:T(8,128)(2,1)S(1)}, bf16[384,384]{1,0:T(8,128)(2,1)S(1)}, u32[]{:S(2)}, u32[]{:S(2)}) collective-permute-start(bf16[384,384]{1,0:T(8,128)(2,1)S(1)} %collective-permute-done.refs_0_), channel_id=1, source_target_pairs={{0,2},{1,3},{2,0},{3,1},{4,6},{5,7},{6,4},{7,5},{8,10},{9,11},{10,... | collective-permute-start | bytes 884744 | tf_op jit(solution)/shard_map/ppermute | solution.py:468
  32.6 12.7 %collective-permute-done.2.refs_2_ = bf16[916,384]{1,0:T(8,128)(2,1)S(1)} collective-permute-done((bf16[916,384]{1,0:T(8,128)(2,1)}, bf16[916,384]{1,0:T(8,128)(2,1)S(1)}, u32[]{:S(2)}, u32[]{:S(2)}) %collective-permute-start.2) | collective-permute-done | bytes 703520 | tf_op jit(solution)/shard_map/ppermute | solution.py:464
  45.4 0.5 collective-permute-done.1.refs_1_
  45.9 0.0 collective-permute-start.5
  45.9 0.5 collective-permute-start.3
  46.4 0.0 collective-permute-start.4
  47.1 1.4 %collective-permute-done.3.refs_3_ = bf16[384,384]{1,0:T(8,128)(2,1)S(1)} collective-permute-done((bf16[384,384]{1,0:T(8,128)(2,1)S(1)}, bf16[384,384]{1,0:T(8,128)(2,1)S(1)}, u32[]{:S(2)}, u32[]{:S(2)}) %collective-permute-start.3) | collective-permute-done | bytes 294944 | tf_op jit(solution)/shard_map/ppermute | solution.py:472
  48.5 0.4 collective-permute-done.4.refs_4_
  48.9 0.0 collective-permute-done.5.refs_5_
  48.9 0.6 all-to-all-done.1
  49.5 0.0 copy-start
  49.5 6.2 %update_memory.1 = (bf16[256,512]{1,0:T(8,128)(2,1)}, bf16[272,512]{1,0:T(8,128)(2,1)}, bf16[896,512]{1,0:T(8,128)(2,1)}) custom-call(s32[6]{0:T(128)S(1)} %stack.27.scalar_ref, s32[1]{0:T(128)S(6)} %copy.20.hub_ref, s32[1,512]{1,0:T(1,128)} %serve_hbm.4, bf16[256,512]{1,0:T(8,128)(2,1)} %memory_hbm.3, f32[2,1536]{1,0:T(2,128)} %bias_hbm.1, ...), custom_call_target="tpu_custom_call" | custom-call | tf_op jit(solution)/shard_map/update_memory/pallas_call | solution.py:447
  55.7 3.8 %all-to-all-start.2 = ((bf16[16,56,512]{2,1,0:T(8,128)(2,1)}), bf16[16,56,512]{2,1,0:T(8,128)(2,1)S(1)}, u32[]{:S(2)}, u32[]{:S(2)}) async-start(bf16[16,56,512]{2,1,0:T(8,128)(2,1)} %bitcast.24), calls=%async_computation.2 | async-start | bytes 1835008 | tf_op jit(solution)/shard_map/all_to_all | solution.py:435
  59.6 2.9 %collective-permute-start.7 = (bf16[272,512]{1,0:T(8,128)(2,1)}, bf16[272,512]{1,0:T(8,128)(2,1)S(1)}, u32[]{:S(2)}, u32[]{:S(2)}) collective-permute-start(bf16[272,512]{1,0:T(8,128)(2,1)} %get-tuple-element.37.own_hbm), channel_id=1, source_target_pairs={{0,8},{8,0},{1,9},{9,1},{2,10},{10,2},{3,11},{11,3},{4,12},{12,4},... | collective-permute-start | bytes 835592 | tf_op jit(solution)/shard_map/ppermute | solution.py:476
  62.4 0.0 copy-done
  62.4 0.1 collective-permute-start.6
  62.6 14.0 %collective-permute-done.6.lookup_hbm = s32[1,1792]{1,0:T(1,128)S(1)} collective-permute-done((s32[1,1792]{1,0:T(1,128)S(1)}, s32[1,1792]{1,0:T(1,128)S(1)}, u32[]{:S(2)}, u32[]{:S(2)}) %collective-permute-start.6) | collective-permute-done | bytes 7200 | tf_op jit(solution)/shard_map/ppermute | solution.py:476
  76.5 0.0 copy-start.1
  76.5 0.0 collective-permute-done.7.other_ref
  76.5 0.6 copy-done.1
  77.1 3.0 %far_rows.1 = bf16[16,64,512]{2,1,0:T(8,128)(2,1)} custom-call(s32[6]{0:T(128)S(1)} %stack.27.scalar_ref, s32[1,1792]{1,0:T(1,128)} %copy-done.1, bf16[272,512]{1,0:T(8,128)(2,1)} %get-tuple-element.37.own_hbm, bf16[272,512]{1,0:T(8,128)(2,1)S(1)} %collective-permute-done.7.other_ref), custom_call_target="tpu_custom_call" | custom-call | tf_op jit(solution)/shard_map/far_rows/pallas_call | solution.py:447
  80.1 0.3 all-to-all-done.2.looked_ref
  80.4 7.8 %all-to-all-start.3 = ((bf16[16,64,512]{2,1,0:T(8,128)(2,1)}), bf16[16,64,512]{2,1,0:T(8,128)(2,1)S(1)}, u32[]{:S(2)}, u32[]{:S(2)}) async-start(bf16[16,64,512]{2,1,0:T(8,128)(2,1)} %far_rows.1), calls=%async_computation.3 | async-start | bytes 2097152 | tf_op jit(solution)/shard_map/all_to_all | solution.py:435
  88.2 3.6 %pick_near.1 = (bf16[896,512]{1,0:T(8,128)(2,1)S(1)}, f32[7,128]{1,0:T(8,128)S(1)}, f32[4,128]{1,0:T(4,128)S(1)}, bf16[1280,128]{1,0:T(8,128)(2,1)}, bf16[8,128]{1,0:T(8,128)(2,1)S(1)}) custom-call(s32[6]{0:T(128)S(1)} %stack.27.scalar_ref, s32[7,128]{1,0:T(8,128)} %bitcast.27, s32[4,128]{1,0:T(4,128)} %bitcast.28, s32[10,128]{1,0:T(8,128)} %bitcast.26, ...), custom_call_target="tpu_custom_call" | custom-call | tf_op jit(solution)/shard_map/pick_near/pallas_call | solution.py:447
  91.8 12.6 %all-to-all-done.3.looked_ref = bf16[16,64,512]{2,1,0:T(8,128)(2,1)S(1)} async-done(((bf16[16,64,512]{2,1,0:T(8,128)(2,1)}), bf16[16,64,512]{2,1,0:T(8,128)(2,1)S(1)}, u32[]{:S(2)}, u32[]{:S(2)}) %all-to-all-start.3) | async-done | bytes 1048608 | tf_op jit(solution)/shard_map/all_to_all | solution.py:435
  104.4 5.1 %attend.1 = bf16[128,512]{1,0:T(8,128)(2,1)} custom-call(bf16[612,512]{1,0:T(8,128)(2,1)} %keyval_hbm.1, bf16[1280,128]{1,0:T(8,128)(2,1)} %get-tuple-element.31.enc_hbm, bf16[612,256]{1,0:T(8,128)(2,1)} %query_hbm.1, bf16[768,512]{1,0:T(8,128)(2,1)} %output_hbm.1, bf16[896,512]{1,0:T(8,128)(2,1)S(1)} %get-tuple-element.32.picked_ref, ...), custom_call_target="tpu_custom_call" | custom-call | tf_op jit(solution)/shard_map/attend/pallas_call | solution.py:447
Async XLA Ops:
  2.7 23.2 %all-to-all-start = ((bf16[32,16,512]{2,1,0:T(8,128)(2,1)}), bf16[32,16,512]{2,1,0:T(8,128)(2,1)S(1)}, u32[]{:S(2)}, u32[]{:S(2)}) async-start(bf16[32,16,512]{2,1,0:T(8,128)(2,1)} %bitcast.23), calls=%async_computation | async-start | bytes 1048576 | tf_op jit(solution)/shard_map/all_to_all | solution.py:435
  11.2 13.4 %collective-permute-start = (bf16[384,384]{1,0:T(8,128)(2,1)S(1)}, bf16[384,384]{1,0:T(8,128)(2,1)S(1)}, u32[]{:S(2)}, u32[]{:S(2)}) collective-permute-start(bf16[384,384]{1,0:T(8,128)(2,1)S(1)} %dynamic_slice.6), channel_id=1, source_target_pairs={{0,16},{16,0},{1,17},{17,1},{2,18},{18,2},{3,19},{19,3},{4,20},{20... | collective-permute-start | bytes 884744 | tf_op jit(solution)/shard_map/ppermute | solution.py:464
  15.1 30.2 %collective-permute-start.2 = (bf16[916,384]{1,0:T(8,128)(2,1)}, bf16[916,384]{1,0:T(8,128)(2,1)S(1)}, u32[]{:S(2)}, u32[]{:S(2)}) collective-permute-start(bf16[916,384]{1,0:T(8,128)(2,1)} %constant_dynamic-slice_fusion), channel_id=1, source_target_pairs={{0,16},{16,0},{1,17},{17,1},{2,18},{18,2},{3,19},{19,3},{4,20},{20... | collective-permute-start | bytes 2110472 | tf_op jit(solution)/shard_map/ppermute | solution.py:464
  27.3 22.3 %all-to-all-start.1 = ((bf16[32,16,640]{2,1,0:T(8,128)(2,1)}), bf16[32,16,640]{2,1,0:T(8,128)(2,1)S(1)}, u32[]{:S(2)}, u32[]{:S(2)}) async-start(bf16[32,16,640]{2,1,0:T(8,128)(2,1)} %bitcast.22), calls=%async_computation.1 | async-start | bytes 1310720 | tf_op jit(solution)/shard_map/all_to_all | solution.py:435
  30.8 15.1 %collective-permute-start.1 = (bf16[384,384]{1,0:T(8,128)(2,1)S(1)}, bf16[384,384]{1,0:T(8,128)(2,1)S(1)}, u32[]{:S(2)}, u32[]{:S(2)}) collective-permute-start(bf16[384,384]{1,0:T(8,128)(2,1)S(1)} %collective-permute-done.refs_0_), channel_id=1, source_target_pairs={{0,2},{1,3},{2,0},{3,1},{4,6},{5,7},{6,4},{7,5},{8,10},{9,11},{10,... | collective-permute-start | bytes 884744 | tf_op jit(solution)/shard_map/ppermute | solution.py:468
  45.9 3.0 %collective-permute-start.5 = (bf16[916,384]{1,0:T(8,128)(2,1)S(1)}, bf16[916,384]{1,0:T(8,128)(2,1)S(1)}, u32[]{:S(2)}, u32[]{:S(2)}) collective-permute-start(bf16[916,384]{1,0:T(8,128)(2,1)S(1)} %collective-permute-done.2.refs_2_), channel_id=1, source_target_pairs={{0,1},{1,0},{2,3},{3,2},{4,5},{5,4},{6,7},{7,6},{8,9},{9,8},{10,11... | collective-permute-start | bytes 2110472 | tf_op jit(solution)/shard_map/ppermute | solution.py:472
  45.9 2.6 %collective-permute-start.3 = (bf16[384,384]{1,0:T(8,128)(2,1)S(1)}, bf16[384,384]{1,0:T(8,128)(2,1)S(1)}, u32[]{:S(2)}, u32[]{:S(2)}) collective-permute-start(bf16[384,384]{1,0:T(8,128)(2,1)S(1)} %collective-permute-done.refs_0_), channel_id=1, source_target_pairs={{0,1},{1,0},{2,3},{3,2},{4,5},{5,4},{6,7},{7,6},{8,9},{9,8},{10,11... | collective-permute-start | bytes 884744 | tf_op jit(solution)/shard_map/ppermute | solution.py:472
  46.4 2.5 %collective-permute-start.4 = (bf16[384,384]{1,0:T(8,128)(2,1)S(1)}, bf16[384,384]{1,0:T(8,128)(2,1)S(1)}, u32[]{:S(2)}, u32[]{:S(2)}) collective-permute-start(bf16[384,384]{1,0:T(8,128)(2,1)S(1)} %collective-permute-done.1.refs_1_), channel_id=1, source_target_pairs={{0,1},{1,0},{2,3},{3,2},{4,5},{5,4},{6,7},{7,6},{8,9},{9,8},{10,11... | collective-permute-start | bytes 884744 | tf_op jit(solution)/shard_map/ppermute | solution.py:472
  49.5 12.9 %copy-start = (s32[1,1792]{1,0:T(1,128)S(1)}, s32[1,1792]{1,0:T(1,128)}, u32[]{:S(2)}) copy-start(s32[1,1792]{1,0:T(1,128)} %lookup_hbm.1) | copy-start | bytes 21508
  55.7 24.7 %all-to-all-start.2 = ((bf16[16,56,512]{2,1,0:T(8,128)(2,1)}), bf16[16,56,512]{2,1,0:T(8,128)(2,1)S(1)}, u32[]{:S(2)}, u32[]{:S(2)}) async-start(bf16[16,56,512]{2,1,0:T(8,128)(2,1)} %bitcast.24), calls=%async_computation.2 | async-start | bytes 1835008 | tf_op jit(solution)/shard_map/all_to_all | solution.py:435
  59.6 17.0 %collective-permute-start.7 = (bf16[272,512]{1,0:T(8,128)(2,1)}, bf16[272,512]{1,0:T(8,128)(2,1)S(1)}, u32[]{:S(2)}, u32[]{:S(2)}) collective-permute-start(bf16[272,512]{1,0:T(8,128)(2,1)} %get-tuple-element.37.own_hbm), channel_id=1, source_target_pairs={{0,8},{8,0},{1,9},{9,1},{2,10},{10,2},{3,11},{11,3},{4,12},{12,4},... | collective-permute-start | bytes 835592 | tf_op jit(solution)/shard_map/ppermute | solution.py:476
  62.4 14.1 %collective-permute-start.6 = (s32[1,1792]{1,0:T(1,128)S(1)}, s32[1,1792]{1,0:T(1,128)S(1)}, u32[]{:S(2)}, u32[]{:S(2)}) collective-permute-start(s32[1,1792]{1,0:T(1,128)S(1)} %copy-done), channel_id=1, source_target_pairs={{0,8},{8,0},{1,9},{9,1},{2,10},{10,2},{3,11},{11,3},{4,12},{12,4},... | collective-permute-start | bytes 21512 | tf_op jit(solution)/shard_map/ppermute | solution.py:476
  76.5 0.6 copy-start.1
  80.4 24.0 %all-to-all-start.3 = ((bf16[16,64,512]{2,1,0:T(8,128)(2,1)}), bf16[16,64,512]{2,1,0:T(8,128)(2,1)S(1)}, u32[]{:S(2)}, u32[]{:S(2)}) async-start(bf16[16,64,512]{2,1,0:T(8,128)(2,1)} %far_rows.1), calls=%async_computation.3 | async-start | bytes 2097152 | tf_op jit(solution)/shard_map/all_to_all | solution.py:435

commit v4 on v3

--- a/solution.py
+++ b/solution.py
@@ -14,8 +14,8 @@
 DIRECT = 2 * SHARED
 BF = jnp.bfloat16
 F32 = jnp.float32
-BOTH = ("ev", "hi", "lo")
-NEAR = ("ev", "lo")
+BOTH = ("ev", "hi", "low", "rest")
+NEAR = ("ev", "rest", "low")
 VMEM = pl.BlockSpec(memory_space=pltpu.VMEM)
 SMEM = pl.BlockSpec(memory_space=pltpu.SMEM)
 HBM = pl.BlockSpec(memory_space=pltpu.HBM)
@@ -89,7 +89,7 @@
 
 def prepare_kernel(
     enc_width,
-    group,
+    sizes,
     scalar_ref,
     serve_hbm,
     time_hbm,
@@ -102,7 +102,8 @@
     tau_ref,
     swap_ref,
     sent_ref,
-    near_hbm,
+    near_ref,
+    away_ref,
     serve,
     time,
     stamp,
@@ -112,7 +113,6 @@
     freq,
     phase,
     column,
-    near,
     sems,
 ):
     copies = fetch(
@@ -131,9 +131,8 @@
     for copy in copies:
         copy.wait()
     column[...] = columns(lookup[...].astype(F32))
-    own_half(scalar_ref[0], column, near, group)
-    out = pltpu.make_async_copy(near, near_hbm, sems.at[0])
-    out.start()
+    of_half(scalar_ref[0], column, near_ref, *sizes)
+    of_half(1 - scalar_ref[0], column, away_ref, *sizes)
     picks = one_hot(columns(serve[...].astype(F32)), time.shape[1]).astype(F32)
     tau = jnp.sum(picks * time[...].astype(F32), axis=1, keepdims=True)
     slots = serve.shape[1]
@@ -161,13 +160,23 @@
     extra = jnp.where(line == rest, high, extra)
     extra = jnp.where(line == rest + 1, stamps - 8.0 * high, extra)
     sent_ref[...] = dot_t((first + second).astype(BF), extra.astype(BF)).astype(BF)
-    out.wait()
-
-
-def own_half(hi, column, near_ref, group):
-    for e in range(near_ref.shape[0] // group):
-        start = pl.multiple_of((2 * e + hi) * group, 8)
-        near_ref[e * group : (e + 1) * group, :] = column[pl.ds(start, group), :]
+
+
+def of_half(half, column, rows_ref, ev_size, low_size, rest_size):
+    block = column.shape[0] // (ev_size * 2 * low_size * rest_size)
+    parts = []
+    for e in range(ev_size):
+        for r in range(rest_size):
+            for w in range(low_size):
+                start = ((2 * e + half) * low_size + w) * rest_size + r
+                parts.append(column[pl.ds(pl.multiple_of(start * block, 8), block), :])
+    joined = jnp.concatenate(parts, axis=0)
+    for i in range(rows_ref.shape[0]):
+        rows_ref[i : i + 1, :] = joined[i * LANES : (i + 1) * LANES, :].T[:1, :]
+
+
+def flat_columns(rows_ref, begin, end):
+    return jnp.concatenate([columns(rows_ref[i : i + 1, :]) for i in range(begin, end)], axis=0)
 
 
 def partner_kernel(swap_ref, sent_ref, fetched_ref, out_ref):
@@ -185,17 +194,18 @@
     serve_hbm,
     memory_hbm,
     bias_hbm,
-    near_hbm,
     own_weight_hbm,
     tau_ref,
+    near_ref,
+    away_ref,
     message_ref,
     *refs,
 ):
     count = 6 if shared else 1
     weight_refs, refs = refs[:count], refs[count:]
-    new_hbm, extended_hbm, rows_hbm, serve, memory_ref, bias, near_ref, own_weight = refs[:8]
-    pre, hid, out, rows_out, sems = refs[8:]
-    pairs = [(serve_hbm, serve), (memory_hbm, memory_ref), (bias_hbm, bias), (near_hbm, near_ref)]
+    new_hbm, extended_hbm, rows_hbm, serve, memory_ref, bias, own_weight = refs[:7]
+    pre, hid, out, rows_out, sems = refs[7:]
+    pairs = [(serve_hbm, serve), (memory_hbm, memory_ref), (bias_hbm, bias)]
     pairs += [(own_weight_hbm, own_weight)] if shared else []
     copies = fetch(pairs, sems)
     nodes, width = memory_ref.shape
@@ -243,7 +253,7 @@
                 + dot(left[:, DIRECT:], lower[: msg_width - DIRECT, :])
             )
             hid[where] = dot(hid_left, lower[base - DIRECT :, :])
-        copies[4].wait()
+        copies[3].wait()
         whole(1, own_weight)
     else:
         whole(1, weight_refs[0])
@@ -271,46 +281,53 @@
     entry = lax.broadcasted_iota(jnp.int32, (16, nodes), 1)
     hub = ((entry == hub_ref[0]) & (line == 0)).astype(F32).astype(BF)
     out[nodes:, :] = dot(hub, new).astype(BF)
+    for begin in range(0, away_ref.shape[0], 8):
+        end = min(begin + 8, away_ref.shape[0])
+        some = away_ref[begin:end, :]
+        if end - begin < 8:
+            some = jnp.concatenate([some, jnp.zeros((8 + begin - end, LANES), F32)], axis=0)
+        out[nodes + 8 :, begin * 16 : begin * 16 + LANES] = some.astype(BF)
     sends = [
         pltpu.make_async_copy(out, extended_hbm, sems.at[0]),
         pltpu.make_async_copy(out.at[:nodes, :], new_hbm, sems.at[1]),
     ]
     for send in sends:
         send.start()
-    copies[3].wait()
-    total = near_ref.shape[0]
-    part = total // 2
-    for i in range(2):
-        some = slice(i * part, (i + 1) * part)
-        rows_out[some, :] = dot(one_hot(near_ref[some, :], nodes), new).astype(BF)
+    count = near_ref.shape[0]
+    for i, (begin, end) in enumerate(((0, count // 2), (count // 2, count))):
+        some = slice(begin * LANES, end * LANES)
+        rows_out[some, :] = dot(one_hot(flat_columns(near_ref, begin, end), nodes), new).astype(BF)
         sends.append(pltpu.make_async_copy(rows_out.at[some, :], rows_hbm.at[some, :], sems.at[2 + i]))
         sends[-1].start()
     for send in sends:
         send.wait()
 
 
-def far_kernel(group, scalar_ref, lookup_hbm, own_hbm, other_ref, out_ref, lookup, hub, column, far, sems):
+def far_kernel(own_hbm, other_ref, out_ref, hub, sems):
     nodes = other_ref.shape[0] - 16
-    copies = fetch([(lookup_hbm, lookup), (own_hbm.at[nodes:, :], hub)], sems)
-    for copy in copies:
-        copy.wait()
-    column[...] = columns(lookup[...].astype(F32))
-    own_half(scalar_ref[0], column, far, group)
-    rows = dot(one_hot(far[...], nodes), other_ref[:nodes, :])
+    copies = fetch([(own_hbm.at[nodes:, :], hub)], sems)
+    count = out_ref.shape[0] * (out_ref.shape[1] - 8) // LANES
+    wanted = other_ref[nodes:, :].astype(F32)[8:, :]
+    index = [wanted[i % 8 : i % 8 + 1, i // 8 * LANES : (i // 8 + 1) * LANES] for i in range(count)]
+    picks = one_hot(jnp.concatenate([columns(row) for row in index], axis=0), nodes)
+    rows = dot(picks, other_ref[:nodes, :])
     near, block, width = out_ref.shape
     out_ref[:, : block - 8, :] = rows.reshape(near, block - 8, width).astype(BF)
+    copies[0].wait()
     hubs = jnp.concatenate(
         [other_ref[nodes : nodes + 1, :], hub[0:1, :], jnp.zeros((6, width), BF)], axis=0
     )
     out_ref[:, block - 8 :, :] = jnp.broadcast_to(hubs[None], (near, 8, width))
 
 
-def places(slot, hi, cap, lo_size):
+def places(slot, hi, cap, low_size, rest_size):
     owner = floor_div(slot, cap)
-    group = floor_div(owner, lo_size)
-    ev = floor_div(group, 2)
-    relay = ev * lo_size + owner - group * lo_size
-    return relay, group - 2.0 * ev == hi, slot - cap * owner
+    line = floor_div(owner, rest_size)
+    rest = owner - rest_size * line
+    half = floor_div(line, low_size)
+    ev = floor_div(half, 2)
+    relay = (ev * rest_size + rest) * low_size + line - low_size * half
+    return relay, half - 2.0 * ev == hi, slot - cap * owner
 
 
 def picks_of(index, width):
@@ -321,7 +338,7 @@
 
 def pick_kernel(
     cap,
-    lo_size,
+    sizes,
     scalar_ref,
     slot_hbm,
     hub_hbm,
@@ -349,14 +366,14 @@
         copy.wait()
     owners, block, width = looked_ref.shape
     hi = scalar_ref[0].astype(F32)
-    relay, near, place = places(slot[...].astype(F32), hi, cap, lo_size)
+    relay, near, place = places(slot[...].astype(F32), hi, cap, *sizes)
     index = jnp.where(near, relay * block + place, -1.0)
     looked = looked_ref[...].reshape(owners * block, width)
     events = gaps.shape[1]
     picks = [one_hot(columns(index[k : k + 1, :]), owners * block) for k in range(slot.shape[0])]
     picked_ref[...] = dot(jnp.concatenate(picks, axis=0), looked).astype(BF)
     far_ref[...] = jnp.where(near, -1.0, relay * (block + 8) + place)
-    relay, near, place = places(hub[...].astype(F32), hi, 1, lo_size)
+    relay, near, place = places(hub[...].astype(F32), hi, 1, *sizes)
     hub_ref[...] = relay * 8.0 + jnp.where(near, 1.0, 0.0)
     freq_row, phase_row = lanes(freq[...]), lanes(phase[...])
     for k in range(gaps.shape[0]):
@@ -439,7 +456,7 @@
     return lax.optimization_barrier((x, *earlier))[0]
 
 
-def call(kernel, name, out_shape, smem, hbm, vmem, fetched=(), scratch=(), left=(), kept=(), limit=20, extra_sems=0):
+def call(kernel, name, out_shape, smem, hbm, vmem, fetched=(), scratch=(), left=(), kept=(), limit=20, extra_sems=0, flops=0):
     many = isinstance(out_shape, tuple)
     specs = tuple(HBM if x in left else VMEM for x in range(len(out_shape))) if many else VMEM
     copies = [pltpu.VMEM(x.shape, x.dtype) for x in fetched]
@@ -452,12 +469,13 @@
         scratch_shapes=copies + list(scratch) + sems,
         compiler_params=pltpu.CompilerParams(vmem_limit_bytes=limit * MIB),
         name=name,
+        cost_estimate=pl.CostEstimate(flops=flops, bytes_accessed=0, transcendentals=0) if flops else None,
     )(*smem, *[pltpu.with_memory_space_constraint(x, pltpu.HBM) for x in hbm], *[pltpu.with_memory_space_constraint(x, pltpu.VMEM) for x in kept], *vmem)
 
 
 def cores_share(gru_weight):
     half = gru_weight.shape[1] // 2
-    return lax.axis_size("ev") == 2 and lax.axis_size("lo") % 4 == 0 and half % LANES == 0
+    return lax.axis_size("ev") == 2 and lax.axis_size("rest") % 4 == 0 and half % LANES == 0
 
 
 def other_ev(x):
@@ -465,11 +483,11 @@
 
 
 def other_x(x):
-    return lax.ppermute(x, "lo", [(i, i ^ 2) for i in range(lax.axis_size("lo"))])
+    return lax.ppermute(x, "rest", [(i, i ^ 2) for i in range(lax.axis_size("rest"))])
 
 
 def other_core(x):
-    return lax.ppermute(x, "lo", [(i, i ^ 1) for i in range(lax.axis_size("lo"))])
+    return lax.ppermute(x, "rest", [(i, i ^ 1) for i in range(lax.axis_size("rest"))])
 
 
 def other_half(x):
@@ -496,17 +514,17 @@
     keyval_weight,
     output_weight,
 ):
-    ev_size, hi_size, lo_size = (lax.axis_size(a) for a in BOTH)
-    ev, hi, lo = (lax.axis_index(a) for a in BOTH)
-    devices = ev_size * hi_size * lo_size
-    near = ev_size * lo_size
+    ev_size, hi_size, low_size, rest_size = (lax.axis_size(a) for a in BOTH)
+    ev, hi, _, rest_index = (lax.axis_index(a) for a in BOTH)
+    near = ev_size * low_size * rest_size
+    devices = hi_size * near
+    sizes = (ev_size, low_size, rest_size)
     nodes, width = memory.shape
     events = event_time.shape[0]
     slots = update_serve.shape[1]
     cap = slots // devices
     cap_lookup = lookup_serve.shape[1] // devices
     block = -(-cap_lookup // 8) * 8
-    group = lo_size * block
     enc_width = time_freq.shape[0]
     edge_width = edge_features.shape[1]
     freq, phase = time_freq[None, :], time_phase[None, :]
@@ -525,17 +543,17 @@
     )
     if shared:
         late_weight = after(gru_weight, rows)
-        side, column_at = lo // 2 % 2, lo % 2 * half
+        side, column_at = rest_index // 2 % 2, rest_index % 2 * half
         first = other_ev(
             lax.dynamic_slice(late_weight, (side * SHARED, column_at), (SHARED, half))
         )
         piece = half
-        core, other = lo % 2, 2 * (1 - ev)
+        core, other = rest_index % 2, 2 * (1 - ev)
         place = [2 * ev, 2 * ev + 1, other + core, other + 1 - core]
     else:
         whole = lax.all_gather(gru_weight, "ev", axis=1, tiled=True)
         piece, place = whole.shape[1], [jnp.int32(0)]
-    scalars = jnp.stack([hi] + place + [lo // 2 % 2]).astype(jnp.int32)
+    scalars = jnp.stack([hi] + place + [rest_index // 2 % 2]).astype(jnp.int32)
     fetched = exchange(rows.reshape(devices, cap, width), BOTH).reshape(slots, width)
 
     lookup_row = lookup_serve
@@ -555,24 +573,22 @@
         freq,
         phase,
     )
-    tau, swap, sent, near_column = call(
-        functools.partial(prepare_kernel, enc_width, group),
+    rows_shape = pltpu.VMEM((near * block // LANES, LANES), F32)
+    tau, swap, sent, near_index, away_index = call(
+        functools.partial(prepare_kernel, enc_width, sizes),
         "prepare",
         (
             pltpu.VMEM((slots + 16, LANES), F32),
             pltpu.VMEM((slots, slots), BF),
             pltpu.VMEM((slots, LANES), BF),
-            sent_shape((near * block, LANES), F32),
+            rows_shape,
+            rows_shape,
         ),
         (scalars,),
         raw,
         (),
         fetched=raw,
-        scratch=(
-            pltpu.VMEM((devices * block, LANES), F32),
-            pltpu.VMEM((near * block, LANES), F32),
-        ),
-        left=(3,),
+        scratch=(pltpu.VMEM((devices * block, LANES), F32),),
     )
     if shared:
         sent = after(sent, first)
@@ -595,7 +611,7 @@
     else:
         pieces = [whole]
     message = exchange(message.reshape(devices, cap, width + LANES), BOTH)
-    raw = (update_serve, memory, gru_bias, near_column, gru_weight)
+    raw = (update_serve, memory, gru_bias, gru_weight)
     parts = pltpu.VMEM((3 * width // piece, nodes, piece), F32)
     new_memory, extended, near_rows = call(
         functools.partial(update_kernel, enc_width, edge_width, shared),
@@ -608,7 +624,7 @@
         (scalars, hub_node),
         raw,
         (message.reshape(slots, width + LANES), *pieces),
-        kept=(tau,),
+        kept=(tau, near_index, away_index),
         fetched=raw,
         scratch=(
             parts,
@@ -621,25 +637,21 @@
     )
     other_extended = other_half(extended)
     near_looked = exchange(near_rows.reshape(near, block, width), NEAR)
-    other_lookup = other_half(after(lookup_row, message))
     far_rows = call(
-        functools.partial(far_kernel, group),
+        far_kernel,
         "far_rows",
         sent_shape((near, block + 8, width), BF),
-        (scalars,),
-        (other_lookup, extended),
+        (),
+        (extended,),
         (other_extended,),
-        fetched=(other_lookup, shape((16, width), BF)),
-        scratch=(
-            pltpu.VMEM((devices * block, LANES), F32),
-            pltpu.VMEM((near * block, LANES), F32),
-        ),
+        fetched=(shape((16, width), BF),),
+        flops=3 * 10**10,
     )
     far_looked = exchange(far_rows, NEAR)
     raw = (lookup_slot.T, hub_choice.T, neighbour_gap.T, freq, phase)
     routes, near_count = lookup_slot.shape[1] * events, neighbour_gap.shape[1] * events
-    picked, far_index, hub_index, enc, own_enc = call(
-        functools.partial(pick_kernel, cap_lookup, lo_size),
+    picked, pick_far, pick_hub, enc, own_enc = call(
+        functools.partial(pick_kernel, cap_lookup, sizes[1:]),
         "pick_near",
         (
             pltpu.VMEM((routes, width), BF),
@@ -661,7 +673,7 @@
         (),
         raw,
         (far_looked,),
-        kept=(picked, far_index, hub_index, own_enc),
+        kept=(picked, pick_far, pick_hub, own_enc),
         fetched=raw,
     )
     return (new_memory, embedding)
@@ -669,7 +681,7 @@
 
 def solution(mesh):
     ev_size, mem_size = mesh.devices.shape
-    split = jax.sharding.Mesh(mesh.devices.reshape(ev_size, 2, mem_size // 2), BOTH)
+    split = jax.sharding.Mesh(mesh.devices.reshape(ev_size, 2, 2, mem_size // 4), BOTH)
     both = P(BOTH)
     rows = P(BOTH, None)
     return jax.shard_map(

time: 110 us -> 105 us (0.955)
  starting transfers between devices: 29.9 us -> 25.6 us
  Pallas kernels: 23.7 us -> 22.1 us
    all_to_all x4, waiting for transfers between devices: 14.9 us -> 20.1 us  [exchange(): return lax.all_to_all(x, axes, split_axis=0, concat_axis=0, tiled=True)]
    ppermute x2 -> x1, waiting for transfers between devices: 14 us -> 9.27 us  [other_half(): return lax.ppermute(x, 'hi', [(0, 1), (1, 0)])]
    all_to_all x4, starting transfers between devices: 22.4 us -> 18.4 us  [exchange(): return lax.all_to_all(x, axes, split_axis=0, concat_axis=0, tiled=True)]
    pallas_call x7, Pallas kernels: 23.7 us -> 22.1 us  [call(): pl.pallas_call(kernel, out_shape=out_shape, in_specs=[SMEM] * len(smem) +...]
    ppermute x2 -> x1, starting transfers between devices: 2.99 us -> 2.74 us  [other_half(): return lax.ppermute(x, 'hi', [(0, 1), (1, 0)])]
  transfers between devices with their start and end apart: 12 -> 11, of which waited for: 10 -> 10; matrix products, arithmetic and copies ran while one was open for 3% -> 3% of each run, Pallas kernels for 9% -> 8%
where the time goes in v4:
time: 105 us; the launch traced here: 104 us
  waiting for transfers between devices  51.5 us (49%)
  starting transfers between devices  25.6 us (24%)
  Pallas kernels  22.1 us (21%)
  local copies, waits for them, and re-layouts  3.26 us (3%)
  between operations  1.42 us (1%)
    pallas_call x7, Pallas kernels, call(): pl.pallas_call(kernel, out_shape=out_shape, in_specs=[SMEM] * len(smem) +...  22.1 us
    all_to_all x4, waiting for transfers between devices, exchange(): return lax.all_to_all(x, axes, split_axis=0, concat_axis=0, tiled=True)  20.1 us
    ppermute x2, waiting for transfers between devices, other_ev(): return lax.ppermute(x, 'ev', [(0, 1), (1, 0)])  19.7 us
    all_to_all x4, starting transfers between devices, exchange(): return lax.all_to_all(x, axes, split_axis=0, concat_axis=0, tiled=True)  18.4 us
    ppermute x1, waiting for transfers between devices, other_half(): return lax.ppermute(x, 'hi', [(0, 1), (1, 0)])  9.27 us
    ppermute x1, starting transfers between devices, other_half(): return lax.ppermute(x, 'hi', [(0, 1), (1, 0)])  2.74 us
  transfers between devices with their start and end apart: 11, of which 10 were waited for; matrix products, arithmetic and copies ran while one was open for 3% of the time, Pallas kernels for 8%

profile of v4, /device:TPU:0, one launch (start us, length us, event | category | flops | bytes accessed | tf_op | source)
XLA Modules:
  0.0 103.8 jit_solution(13584022258400204409)
XLA Ops:
  0.6 2.1 %serve_endpoints.1 = bf16[512,512]{1,0:T(8,128)(2,1)} custom-call(s32[1,512]{1,0:T(1,128)} %serve_hbm.4, bf16[256,512]{1,0:T(8,128)(2,1)} %memory_hbm.3), custom_call_target="tpu_custom_call" | custom-call | tf_op jit(solution)/shard_map/serve_endpoints/pallas_call | solution.py:464
  2.7 7.3 %all-to-all-start = ((bf16[32,16,512]{2,1,0:T(8,128)(2,1)}), bf16[32,16,512]{2,1,0:T(8,128)(2,1)S(1)}, u32[]{:S(2)}, u32[]{:S(2)}) async-start(bf16[32,16,512]{2,1,0:T(8,128)(2,1)} %bitcast.23), calls=%async_computation | async-start | bytes 1048576 | tf_op jit(solution)/shard_map/all_to_all | solution.py:452
  10.1 1.1 %dynamic_slice.6 = bf16[384,384]{1,0:T(8,128)(2,1)S(1)} dynamic-slice(bf16[1684,768]{1,0:T(8,128)(2,1)} %own_weight_hbm.1, s32[]{:T(128)S(6)} %select_n.30, s32[]{:T(128)S(6)} %select_n.31), dynamic_slice_sizes={384,384} | dynamic-slice | bytes 589828 | tf_op jit(solution)/shard_map/dynamic_slice | solution.py:548
  11.2 1.8 %collective-permute-start = (bf16[384,384]{1,0:T(8,128)(2,1)S(1)}, bf16[384,384]{1,0:T(8,128)(2,1)S(1)}, u32[]{:S(2)}, u32[]{:S(2)}) collective-permute-start(bf16[384,384]{1,0:T(8,128)(2,1)S(1)} %dynamic_slice.6), channel_id=1, source_target_pairs={{0,16},{16,0},{1,17},{17,1},{2,18},{18,2},{3,19},{19,3},{4,20},{20... | collective-permute-start | bytes 884744 | tf_op jit(solution)/shard_map/ppermute | solution.py:482
  13.1 2.0 %constant_dynamic-slice_fusion = bf16[916,384]{1,0:T(8,128)(2,1)} fusion(bf16[1684,768]{1,0:T(8,128)(2,1)} %own_weight_hbm.1, s32[]{:T(128)S(6)} %select_n.31), kind=kLoop, calls=%fused_computation | loop fusion | bytes 1406980 | tf_op jit(solution)/shard_map/dynamic_slice | solution.py:606
  15.1 0.3 collective-permute-start.2
  15.4 0.1 stack.27.scalar_ref
  15.5 2.2 %prepare.1 = (f32[528,128]{1,0:T(8,128)S(1)}, bf16[512,512]{1,0:T(8,128)(2,1)S(1)}, bf16[512,128]{1,0:T(8,128)(2,1)S(1)}, f32[7,128]{1,0:T(8,128)S(1)}, f32[7,128]{1,0:T(8,128)S(1)}) custom-call(s32[6]{0:T(128)S(1)} %stack.27.scalar_ref, s32[1,512]{1,0:T(1,128)} %serve_hbm.4, s32[1,256]{1,0:T(1,128)} %bitcast.33, s32[1,128]{1,0:T(1,128)} %bitcast.35, ...), custom_call_target="tpu_custom_call" | custom-call | tf_op jit(solution)/shard_map/prepare/pallas_call | solution.py:464
  17.6 7.0 %collective-permute-done.refs_0_ = bf16[384,384]{1,0:T(8,128)(2,1)S(1)} collective-permute-done((bf16[384,384]{1,0:T(8,128)(2,1)S(1)}, bf16[384,384]{1,0:T(8,128)(2,1)S(1)}, u32[]{:S(2)}, u32[]{:S(2)}) %collective-permute-start) | collective-permute-done | bytes 294944 | tf_op jit(solution)/shard_map/ppermute | solution.py:482
  24.6 1.4 %all-to-all-done = bf16[32,16,512]{2,1,0:T(8,128)(2,1)S(1)} async-done(((bf16[32,16,512]{2,1,0:T(8,128)(2,1)}), bf16[32,16,512]{2,1,0:T(8,128)(2,1)S(1)}, u32[]{:S(2)}, u32[]{:S(2)}) %all-to-all-start) | async-done | bytes 524320 | tf_op jit(solution)/shard_map/all_to_all | solution.py:452
  26.0 1.3 %partner_rows.1 = bf16[512,640]{1,0:T(8,128)(2,1)} custom-call(bf16[512,512]{1,0:T(8,128)(2,1)S(1)} %get-tuple-element.24.swap_ref, bf16[512,128]{1,0:T(8,128)(2,1)S(1)} %get-tuple-element.27.sent_ref, bf16[512,512]{1,0:T(8,128)(2,1)S(1)} %bitcast.21), custom_call_target="tpu_custom_call" | custom-call | tf_op jit(solution)/shard_map/partner_rows/pallas_call | solution.py:464
  27.3 3.5 %all-to-all-start.1 = ((bf16[32,16,640]{2,1,0:T(8,128)(2,1)}), bf16[32,16,640]{2,1,0:T(8,128)(2,1)S(1)}, u32[]{:S(2)}, u32[]{:S(2)}) async-start(bf16[32,16,640]{2,1,0:T(8,128)(2,1)} %bitcast.22), calls=%async_computation.1 | async-start | bytes 1310720 | tf_op jit(solution)/shard_map/all_to_all | solution.py:452
  30.8 1.8 %collective-permute-start.1 = (bf16[384,384]{1,0:T(8,128)(2,1)S(1)}, bf16[384,384]{1,0:T(8,128)(2,1)S(1)}, u32[]{:S(2)}, u32[]{:S(2)}) collective-permute-start(bf16[384,384]{1,0:T(8,128)(2,1)S(1)} %collective-permute-done.refs_0_), channel_id=1, source_target_pairs={{0,2},{1,3},{2,0},{3,1},{4,6},{5,7},{6,4},{7,5},{8,10},{9,11},{10,... | collective-permute-start | bytes 884744 | tf_op jit(solution)/shard_map/ppermute | solution.py:486
  32.6 12.7 %collective-permute-done.2.refs_2_ = bf16[916,384]{1,0:T(8,128)(2,1)S(1)} collective-permute-done((bf16[916,384]{1,0:T(8,128)(2,1)}, bf16[916,384]{1,0:T(8,128)(2,1)S(1)}, u32[]{:S(2)}, u32[]{:S(2)}) %collective-permute-start.2) | collective-permute-done | bytes 703520 | tf_op jit(solution)/shard_map/ppermute | solution.py:482
  45.4 0.6 collective-permute-done.1.refs_1_
  45.9 0.0 collective-permute-start.5
  45.9 0.5 collective-permute-start.3
  46.4 0.0 collective-permute-start.4
  47.1 1.4 %collective-permute-done.3.refs_3_ = bf16[384,384]{1,0:T(8,128)(2,1)S(1)} collective-permute-done((bf16[384,384]{1,0:T(8,128)(2,1)S(1)}, bf16[384,384]{1,0:T(8,128)(2,1)S(1)}, u32[]{:S(2)}, u32[]{:S(2)}) %collective-permute-start.3) | collective-permute-done | bytes 294944 | tf_op jit(solution)/shard_map/ppermute | solution.py:490
  48.5 0.4 collective-permute-done.4.refs_4_
  48.9 0.0 collective-permute-done.5.refs_5_
  48.9 0.6 all-to-all-done.1
  49.5 6.1 %update_memory.1 = (bf16[256,512]{1,0:T(8,128)(2,1)}, bf16[272,512]{1,0:T(8,128)(2,1)}, bf16[896,512]{1,0:T(8,128)(2,1)}) custom-call(s32[6]{0:T(128)S(1)} %stack.27.scalar_ref, s32[1]{0:T(128)S(6)} %copy.20.hub_ref, s32[1,512]{1,0:T(1,128)} %serve_hbm.4, bf16[256,512]{1,0:T(8,128)(2,1)} %memory_hbm.3, f32[2,1536]{1,0:T(2,128)} %bias_hbm.1, ...), custom_call_target="tpu_custom_call" | custom-call | tf_op jit(solution)/shard_map/update_memory/pallas_call | solution.py:464
  55.6 2.7 %collective-permute-start.6 = (bf16[272,512]{1,0:T(8,128)(2,1)}, bf16[272,512]{1,0:T(8,128)(2,1)S(1)}, u32[]{:S(2)}, u32[]{:S(2)}) collective-permute-start(bf16[272,512]{1,0:T(8,128)(2,1)} %get-tuple-element.37.own_hbm), channel_id=1, source_target_pairs={{0,8},{8,0},{1,9},{9,1},{2,10},{10,2},{3,11},{11,3},{4,12},{12,4},... | collective-permute-start | bytes 835592 | tf_op jit(solution)/shard_map/ppermute | solution.py:494
  58.3 3.9 %all-to-all-start.2 = ((bf16[16,56,512]{2,1,0:T(8,128)(2,1)}), bf16[16,56,512]{2,1,0:T(8,128)(2,1)S(1)}, u32[]{:S(2)}, u32[]{:S(2)}) async-start(bf16[16,56,512]{2,1,0:T(8,128)(2,1)} %bitcast.24), calls=%async_computation.2 | async-start | bytes 1835008 | tf_op jit(solution)/shard_map/all_to_all | solution.py:452
  62.3 9.3 %collective-permute-done.6.other_ref = bf16[272,512]{1,0:T(8,128)(2,1)S(1)} collective-permute-done((bf16[272,512]{1,0:T(8,128)(2,1)}, bf16[272,512]{1,0:T(8,128)(2,1)S(1)}, u32[]{:S(2)}, u32[]{:S(2)}) %collective-permute-start.6) | collective-permute-done | bytes 278560 | tf_op jit(solution)/shard_map/ppermute | solution.py:494
  71.5 1.8 %far_rows.1 = bf16[16,64,512]{2,1,0:T(8,128)(2,1)} custom-call(bf16[272,512]{1,0:T(8,128)(2,1)} %get-tuple-element.37.own_hbm, bf16[272,512]{1,0:T(8,128)(2,1)S(1)} %collective-permute-done.6.other_ref), custom_call_target="tpu_custom_call" | custom-call | flops 30000001024 | tf_op jit(solution)/shard_map/far_rows/pallas_call | solution.py:464
  73.3 6.8 %all-to-all-done.2.looked_ref = bf16[16,56,512]{2,1,0:T(8,128)(2,1)S(1)} async-done(((bf16[16,56,512]{2,1,0:T(8,128)(2,1)}), bf16[16,56,512]{2,1,0:T(8,128)(2,1)S(1)}, u32[]{:S(2)}, u32[]{:S(2)}) %all-to-all-start.2) | async-done | bytes 917536 | tf_op jit(solution)/shard_map/all_to_all | solution.py:452
  80.1 3.7 %all-to-all-start.3 = ((bf16[16,64,512]{2,1,0:T(8,128)(2,1)}), bf16[16,64,512]{2,1,0:T(8,128)(2,1)S(1)}, u32[]{:S(2)}, u32[]{:S(2)}) async-start(bf16[16,64,512]{2,1,0:T(8,128)(2,1)} %far_rows.1), calls=%async_computation.3 | async-start | bytes 2097152 | tf_op jit(solution)/shard_map/all_to_all | solution.py:452
  83.7 3.6 %pick_near.1 = (bf16[896,512]{1,0:T(8,128)(2,1)S(1)}, f32[7,128]{1,0:T(8,128)S(1)}, f32[4,128]{1,0:T(4,128)S(1)}, bf16[1280,128]{1,0:T(8,128)(2,1)}, bf16[8,128]{1,0:T(8,128)(2,1)S(1)}) custom-call(s32[6]{0:T(128)S(1)} %stack.27.scalar_ref, s32[7,128]{1,0:T(8,128)} %bitcast.27, s32[4,128]{1,0:T(4,128)} %bitcast.28, s32[10,128]{1,0:T(8,128)} %bitcast.26, ...), custom_call_target="tpu_custom_call" | custom-call | tf_op jit(solution)/shard_map/pick_near/pallas_call | solution.py:464
  87.3 11.4 %all-to-all-done.3.looked_ref = bf16[16,64,512]{2,1,0:T(8,128)(2,1)S(1)} async-done(((bf16[16,64,512]{2,1,0:T(8,128)(2,1)}), bf16[16,64,512]{2,1,0:T(8,128)(2,1)S(1)}, u32[]{:S(2)}, u32[]{:S(2)}) %all-to-all-start.3) | async-done | bytes 1048608 | tf_op jit(solution)/shard_map/all_to_all | solution.py:452
  98.7 5.1 %attend.1 = bf16[128,512]{1,0:T(8,128)(2,1)} custom-call(bf16[612,512]{1,0:T(8,128)(2,1)} %keyval_hbm.1, bf16[1280,128]{1,0:T(8,128)(2,1)} %get-tuple-element.32.enc_hbm, bf16[612,256]{1,0:T(8,128)(2,1)} %query_hbm.1, bf16[768,512]{1,0:T(8,128)(2,1)} %output_hbm.1, bf16[896,512]{1,0:T(8,128)(2,1)S(1)} %get-tuple-element.33.picked_ref, ...), custom_call_target="tpu_custom_call" | custom-call | tf_op jit(solution)/shard_map/attend/pallas_call | solution.py:464
Async XLA Ops:
  2.7 23.2 %all-to-all-start = ((bf16[32,16,512]{2,1,0:T(8,128)(2,1)}), bf16[32,16,512]{2,1,0:T(8,128)(2,1)S(1)}, u32[]{:S(2)}, u32[]{:S(2)}) async-start(bf16[32,16,512]{2,1,0:T(8,128)(2,1)} %bitcast.23), calls=%async_computation | async-start | bytes 1048576 | tf_op jit(solution)/shard_map/all_to_all | solution.py:452
  11.2 13.4 %collective-permute-start = (bf16[384,384]{1,0:T(8,128)(2,1)S(1)}, bf16[384,384]{1,0:T(8,128)(2,1)S(1)}, u32[]{:S(2)}, u32[]{:S(2)}) collective-permute-start(bf16[384,384]{1,0:T(8,128)(2,1)S(1)} %dynamic_slice.6), channel_id=1, source_target_pairs={{0,16},{16,0},{1,17},{17,1},{2,18},{18,2},{3,19},{19,3},{4,20},{20... | collective-permute-start | bytes 884744 | tf_op jit(solution)/shard_map/ppermute | solution.py:482
  15.1 30.2 %collective-permute-start.2 = (bf16[916,384]{1,0:T(8,128)(2,1)}, bf16[916,384]{1,0:T(8,128)(2,1)S(1)}, u32[]{:S(2)}, u32[]{:S(2)}) collective-permute-start(bf16[916,384]{1,0:T(8,128)(2,1)} %constant_dynamic-slice_fusion), channel_id=1, source_target_pairs={{0,16},{16,0},{1,17},{17,1},{2,18},{18,2},{3,19},{19,3},{4,20},{20... | collective-permute-start | bytes 2110472 | tf_op jit(solution)/shard_map/ppermute | solution.py:482
  27.3 22.3 %all-to-all-start.1 = ((bf16[32,16,640]{2,1,0:T(8,128)(2,1)}), bf16[32,16,640]{2,1,0:T(8,128)(2,1)S(1)}, u32[]{:S(2)}, u32[]{:S(2)}) async-start(bf16[32,16,640]{2,1,0:T(8,128)(2,1)} %bitcast.22), calls=%async_computation.1 | async-start | bytes 1310720 | tf_op jit(solution)/shard_map/all_to_all | solution.py:452
  30.8 15.1 %collective-permute-start.1 = (bf16[384,384]{1,0:T(8,128)(2,1)S(1)}, bf16[384,384]{1,0:T(8,128)(2,1)S(1)}, u32[]{:S(2)}, u32[]{:S(2)}) collective-permute-start(bf16[384,384]{1,0:T(8,128)(2,1)S(1)} %collective-permute-done.refs_0_), channel_id=1, source_target_pairs={{0,2},{1,3},{2,0},{3,1},{4,6},{5,7},{6,4},{7,5},{8,10},{9,11},{10,... | collective-permute-start | bytes 884744 | tf_op jit(solution)/shard_map/ppermute | solution.py:486
  45.9 3.0 %collective-permute-start.5 = (bf16[916,384]{1,0:T(8,128)(2,1)S(1)}, bf16[916,384]{1,0:T(8,128)(2,1)S(1)}, u32[]{:S(2)}, u32[]{:S(2)}) collective-permute-start(bf16[916,384]{1,0:T(8,128)(2,1)S(1)} %collective-permute-done.2.refs_2_), channel_id=1, source_target_pairs={{0,1},{1,0},{2,3},{3,2},{4,5},{5,4},{6,7},{7,6},{8,9},{9,8},{10,11... | collective-permute-start | bytes 2110472 | tf_op jit(solution)/shard_map/ppermute | solution.py:490
  45.9 2.6 %collective-permute-start.3 = (bf16[384,384]{1,0:T(8,128)(2,1)S(1)}, bf16[384,384]{1,0:T(8,128)(2,1)S(1)}, u32[]{:S(2)}, u32[]{:S(2)}) collective-permute-start(bf16[384,384]{1,0:T(8,128)(2,1)S(1)} %collective-permute-done.refs_0_), channel_id=1, source_target_pairs={{0,1},{1,0},{2,3},{3,2},{4,5},{5,4},{6,7},{7,6},{8,9},{9,8},{10,11... | collective-permute-start | bytes 884744 | tf_op jit(solution)/shard_map/ppermute | solution.py:490
  46.4 2.5 %collective-permute-start.4 = (bf16[384,384]{1,0:T(8,128)(2,1)S(1)}, bf16[384,384]{1,0:T(8,128)(2,1)S(1)}, u32[]{:S(2)}, u32[]{:S(2)}) collective-permute-start(bf16[384,384]{1,0:T(8,128)(2,1)S(1)} %collective-permute-done.1.refs_1_), channel_id=1, source_target_pairs={{0,1},{1,0},{2,3},{3,2},{4,5},{5,4},{6,7},{7,6},{8,9},{9,8},{10,11... | collective-permute-start | bytes 884744 | tf_op jit(solution)/shard_map/ppermute | solution.py:490
  55.6 16.0 %collective-permute-start.6 = (bf16[272,512]{1,0:T(8,128)(2,1)}, bf16[272,512]{1,0:T(8,128)(2,1)S(1)}, u32[]{:S(2)}, u32[]{:S(2)}) collective-permute-start(bf16[272,512]{1,0:T(8,128)(2,1)} %get-tuple-element.37.own_hbm), channel_id=1, source_target_pairs={{0,8},{8,0},{1,9},{9,1},{2,10},{10,2},{3,11},{11,3},{4,12},{12,4},... | collective-permute-start | bytes 835592 | tf_op jit(solution)/shard_map/ppermute | solution.py:494
  58.3 21.8 %all-to-all-start.2 = ((bf16[16,56,512]{2,1,0:T(8,128)(2,1)}), bf16[16,56,512]{2,1,0:T(8,128)(2,1)S(1)}, u32[]{:S(2)}, u32[]{:S(2)}) async-start(bf16[16,56,512]{2,1,0:T(8,128)(2,1)} %bitcast.24), calls=%async_computation.2 | async-start | bytes 1835008 | tf_op jit(solution)/shard_map/all_to_all | solution.py:452
  80.1 18.6 %all-to-all-start.3 = ((bf16[16,64,512]{2,1,0:T(8,128)(2,1)}), bf16[16,64,512]{2,1,0:T(8,128)(2,1)S(1)}, u32[]{:S(2)}, u32[]{:S(2)}) async-start(bf16[16,64,512]{2,1,0:T(8,128)(2,1)} %far_rows.1), calls=%async_computation.3 | async-start | bytes 2097152 | tf_op jit(solution)/shard_map/all_to_all | solution.py:452

commit v5 on v4

--- a/solution.py
+++ b/solution.py
@@ -159,7 +159,12 @@
     line = lax.broadcasted_iota(jnp.int32, extra.shape, 0)
     extra = jnp.where(line == rest, high, extra)
     extra = jnp.where(line == rest + 1, stamps - 8.0 * high, extra)
-    sent_ref[...] = dot_t((first + second).astype(BF), extra.astype(BF)).astype(BF)
+    sent = dot_t((first + second).astype(BF), extra.astype(BF))
+    if len(sent_ref.shape) == 3:
+        sent = sent.reshape(sent_ref.shape[0], -1, LANES)
+        lines = sent_ref.shape[1]
+        sent = sent[:, :lines, :] + half_turn(sent[:, lines:, :])
+    sent_ref[...] = sent.astype(BF)
 
 
 def of_half(half, column, rows_ref, ev_size, low_size, rest_size):
@@ -179,10 +184,35 @@
     return jnp.concatenate([columns(rows_ref[i : i + 1, :]) for i in range(begin, end)], axis=0)
 
 
+def half_turn(x):
+    return jnp.concatenate([x[..., LANES // 2 :], x[..., : LANES // 2]], axis=x.ndim - 1)
+
+
 def partner_kernel(swap_ref, sent_ref, fetched_ref, out_ref):
     width = fetched_ref.shape[1]
-    out_ref[:, :width] = dot(swap_ref[...], fetched_ref[...]).astype(BF)
-    out_ref[:, width:] = sent_ref[...]
+    rows = dot(swap_ref[...], fetched_ref[...])
+    if len(out_ref.shape) == 3:
+        to_chunks(rows, out_ref)
+        out_ref[:, out_ref.shape[1] - sent_ref.shape[1] :, :] = sent_ref[...]
+    else:
+        out_ref[:, :width] = rows.astype(BF)
+        out_ref[:, width:] = sent_ref[...]
+
+
+def to_chunks(rows, out_ref):
+    blocks = out_ref.shape[0]
+    lines = rows.shape[0] // blocks
+    for c in range(rows.shape[1] // LANES):
+        chunk = rows[:, c * LANES : (c + 1) * LANES].reshape(blocks, lines, LANES)
+        out_ref[:, c * lines : (c + 1) * lines, :] = chunk.astype(BF)
+
+
+def from_chunks(ref, lines, count):
+    blocks = ref.shape[0]
+    chunks = [
+        ref[:, c * lines : (c + 1) * lines, :].reshape(blocks * lines, LANES) for c in range(count)
+    ]
+    return jnp.concatenate(chunks, axis=1)
 
 
 def update_kernel(
@@ -209,16 +239,24 @@
     pairs += [(own_weight_hbm, own_weight)] if shared else []
     copies = fetch(pairs, sems)
     nodes, width = memory_ref.shape
-    slots = message_ref.shape[0]
+    slots = serve.shape[1]
     lane = lax.broadcasted_iota(jnp.int32, (slots, LANES), 1)
     rest = enc_width + edge_width - LANES
-    extra = message_ref[:, width:].astype(F32)
+    if len(message_ref.shape) == 3:
+        lines = slots // message_ref.shape[0]
+        chunks = width // LANES
+        partner = from_chunks(message_ref, lines, chunks)
+        extra = message_ref[:, chunks * lines :, :].astype(F32)
+        extra = jnp.concatenate([extra, half_turn(extra)], axis=1).reshape(slots, LANES)
+    else:
+        partner = message_ref[:, :width]
+        extra = message_ref[:, width:].astype(F32)
     stamp = extra[:, rest : rest + 1] * 8.0 + extra[:, rest + 1 : rest + 2]
     gap = stamp - tau_ref[:slots, :]
     enc = cosine(gap * tau_ref[slots : slots + 1, :] + tau_ref[slots + 8 : slots + 9, :])
     mixed = jnp.where(lane < enc_width, enc, extra).astype(BF)
     tail = jnp.where(lane < rest, extra, 0.0).astype(BF)
-    messages = jnp.concatenate([message_ref[:, :width], mixed, tail], axis=1)
+    messages = jnp.concatenate([partner, mixed, tail], axis=1)
     copies[0].wait()
     match = one_hot_rows(serve[...].astype(F32), nodes)
     counts = jnp.sum(match, axis=1, keepdims=True)
@@ -304,20 +342,20 @@
 
 
 def far_kernel(own_hbm, other_ref, out_ref, hub, sems):
-    nodes = other_ref.shape[0] - 16
+    nodes, width = other_ref.shape[0] - 16, other_ref.shape[1]
     copies = fetch([(own_hbm.at[nodes:, :], hub)], sems)
-    count = out_ref.shape[0] * (out_ref.shape[1] - 8) // LANES
+    chunks = width // LANES
+    near, lines, _ = out_ref.shape
     wanted = other_ref[nodes:, :].astype(F32)[8:, :]
+    count = near * (lines - 8) // chunks // LANES
     index = [wanted[i % 8 : i % 8 + 1, i // 8 * LANES : (i // 8 + 1) * LANES] for i in range(count)]
     picks = one_hot(jnp.concatenate([columns(row) for row in index], axis=0), nodes)
-    rows = dot(picks, other_ref[:nodes, :])
-    near, block, width = out_ref.shape
-    out_ref[:, : block - 8, :] = rows.reshape(near, block - 8, width).astype(BF)
+    to_chunks(dot(picks, other_ref[:nodes, :]), out_ref)
     copies[0].wait()
-    hubs = jnp.concatenate(
-        [other_ref[nodes : nodes + 1, :], hub[0:1, :], jnp.zeros((6, width), BF)], axis=0
-    )
-    out_ref[:, block - 8 :, :] = jnp.broadcast_to(hubs[None], (near, 8, width))
+    hubs = [other_ref[nodes : nodes + 1, :], hub[0:1, :]]
+    parts = [h[:, c * LANES : (c + 1) * LANES].astype(F32) for h in hubs for c in range(chunks)]
+    parts = jnp.concatenate(parts, axis=0).astype(BF)
+    out_ref[:, lines - 8 :, :] = jnp.broadcast_to(parts[None], (near, 8, LANES))
 
 
 def places(slot, hi, cap, low_size, rest_size):
@@ -372,9 +410,9 @@
     events = gaps.shape[1]
     picks = [one_hot(columns(index[k : k + 1, :]), owners * block) for k in range(slot.shape[0])]
     picked_ref[...] = dot(jnp.concatenate(picks, axis=0), looked).astype(BF)
-    far_ref[...] = jnp.where(near, -1.0, relay * (block + 8) + place)
+    far_ref[...] = jnp.where(near, -1.0, relay * block + place)
     relay, near, place = places(hub[...].astype(F32), hi, 1, *sizes)
-    hub_ref[...] = relay * 8.0 + jnp.where(near, 1.0, 0.0)
+    hub_ref[...] = relay * 8.0 + jnp.where(near, 4.0, 0.0)
     freq_row, phase_row = lanes(freq[...]), lanes(phase[...])
     for k in range(gaps.shape[0]):
         angle = columns(gaps[k : k + 1, :].astype(F32)) * freq_row + phase_row
@@ -408,13 +446,19 @@
         ],
         sems,
     )
-    owners, block, width = looked_ref.shape
-    events = out_ref.shape[0]
+    events, width = out_ref.shape
+    chunks = width // LANES
+    owners = looked_ref.shape[0]
+    block = (looked_ref.shape[1] - 8) // chunks
     near = enc_ref.shape[0] // events
     att = query_ref.shape[1]
     head = att // HEADS
-    looked = looked_ref[...].reshape(owners * block, width)
-    hub_rows = looked_ref[:, block - 8 :, :].reshape(owners * 8, width)
+    looked = from_chunks(looked_ref, block, chunks)
+    hub_lines = looked_ref[:, chunks * block :, :].astype(F32).reshape(owners * 8, LANES)
+    hub_rows = [hub_lines] + [
+        jnp.concatenate([hub_lines[c:], hub_lines[:c]], axis=0) for c in range(1, chunks)
+    ]
+    hub_rows = jnp.concatenate(hub_rows, axis=1).astype(BF)
     hub_near = dot(picks_of(hub_ref[...], owners * 8), hub_rows).astype(BF)
     picks = picks_of(far_ref[...], owners * block)
     rows = (dot(picks, looked) + picked_ref[...].astype(F32)).astype(BF)
@@ -574,13 +618,18 @@
         phase,
     )
     rows_shape = pltpu.VMEM((near * block // LANES, LANES), F32)
+    packed = cap % 16 == 0
+    sent_lines = (devices, cap // 2, LANES) if packed else (slots, LANES)
+    message_shape = (slots, width + LANES)
+    if packed:
+        message_shape = (devices, cap * width // LANES + cap // 2, LANES)
     tau, swap, sent, near_index, away_index = call(
         functools.partial(prepare_kernel, enc_width, sizes),
         "prepare",
         (
             pltpu.VMEM((slots + 16, LANES), F32),
             pltpu.VMEM((slots, slots), BF),
-            pltpu.VMEM((slots, LANES), BF),
+            pltpu.VMEM(sent_lines, BF),
             rows_shape,
             rows_shape,
         ),
@@ -595,7 +644,7 @@
     message = call(
         partner_kernel,
         "partner_rows",
-        sent_shape((slots, width + LANES), BF),
+        sent_shape(message_shape, BF),
         (),
         (),
         (fetched,),
@@ -610,7 +659,7 @@
         pieces += [other_core(x) for x in pieces]
     else:
         pieces = [whole]
-    message = exchange(message.reshape(devices, cap, width + LANES), BOTH)
+    message = exchange(message.reshape(devices, -1, message_shape[-1]), BOTH)
     raw = (update_serve, memory, gru_bias, gru_weight)
     parts = pltpu.VMEM((3 * width // piece, nodes, piece), F32)
     new_memory, extended, near_rows = call(
@@ -623,7 +672,7 @@
         ),
         (scalars, hub_node),
         raw,
-        (message.reshape(slots, width + LANES), *pieces),
+        (message.reshape(message_shape), *pieces),
         kept=(tau, near_index, away_index),
         fetched=raw,
         scratch=(
@@ -640,7 +689,7 @@
     far_rows = call(
         far_kernel,
         "far_rows",
-        sent_shape((near, block + 8, width), BF),
+        sent_shape((near, block * width // LANES + 8, LANES), BF),
         (),
         (extended,),
         (other_extended,),

time: 105 us -> 103 us (0.981)
  waiting for transfers between devices: 51.5 us -> 49 us
    all_to_all x4, waiting for transfers between devices: 20.1 us -> 18.2 us  [exchange(): return lax.all_to_all(x, axes, split_axis=0, concat_axis=0, tiled=True)]
  transfers between devices with their start and end apart: 11 -> 11, of which waited for: 10 -> 9; matrix products, arithmetic and copies ran while one was open for 3% -> 3% of each run, Pallas kernels for 8% -> 9%
where the time goes in v5:
time: 103 us; the launch traced here: 102 us
  waiting for transfers between devices  49 us (48%)
  starting transfers between devices  26.2 us (25%)
  Pallas kernels  22 us (21%)
  local copies, waits for them, and re-layouts  3.26 us (3%)
  between operations  1.42 us (1%)
    pallas_call x7, Pallas kernels, call(): pl.pallas_call(kernel, out_shape=out_shape, in_specs=[SMEM] * len(smem) +...  22 us
    ppermute x2, waiting for transfers between devices, other_ev(): return lax.ppermute(x, 'ev', [(0, 1), (1, 0)])  19.2 us
    all_to_all x4, starting transfers between devices, exchange(): return lax.all_to_all(x, axes, split_axis=0, concat_axis=0, tiled=True)  18.4 us
    all_to_all x4, waiting for transfers between devices, exchange(): return lax.all_to_all(x, axes, split_axis=0, concat_axis=0, tiled=True)  18.2 us
    ppermute x1, waiting for transfers between devices, other_half(): return lax.ppermute(x, 'hi', [(0, 1), (1, 0)])  9.34 us
    ppermute x1, starting transfers between devices, other_half(): return lax.ppermute(x, 'hi', [(0, 1), (1, 0)])  3.33 us
    ppermute x2, starting transfers between devices, other_ev(): return lax.ppermute(x, 'ev', [(0, 1), (1, 0)])  2.09 us
  transfers between devices with their start and end apart: 11, of which 9 were waited for; matrix products, arithmetic and copies ran while one was open for 3% of the time, Pallas kernels for 9%

profile of v5, /device:TPU:0, one launch (start us, length us, event | category | flops | bytes accessed | tf_op | source)
XLA Modules:
  0.0 101.9 jit_solution(12611880947422986421)
XLA Ops:
  0.6 2.1 %serve_endpoints.1 = bf16[512,512]{1,0:T(8,128)(2,1)} custom-call(s32[1,512]{1,0:T(1,128)} %serve_hbm.4, bf16[256,512]{1,0:T(8,128)(2,1)} %memory_hbm.3), custom_call_target="tpu_custom_call" | custom-call | tf_op jit(solution)/shard_map/serve_endpoints/pallas_call | solution.py:508
  2.7 7.3 %all-to-all-start = ((bf16[32,16,512]{2,1,0:T(8,128)(2,1)}), bf16[32,16,512]{2,1,0:T(8,128)(2,1)S(1)}, u32[]{:S(2)}, u32[]{:S(2)}) async-start(bf16[32,16,512]{2,1,0:T(8,128)(2,1)} %bitcast.19), calls=%async_computation | async-start | bytes 1048576 | tf_op jit(solution)/shard_map/all_to_all | solution.py:496
  10.1 1.1 %dynamic_slice.6 = bf16[384,384]{1,0:T(8,128)(2,1)S(1)} dynamic-slice(bf16[1684,768]{1,0:T(8,128)(2,1)} %own_weight_hbm.1, s32[]{:T(128)S(6)} %select_n.30, s32[]{:T(128)S(6)} %select_n.31), dynamic_slice_sizes={384,384} | dynamic-slice | bytes 589828 | tf_op jit(solution)/shard_map/dynamic_slice | solution.py:592
  11.2 1.8 %collective-permute-start = (bf16[384,384]{1,0:T(8,128)(2,1)S(1)}, bf16[384,384]{1,0:T(8,128)(2,1)S(1)}, u32[]{:S(2)}, u32[]{:S(2)}) collective-permute-start(bf16[384,384]{1,0:T(8,128)(2,1)S(1)} %dynamic_slice.6), channel_id=1, source_target_pairs={{0,16},{16,0},{1,17},{17,1},{2,18},{18,2},{3,19},{19,3},{4,20},{20... | collective-permute-start | bytes 884744 | tf_op jit(solution)/shard_map/ppermute | solution.py:526
  13.1 2.0 %constant_dynamic-slice_fusion = bf16[916,384]{1,0:T(8,128)(2,1)} fusion(bf16[1684,768]{1,0:T(8,128)(2,1)} %own_weight_hbm.1, s32[]{:T(128)S(6)} %select_n.31), kind=kLoop, calls=%fused_computation | loop fusion | bytes 1406980 | tf_op jit(solution)/shard_map/dynamic_slice | solution.py:655
  15.1 0.3 collective-permute-start.2
  15.4 0.1 stack.27.scalar_ref
  15.5 2.2 %prepare.1 = (f32[528,128]{1,0:T(8,128)S(1)}, bf16[512,512]{1,0:T(8,128)(2,1)S(1)}, bf16[32,8,128]{2,1,0:T(8,128)(2,1)S(1)}, f32[7,128]{1,0:T(8,128)S(1)}, f32[7,128]{1,0:T(8,128)S(1)}) custom-call(s32[6]{0:T(128)S(1)} %stack.27.scalar_ref, s32[1,512]{1,0:T(1,128)} %serve_hbm.4, s32[1,256]{1,0:T(1,128)} %bitcast.29, s32[1,128]{1,0:T(1,128)} %bitcast.31, ...), custom_call_target="tpu_custom_call" | custom-call | tf_op jit(solution)/shard_map/prepare/pallas_call | solution.py:508
  17.7 6.9 %collective-permute-done.refs_0_ = bf16[384,384]{1,0:T(8,128)(2,1)S(1)} collective-permute-done((bf16[384,384]{1,0:T(8,128)(2,1)S(1)}, bf16[384,384]{1,0:T(8,128)(2,1)S(1)}, u32[]{:S(2)}, u32[]{:S(2)}) %collective-permute-start) | collective-permute-done | bytes 294944 | tf_op jit(solution)/shard_map/ppermute | solution.py:526
  24.6 1.4 %all-to-all-done = bf16[32,16,512]{2,1,0:T(8,128)(2,1)S(1)} async-done(((bf16[32,16,512]{2,1,0:T(8,128)(2,1)}), bf16[32,16,512]{2,1,0:T(8,128)(2,1)S(1)}, u32[]{:S(2)}, u32[]{:S(2)}) %all-to-all-start) | async-done | bytes 524320 | tf_op jit(solution)/shard_map/all_to_all | solution.py:496
  26.0 1.3 %partner_rows.1 = bf16[32,72,128]{2,1,0:T(8,128)(2,1)} custom-call(bf16[512,512]{1,0:T(8,128)(2,1)S(1)} %get-tuple-element.24.swap_ref, bf16[32,8,128]{2,1,0:T(8,128)(2,1)S(1)} %get-tuple-element.27.sent_ref, bf16[512,512]{1,0:T(8,128)(2,1)S(1)} %bitcast.18), custom_call_target="tpu_custom_call" | custom-call | tf_op jit(solution)/shard_map/partner_rows/pallas_call | solution.py:508
  27.3 3.5 %all-to-all-start.1 = ((bf16[32,72,128]{2,1,0:T(8,128)(2,1)}), bf16[32,72,128]{2,1,0:T(8,128)(2,1)S(1)}, u32[]{:S(2)}, u32[]{:S(2)}) async-start(bf16[32,72,128]{2,1,0:T(8,128)(2,1)} %partner_rows.1), calls=%async_computation.1 | async-start | bytes 1179648 | tf_op jit(solution)/shard_map/all_to_all | solution.py:496
  30.8 1.8 %collective-permute-start.1 = (bf16[384,384]{1,0:T(8,128)(2,1)S(1)}, bf16[384,384]{1,0:T(8,128)(2,1)S(1)}, u32[]{:S(2)}, u32[]{:S(2)}) collective-permute-start(bf16[384,384]{1,0:T(8,128)(2,1)S(1)} %collective-permute-done.refs_0_), channel_id=1, source_target_pairs={{0,2},{1,3},{2,0},{3,1},{4,6},{5,7},{6,4},{7,5},{8,10},{9,11},{10,... | collective-permute-start | bytes 884744 | tf_op jit(solution)/shard_map/ppermute | solution.py:530
  32.6 12.3 %collective-permute-done.2.refs_2_ = bf16[916,384]{1,0:T(8,128)(2,1)S(1)} collective-permute-done((bf16[916,384]{1,0:T(8,128)(2,1)}, bf16[916,384]{1,0:T(8,128)(2,1)S(1)}, u32[]{:S(2)}, u32[]{:S(2)}) %collective-permute-start.2) | collective-permute-done | bytes 703520 | tf_op jit(solution)/shard_map/ppermute | solution.py:526
  44.9 0.5 collective-permute-done.1.refs_1_
  45.3 0.0 collective-permute-start.5
  45.3 0.5 collective-permute-start.3
  45.9 0.0 collective-permute-start.4
  46.5 1.4 %collective-permute-done.3.refs_3_ = bf16[384,384]{1,0:T(8,128)(2,1)S(1)} collective-permute-done((bf16[384,384]{1,0:T(8,128)(2,1)S(1)}, bf16[384,384]{1,0:T(8,128)(2,1)S(1)}, u32[]{:S(2)}, u32[]{:S(2)}) %collective-permute-start.3) | collective-permute-done | bytes 294944 | tf_op jit(solution)/shard_map/ppermute | solution.py:534
  47.9 0.4 collective-permute-done.4.refs_4_
  48.4 0.0 collective-permute-done.5.refs_5_
  48.4 0.0 all-to-all-done.1.message_ref
  48.4 6.0 %update_memory.1 = (bf16[256,512]{1,0:T(8,128)(2,1)}, bf16[272,512]{1,0:T(8,128)(2,1)}, bf16[896,512]{1,0:T(8,128)(2,1)}) custom-call(s32[6]{0:T(128)S(1)} %stack.27.scalar_ref, s32[1]{0:T(128)S(6)} %copy.20.hub_ref, s32[1,512]{1,0:T(1,128)} %serve_hbm.4, bf16[256,512]{1,0:T(8,128)(2,1)} %memory_hbm.3, f32[2,1536]{1,0:T(2,128)} %bias_hbm.1, ...), custom_call_target="tpu_custom_call" | custom-call | tf_op jit(solution)/shard_map/update_memory/pallas_call | solution.py:508
  54.4 3.3 %collective-permute-start.6 = (bf16[272,512]{1,0:T(8,128)(2,1)}, bf16[272,512]{1,0:T(8,128)(2,1)S(1)}, u32[]{:S(2)}, u32[]{:S(2)}) collective-permute-start(bf16[272,512]{1,0:T(8,128)(2,1)} %get-tuple-element.37.own_hbm), channel_id=1, source_target_pairs={{0,8},{8,0},{1,9},{9,1},{2,10},{10,2},{3,11},{11,3},{4,12},{12,4},... | collective-permute-start | bytes 835592 | tf_op jit(solution)/shard_map/ppermute | solution.py:538
  57.8 3.9 %all-to-all-start.2 = ((bf16[16,56,512]{2,1,0:T(8,128)(2,1)}), bf16[16,56,512]{2,1,0:T(8,128)(2,1)S(1)}, u32[]{:S(2)}, u32[]{:S(2)}) async-start(bf16[16,56,512]{2,1,0:T(8,128)(2,1)} %bitcast.20), calls=%async_computation.2 | async-start | bytes 1835008 | tf_op jit(solution)/shard_map/all_to_all | solution.py:496
  61.6 9.3 %collective-permute-done.6.other_ref = bf16[272,512]{1,0:T(8,128)(2,1)S(1)} collective-permute-done((bf16[272,512]{1,0:T(8,128)(2,1)}, bf16[272,512]{1,0:T(8,128)(2,1)S(1)}, u32[]{:S(2)}, u32[]{:S(2)}) %collective-permute-start.6) | collective-permute-done | bytes 278560 | tf_op jit(solution)/shard_map/ppermute | solution.py:538
  71.0 1.7 %far_rows.1 = bf16[16,232,128]{2,1,0:T(8,128)(2,1)} custom-call(bf16[272,512]{1,0:T(8,128)(2,1)} %get-tuple-element.37.own_hbm, bf16[272,512]{1,0:T(8,128)(2,1)S(1)} %collective-permute-done.6.other_ref), custom_call_target="tpu_custom_call" | custom-call | flops 30000001024 | tf_op jit(solution)/shard_map/far_rows/pallas_call | solution.py:508
  72.7 6.8 %all-to-all-done.2.looked_ref = bf16[16,56,512]{2,1,0:T(8,128)(2,1)S(1)} async-done(((bf16[16,56,512]{2,1,0:T(8,128)(2,1)}), bf16[16,56,512]{2,1,0:T(8,128)(2,1)S(1)}, u32[]{:S(2)}, u32[]{:S(2)}) %all-to-all-start.2) | async-done | bytes 917536 | tf_op jit(solution)/shard_map/all_to_all | solution.py:496
  79.5 3.7 %all-to-all-start.3 = ((bf16[16,232,128]{2,1,0:T(8,128)(2,1)}), bf16[16,232,128]{2,1,0:T(8,128)(2,1)S(1)}, u32[]{:S(2)}, u32[]{:S(2)}) async-start(bf16[16,232,128]{2,1,0:T(8,128)(2,1)} %far_rows.1), calls=%async_computation.3 | async-start | bytes 1900544 | tf_op jit(solution)/shard_map/all_to_all | solution.py:496
  83.2 3.6 %pick_near.1 = (bf16[896,512]{1,0:T(8,128)(2,1)S(1)}, f32[7,128]{1,0:T(8,128)S(1)}, f32[4,128]{1,0:T(4,128)S(1)}, bf16[1280,128]{1,0:T(8,128)(2,1)}, bf16[8,128]{1,0:T(8,128)(2,1)S(1)}) custom-call(s32[6]{0:T(128)S(1)} %stack.27.scalar_ref, s32[7,128]{1,0:T(8,128)} %bitcast.23, s32[4,128]{1,0:T(4,128)} %bitcast.24, s32[10,128]{1,0:T(8,128)} %bitcast.22, ...), custom_call_target="tpu_custom_call" | custom-call | tf_op jit(solution)/shard_map/pick_near/pallas_call | solution.py:508
  86.8 10.0 %all-to-all-done.3.looked_ref = bf16[16,232,128]{2,1,0:T(8,128)(2,1)S(1)} async-done(((bf16[16,232,128]{2,1,0:T(8,128)(2,1)}), bf16[16,232,128]{2,1,0:T(8,128)(2,1)S(1)}, u32[]{:S(2)}, u32[]{:S(2)}) %all-to-all-start.3) | async-done | bytes 950304 | tf_op jit(solution)/shard_map/all_to_all | solution.py:496
  96.8 5.1 %attend.1 = bf16[128,512]{1,0:T(8,128)(2,1)} custom-call(bf16[612,512]{1,0:T(8,128)(2,1)} %keyval_hbm.1, bf16[1280,128]{1,0:T(8,128)(2,1)} %get-tuple-element.32.enc_hbm, bf16[612,256]{1,0:T(8,128)(2,1)} %query_hbm.1, bf16[768,512]{1,0:T(8,128)(2,1)} %output_hbm.1, bf16[896,512]{1,0:T(8,128)(2,1)S(1)} %get-tuple-element.33.picked_ref, ...), custom_call_target="tpu_custom_call" | custom-call | tf_op jit(solution)/shard_map/attend/pallas_call | solution.py:508
Async XLA Ops:
  2.7 23.2 %all-to-all-start = ((bf16[32,16,512]{2,1,0:T(8,128)(2,1)}), bf16[32,16,512]{2,1,0:T(8,128)(2,1)S(1)}, u32[]{:S(2)}, u32[]{:S(2)}) async-start(bf16[32,16,512]{2,1,0:T(8,128)(2,1)} %bitcast.19), calls=%async_computation | async-start | bytes 1048576 | tf_op jit(solution)/shard_map/all_to_all | solution.py:496
  11.2 13.4 %collective-permute-start = (bf16[384,384]{1,0:T(8,128)(2,1)S(1)}, bf16[384,384]{1,0:T(8,128)(2,1)S(1)}, u32[]{:S(2)}, u32[]{:S(2)}) collective-permute-start(bf16[384,384]{1,0:T(8,128)(2,1)S(1)} %dynamic_slice.6), channel_id=1, source_target_pairs={{0,16},{16,0},{1,17},{17,1},{2,18},{18,2},{3,19},{19,3},{4,20},{20... | collective-permute-start | bytes 884744 | tf_op jit(solution)/shard_map/ppermute | solution.py:526
  15.1 29.8 %collective-permute-start.2 = (bf16[916,384]{1,0:T(8,128)(2,1)}, bf16[916,384]{1,0:T(8,128)(2,1)S(1)}, u32[]{:S(2)}, u32[]{:S(2)}) collective-permute-start(bf16[916,384]{1,0:T(8,128)(2,1)} %constant_dynamic-slice_fusion), channel_id=1, source_target_pairs={{0,16},{16,0},{1,17},{17,1},{2,18},{18,2},{3,19},{19,3},{4,20},{20... | collective-permute-start | bytes 2110472 | tf_op jit(solution)/shard_map/ppermute | solution.py:526
  27.3 21.1 %all-to-all-start.1 = ((bf16[32,72,128]{2,1,0:T(8,128)(2,1)}), bf16[32,72,128]{2,1,0:T(8,128)(2,1)S(1)}, u32[]{:S(2)}, u32[]{:S(2)}) async-start(bf16[32,72,128]{2,1,0:T(8,128)(2,1)} %partner_rows.1), calls=%async_computation.1 | async-start | bytes 1179648 | tf_op jit(solution)/shard_map/all_to_all | solution.py:496
  30.8 14.6 %collective-permute-start.1 = (bf16[384,384]{1,0:T(8,128)(2,1)S(1)}, bf16[384,384]{1,0:T(8,128)(2,1)S(1)}, u32[]{:S(2)}, u32[]{:S(2)}) collective-permute-start(bf16[384,384]{1,0:T(8,128)(2,1)S(1)} %collective-permute-done.refs_0_), channel_id=1, source_target_pairs={{0,2},{1,3},{2,0},{3,1},{4,6},{5,7},{6,4},{7,5},{8,10},{9,11},{10,... | collective-permute-start | bytes 884744 | tf_op jit(solution)/shard_map/ppermute | solution.py:530
  45.3 3.0 %collective-permute-start.5 = (bf16[916,384]{1,0:T(8,128)(2,1)S(1)}, bf16[916,384]{1,0:T(8,128)(2,1)S(1)}, u32[]{:S(2)}, u32[]{:S(2)}) collective-permute-start(bf16[916,384]{1,0:T(8,128)(2,1)S(1)} %collective-permute-done.2.refs_2_), channel_id=1, source_target_pairs={{0,1},{1,0},{2,3},{3,2},{4,5},{5,4},{6,7},{7,6},{8,9},{9,8},{10,11... | collective-permute-start | bytes 2110472 | tf_op jit(solution)/shard_map/ppermute | solution.py:534
  45.3 2.6 %collective-permute-start.3 = (bf16[384,384]{1,0:T(8,128)(2,1)S(1)}, bf16[384,384]{1,0:T(8,128)(2,1)S(1)}, u32[]{:S(2)}, u32[]{:S(2)}) collective-permute-start(bf16[384,384]{1,0:T(8,128)(2,1)S(1)} %collective-permute-done.refs_0_), channel_id=1, source_target_pairs={{0,1},{1,0},{2,3},{3,2},{4,5},{5,4},{6,7},{7,6},{8,9},{9,8},{10,11... | collective-permute-start | bytes 884744 | tf_op jit(solution)/shard_map/ppermute | solution.py:534
  45.9 2.5 %collective-permute-start.4 = (bf16[384,384]{1,0:T(8,128)(2,1)S(1)}, bf16[384,384]{1,0:T(8,128)(2,1)S(1)}, u32[]{:S(2)}, u32[]{:S(2)}) collective-permute-start(bf16[384,384]{1,0:T(8,128)(2,1)S(1)} %collective-permute-done.1.refs_1_), channel_id=1, source_target_pairs={{0,1},{1,0},{2,3},{3,2},{4,5},{5,4},{6,7},{7,6},{8,9},{9,8},{10,11... | collective-permute-start | bytes 884744 | tf_op jit(solution)/shard_map/ppermute | solution.py:534
  54.4 16.6 %collective-permute-start.6 = (bf16[272,512]{1,0:T(8,128)(2,1)}, bf16[272,512]{1,0:T(8,128)(2,1)S(1)}, u32[]{:S(2)}, u32[]{:S(2)}) collective-permute-start(bf16[272,512]{1,0:T(8,128)(2,1)} %get-tuple-element.37.own_hbm), channel_id=1, source_target_pairs={{0,8},{8,0},{1,9},{9,1},{2,10},{10,2},{3,11},{11,3},{4,12},{12,4},... | collective-permute-start | bytes 835592 | tf_op jit(solution)/shard_map/ppermute | solution.py:538
  57.8 21.7 %all-to-all-start.2 = ((bf16[16,56,512]{2,1,0:T(8,128)(2,1)}), bf16[16,56,512]{2,1,0:T(8,128)(2,1)S(1)}, u32[]{:S(2)}, u32[]{:S(2)}) async-start(bf16[16,56,512]{2,1,0:T(8,128)(2,1)} %bitcast.20), calls=%async_computation.2 | async-start | bytes 1835008 | tf_op jit(solution)/shard_map/all_to_all | solution.py:496
  79.5 17.3 %all-to-all-start.3 = ((bf16[16,232,128]{2,1,0:T(8,128)(2,1)}), bf16[16,232,128]{2,1,0:T(8,128)(2,1)S(1)}, u32[]{:S(2)}, u32[]{:S(2)}) async-start(bf16[16,232,128]{2,1,0:T(8,128)(2,1)} %far_rows.1), calls=%async_computation.3 | async-start | bytes 1900544 | tf_op jit(solution)/shard_map/all_to_all | solution.py:496

commit v6 on v5

--- a/solution.py
+++ b/solution.py
@@ -461,7 +461,7 @@
     hub_rows = jnp.concatenate(hub_rows, axis=1).astype(BF)
     hub_near = dot(picks_of(hub_ref[...], owners * 8), hub_rows).astype(BF)
     picks = picks_of(far_ref[...], owners * block)
-    rows = (dot(picks, looked) + picked_ref[...].astype(F32)).astype(BF)
+    rows = dot(picks, looked).astype(BF) + picked_ref[...]
     own = rows[:events]
     near_rows = jnp.concatenate([rows[events:], hub_near], axis=0)
     copies[0].wait()

time: 103 us -> 102 us (level)
  no operation moved by 1% of the time
where the time goes in v6:
time: 102 us; the launch traced here: 101 us
  waiting for transfers between devices  49 us (48%)
  starting transfers between devices  26.2 us (26%)
  Pallas kernels  21.3 us (21%)
  local copies, waits for them, and re-layouts  3.26 us (3%)
  between operations  1.42 us (1%)
    pallas_call x7, Pallas kernels, call(): pl.pallas_call(kernel, out_shape=out_shape, in_specs=[SMEM] * len(smem) +...  21.3 us
    ppermute x2, waiting for transfers between devices, other_ev(): return lax.ppermute(x, 'ev', [(0, 1), (1, 0)])  19.2 us
    all_to_all x4, starting transfers between devices, exchange(): return lax.all_to_all(x, axes, split_axis=0, concat_axis=0, tiled=True)  18.4 us
    all_to_all x4, waiting for transfers between devices, exchange(): return lax.all_to_all(x, axes, split_axis=0, concat_axis=0, tiled=True)  18.2 us
    ppermute x1, waiting for transfers between devices, other_half(): return lax.ppermute(x, 'hi', [(0, 1), (1, 0)])  9.34 us
    ppermute x1, starting transfers between devices, other_half(): return lax.ppermute(x, 'hi', [(0, 1), (1, 0)])  3.33 us
    ppermute x2, starting transfers between devices, other_ev(): return lax.ppermute(x, 'ev', [(0, 1), (1, 0)])  2.09 us
  transfers between devices with their start and end apart: 11, of which 9 were waited for; matrix products, arithmetic and copies ran while one was open for 3% of the time, Pallas kernels for 9%

profile of v6, /device:TPU:0, one launch (start us, length us, event | category | flops | bytes accessed | tf_op | source)
XLA Modules:
  0.0 101.2 jit_solution(12813922908837353456)
XLA Ops:
  0.6 2.1 %serve_endpoints.1 = bf16[512,512]{1,0:T(8,128)(2,1)} custom-call(s32[1,512]{1,0:T(1,128)} %serve_hbm.4, bf16[256,512]{1,0:T(8,128)(2,1)} %memory_hbm.3), custom_call_target="tpu_custom_call" | custom-call | tf_op jit(solution)/shard_map/serve_endpoints/pallas_call | solution.py:508
  2.7 7.3 %all-to-all-start = ((bf16[32,16,512]{2,1,0:T(8,128)(2,1)}), bf16[32,16,512]{2,1,0:T(8,128)(2,1)S(1)}, u32[]{:S(2)}, u32[]{:S(2)}) async-start(bf16[32,16,512]{2,1,0:T(8,128)(2,1)} %bitcast.19), calls=%async_computation | async-start | bytes 1048576 | tf_op jit(solution)/shard_map/all_to_all | solution.py:496
  10.1 1.1 %dynamic_slice.6 = bf16[384,384]{1,0:T(8,128)(2,1)S(1)} dynamic-slice(bf16[1684,768]{1,0:T(8,128)(2,1)} %own_weight_hbm.1, s32[]{:T(128)S(6)} %select_n.30, s32[]{:T(128)S(6)} %select_n.31), dynamic_slice_sizes={384,384} | dynamic-slice | bytes 589828 | tf_op jit(solution)/shard_map/dynamic_slice | solution.py:592
  11.2 1.8 %collective-permute-start = (bf16[384,384]{1,0:T(8,128)(2,1)S(1)}, bf16[384,384]{1,0:T(8,128)(2,1)S(1)}, u32[]{:S(2)}, u32[]{:S(2)}) collective-permute-start(bf16[384,384]{1,0:T(8,128)(2,1)S(1)} %dynamic_slice.6), channel_id=1, source_target_pairs={{0,16},{16,0},{1,17},{17,1},{2,18},{18,2},{3,19},{19,3},{4,20},{20... | collective-permute-start | bytes 884744 | tf_op jit(solution)/shard_map/ppermute | solution.py:526
  13.1 2.0 %constant_dynamic-slice_fusion = bf16[916,384]{1,0:T(8,128)(2,1)} fusion(bf16[1684,768]{1,0:T(8,128)(2,1)} %own_weight_hbm.1, s32[]{:T(128)S(6)} %select_n.31), kind=kLoop, calls=%fused_computation | loop fusion | bytes 1406980 | tf_op jit(solution)/shard_map/dynamic_slice | solution.py:655
  15.1 0.3 collective-permute-start.2
  15.4 0.1 stack.27.scalar_ref
  15.5 2.2 %prepare.1 = (f32[528,128]{1,0:T(8,128)S(1)}, bf16[512,512]{1,0:T(8,128)(2,1)S(1)}, bf16[32,8,128]{2,1,0:T(8,128)(2,1)S(1)}, f32[7,128]{1,0:T(8,128)S(1)}, f32[7,128]{1,0:T(8,128)S(1)}) custom-call(s32[6]{0:T(128)S(1)} %stack.27.scalar_ref, s32[1,512]{1,0:T(1,128)} %serve_hbm.4, s32[1,256]{1,0:T(1,128)} %bitcast.29, s32[1,128]{1,0:T(1,128)} %bitcast.31, ...), custom_call_target="tpu_custom_call" | custom-call | tf_op jit(solution)/shard_map/prepare/pallas_call | solution.py:508
  17.7 6.9 %collective-permute-done.refs_0_ = bf16[384,384]{1,0:T(8,128)(2,1)S(1)} collective-permute-done((bf16[384,384]{1,0:T(8,128)(2,1)S(1)}, bf16[384,384]{1,0:T(8,128)(2,1)S(1)}, u32[]{:S(2)}, u32[]{:S(2)}) %collective-permute-start) | collective-permute-done | bytes 294944 | tf_op jit(solution)/shard_map/ppermute | solution.py:526
  24.6 1.4 %all-to-all-done = bf16[32,16,512]{2,1,0:T(8,128)(2,1)S(1)} async-done(((bf16[32,16,512]{2,1,0:T(8,128)(2,1)}), bf16[32,16,512]{2,1,0:T(8,128)(2,1)S(1)}, u32[]{:S(2)}, u32[]{:S(2)}) %all-to-all-start) | async-done | bytes 524320 | tf_op jit(solution)/shard_map/all_to_all | solution.py:496
  26.0 1.3 %partner_rows.1 = bf16[32,72,128]{2,1,0:T(8,128)(2,1)} custom-call(bf16[512,512]{1,0:T(8,128)(2,1)S(1)} %get-tuple-element.24.swap_ref, bf16[32,8,128]{2,1,0:T(8,128)(2,1)S(1)} %get-tuple-element.27.sent_ref, bf16[512,512]{1,0:T(8,128)(2,1)S(1)} %bitcast.18), custom_call_target="tpu_custom_call" | custom-call | tf_op jit(solution)/shard_map/partner_rows/pallas_call | solution.py:508
  27.3 3.5 %all-to-all-start.1 = ((bf16[32,72,128]{2,1,0:T(8,128)(2,1)}), bf16[32,72,128]{2,1,0:T(8,128)(2,1)S(1)}, u32[]{:S(2)}, u32[]{:S(2)}) async-start(bf16[32,72,128]{2,1,0:T(8,128)(2,1)} %partner_rows.1), calls=%async_computation.1 | async-start | bytes 1179648 | tf_op jit(solution)/shard_map/all_to_all | solution.py:496
  30.8 1.8 %collective-permute-start.1 = (bf16[384,384]{1,0:T(8,128)(2,1)S(1)}, bf16[384,384]{1,0:T(8,128)(2,1)S(1)}, u32[]{:S(2)}, u32[]{:S(2)}) collective-permute-start(bf16[384,384]{1,0:T(8,128)(2,1)S(1)} %collective-permute-done.refs_0_), channel_id=1, source_target_pairs={{0,2},{1,3},{2,0},{3,1},{4,6},{5,7},{6,4},{7,5},{8,10},{9,11},{10,... | collective-permute-start | bytes 884744 | tf_op jit(solution)/shard_map/ppermute | solution.py:530
  32.6 12.3 %collective-permute-done.2.refs_2_ = bf16[916,384]{1,0:T(8,128)(2,1)S(1)} collective-permute-done((bf16[916,384]{1,0:T(8,128)(2,1)}, bf16[916,384]{1,0:T(8,128)(2,1)S(1)}, u32[]{:S(2)}, u32[]{:S(2)}) %collective-permute-start.2) | collective-permute-done | bytes 703520 | tf_op jit(solution)/shard_map/ppermute | solution.py:526
  44.9 0.5 collective-permute-done.1.refs_1_
  45.3 0.0 collective-permute-start.5
  45.3 0.5 collective-permute-start.3
  45.9 0.0 collective-permute-start.4
  46.5 1.4 %collective-permute-done.3.refs_3_ = bf16[384,384]{1,0:T(8,128)(2,1)S(1)} collective-permute-done((bf16[384,384]{1,0:T(8,128)(2,1)S(1)}, bf16[384,384]{1,0:T(8,128)(2,1)S(1)}, u32[]{:S(2)}, u32[]{:S(2)}) %collective-permute-start.3) | collective-permute-done | bytes 294944 | tf_op jit(solution)/shard_map/ppermute | solution.py:534
  47.9 0.4 collective-permute-done.4.refs_4_
  48.4 0.0 collective-permute-done.5.refs_5_
  48.4 0.0 all-to-all-done.1.message_ref
  48.4 6.0 %update_memory.1 = (bf16[256,512]{1,0:T(8,128)(2,1)}, bf16[272,512]{1,0:T(8,128)(2,1)}, bf16[896,512]{1,0:T(8,128)(2,1)}) custom-call(s32[6]{0:T(128)S(1)} %stack.27.scalar_ref, s32[1]{0:T(128)S(6)} %copy.20.hub_ref, s32[1,512]{1,0:T(1,128)} %serve_hbm.4, bf16[256,512]{1,0:T(8,128)(2,1)} %memory_hbm.3, f32[2,1536]{1,0:T(2,128)} %bias_hbm.1, ...), custom_call_target="tpu_custom_call" | custom-call | tf_op jit(solution)/shard_map/update_memory/pallas_call | solution.py:508
  54.4 3.3 %collective-permute-start.6 = (bf16[272,512]{1,0:T(8,128)(2,1)}, bf16[272,512]{1,0:T(8,128)(2,1)S(1)}, u32[]{:S(2)}, u32[]{:S(2)}) collective-permute-start(bf16[272,512]{1,0:T(8,128)(2,1)} %get-tuple-element.37.own_hbm), channel_id=1, source_target_pairs={{0,8},{8,0},{1,9},{9,1},{2,10},{10,2},{3,11},{11,3},{4,12},{12,4},... | collective-permute-start | bytes 835592 | tf_op jit(solution)/shard_map/ppermute | solution.py:538
  57.8 3.9 %all-to-all-start.2 = ((bf16[16,56,512]{2,1,0:T(8,128)(2,1)}), bf16[16,56,512]{2,1,0:T(8,128)(2,1)S(1)}, u32[]{:S(2)}, u32[]{:S(2)}) async-start(bf16[16,56,512]{2,1,0:T(8,128)(2,1)} %bitcast.20), calls=%async_computation.2 | async-start | bytes 1835008 | tf_op jit(solution)/shard_map/all_to_all | solution.py:496
  61.6 9.3 %collective-permute-done.6.other_ref = bf16[272,512]{1,0:T(8,128)(2,1)S(1)} collective-permute-done((bf16[272,512]{1,0:T(8,128)(2,1)}, bf16[272,512]{1,0:T(8,128)(2,1)S(1)}, u32[]{:S(2)}, u32[]{:S(2)}) %collective-permute-start.6) | collective-permute-done | bytes 278560 | tf_op jit(solution)/shard_map/ppermute | solution.py:538
  71.0 1.7 %far_rows.1 = bf16[16,232,128]{2,1,0:T(8,128)(2,1)} custom-call(bf16[272,512]{1,0:T(8,128)(2,1)} %get-tuple-element.37.own_hbm, bf16[272,512]{1,0:T(8,128)(2,1)S(1)} %collective-permute-done.6.other_ref), custom_call_target="tpu_custom_call" | custom-call | flops 30000001024 | tf_op jit(solution)/shard_map/far_rows/pallas_call | solution.py:508
  72.7 6.8 %all-to-all-done.2.looked_ref = bf16[16,56,512]{2,1,0:T(8,128)(2,1)S(1)} async-done(((bf16[16,56,512]{2,1,0:T(8,128)(2,1)}), bf16[16,56,512]{2,1,0:T(8,128)(2,1)S(1)}, u32[]{:S(2)}, u32[]{:S(2)}) %all-to-all-start.2) | async-done | bytes 917536 | tf_op jit(solution)/shard_map/all_to_all | solution.py:496
  79.5 3.7 %all-to-all-start.3 = ((bf16[16,232,128]{2,1,0:T(8,128)(2,1)}), bf16[16,232,128]{2,1,0:T(8,128)(2,1)S(1)}, u32[]{:S(2)}, u32[]{:S(2)}) async-start(bf16[16,232,128]{2,1,0:T(8,128)(2,1)} %far_rows.1), calls=%async_computation.3 | async-start | bytes 1900544 | tf_op jit(solution)/shard_map/all_to_all | solution.py:496
  83.2 3.6 %pick_near.1 = (bf16[896,512]{1,0:T(8,128)(2,1)S(1)}, f32[7,128]{1,0:T(8,128)S(1)}, f32[4,128]{1,0:T(4,128)S(1)}, bf16[1280,128]{1,0:T(8,128)(2,1)}, bf16[8,128]{1,0:T(8,128)(2,1)S(1)}) custom-call(s32[6]{0:T(128)S(1)} %stack.27.scalar_ref, s32[7,128]{1,0:T(8,128)} %bitcast.23, s32[4,128]{1,0:T(4,128)} %bitcast.24, s32[10,128]{1,0:T(8,128)} %bitcast.22, ...), custom_call_target="tpu_custom_call" | custom-call | tf_op jit(solution)/shard_map/pick_near/pallas_call | solution.py:508
  86.8 10.0 %all-to-all-done.3.looked_ref = bf16[16,232,128]{2,1,0:T(8,128)(2,1)S(1)} async-done(((bf16[16,232,128]{2,1,0:T(8,128)(2,1)}), bf16[16,232,128]{2,1,0:T(8,128)(2,1)S(1)}, u32[]{:S(2)}, u32[]{:S(2)}) %all-to-all-start.3) | async-done | bytes 950304 | tf_op jit(solution)/shard_map/all_to_all | solution.py:496
  96.8 4.4 %attend.1 = bf16[128,512]{1,0:T(8,128)(2,1)} custom-call(bf16[612,512]{1,0:T(8,128)(2,1)} %keyval_hbm.1, bf16[1280,128]{1,0:T(8,128)(2,1)} %get-tuple-element.32.enc_hbm, bf16[612,256]{1,0:T(8,128)(2,1)} %query_hbm.1, bf16[768,512]{1,0:T(8,128)(2,1)} %output_hbm.1, bf16[896,512]{1,0:T(8,128)(2,1)S(1)} %get-tuple-element.33.picked_ref, ...), custom_call_target="tpu_custom_call" | custom-call | tf_op jit(solution)/shard_map/attend/pallas_call | solution.py:508
Async XLA Ops:
  2.7 23.2 %all-to-all-start = ((bf16[32,16,512]{2,1,0:T(8,128)(2,1)}), bf16[32,16,512]{2,1,0:T(8,128)(2,1)S(1)}, u32[]{:S(2)}, u32[]{:S(2)}) async-start(bf16[32,16,512]{2,1,0:T(8,128)(2,1)} %bitcast.19), calls=%async_computation | async-start | bytes 1048576 | tf_op jit(solution)/shard_map/all_to_all | solution.py:496
  11.2 13.4 %collective-permute-start = (bf16[384,384]{1,0:T(8,128)(2,1)S(1)}, bf16[384,384]{1,0:T(8,128)(2,1)S(1)}, u32[]{:S(2)}, u32[]{:S(2)}) collective-permute-start(bf16[384,384]{1,0:T(8,128)(2,1)S(1)} %dynamic_slice.6), channel_id=1, source_target_pairs={{0,16},{16,0},{1,17},{17,1},{2,18},{18,2},{3,19},{19,3},{4,20},{20... | collective-permute-start | bytes 884744 | tf_op jit(solution)/shard_map/ppermute | solution.py:526
  15.1 29.8 %collective-permute-start.2 = (bf16[916,384]{1,0:T(8,128)(2,1)}, bf16[916,384]{1,0:T(8,128)(2,1)S(1)}, u32[]{:S(2)}, u32[]{:S(2)}) collective-permute-start(bf16[916,384]{1,0:T(8,128)(2,1)} %constant_dynamic-slice_fusion), channel_id=1, source_target_pairs={{0,16},{16,0},{1,17},{17,1},{2,18},{18,2},{3,19},{19,3},{4,20},{20... | collective-permute-start | bytes 2110472 | tf_op jit(solution)/shard_map/ppermute | solution.py:526
  27.3 21.1 %all-to-all-start.1 = ((bf16[32,72,128]{2,1,0:T(8,128)(2,1)}), bf16[32,72,128]{2,1,0:T(8,128)(2,1)S(1)}, u32[]{:S(2)}, u32[]{:S(2)}) async-start(bf16[32,72,128]{2,1,0:T(8,128)(2,1)} %partner_rows.1), calls=%async_computation.1 | async-start | bytes 1179648 | tf_op jit(solution)/shard_map/all_to_all | solution.py:496
  30.8 14.6 %collective-permute-start.1 = (bf16[384,384]{1,0:T(8,128)(2,1)S(1)}, bf16[384,384]{1,0:T(8,128)(2,1)S(1)}, u32[]{:S(2)}, u32[]{:S(2)}) collective-permute-start(bf16[384,384]{1,0:T(8,128)(2,1)S(1)} %collective-permute-done.refs_0_), channel_id=1, source_target_pairs={{0,2},{1,3},{2,0},{3,1},{4,6},{5,7},{6,4},{7,5},{8,10},{9,11},{10,... | collective-permute-start | bytes 884744 | tf_op jit(solution)/shard_map/ppermute | solution.py:530
  45.3 3.0 %collective-permute-start.5 = (bf16[916,384]{1,0:T(8,128)(2,1)S(1)}, bf16[916,384]{1,0:T(8,128)(2,1)S(1)}, u32[]{:S(2)}, u32[]{:S(2)}) collective-permute-start(bf16[916,384]{1,0:T(8,128)(2,1)S(1)} %collective-permute-done.2.refs_2_), channel_id=1, source_target_pairs={{0,1},{1,0},{2,3},{3,2},{4,5},{5,4},{6,7},{7,6},{8,9},{9,8},{10,11... | collective-permute-start | bytes 2110472 | tf_op jit(solution)/shard_map/ppermute | solution.py:534
  45.3 2.6 %collective-permute-start.3 = (bf16[384,384]{1,0:T(8,128)(2,1)S(1)}, bf16[384,384]{1,0:T(8,128)(2,1)S(1)}, u32[]{:S(2)}, u32[]{:S(2)}) collective-permute-start(bf16[384,384]{1,0:T(8,128)(2,1)S(1)} %collective-permute-done.refs_0_), channel_id=1, source_target_pairs={{0,1},{1,0},{2,3},{3,2},{4,5},{5,4},{6,7},{7,6},{8,9},{9,8},{10,11... | collective-permute-start | bytes 884744 | tf_op jit(solution)/shard_map/ppermute | solution.py:534
  45.9 2.5 %collective-permute-start.4 = (bf16[384,384]{1,0:T(8,128)(2,1)S(1)}, bf16[384,384]{1,0:T(8,128)(2,1)S(1)}, u32[]{:S(2)}, u32[]{:S(2)}) collective-permute-start(bf16[384,384]{1,0:T(8,128)(2,1)S(1)} %collective-permute-done.1.refs_1_), channel_id=1, source_target_pairs={{0,1},{1,0},{2,3},{3,2},{4,5},{5,4},{6,7},{7,6},{8,9},{9,8},{10,11... | collective-permute-start | bytes 884744 | tf_op jit(solution)/shard_map/ppermute | solution.py:534
  54.4 16.6 %collective-permute-start.6 = (bf16[272,512]{1,0:T(8,128)(2,1)}, bf16[272,512]{1,0:T(8,128)(2,1)S(1)}, u32[]{:S(2)}, u32[]{:S(2)}) collective-permute-start(bf16[272,512]{1,0:T(8,128)(2,1)} %get-tuple-element.37.own_hbm), channel_id=1, source_target_pairs={{0,8},{8,0},{1,9},{9,1},{2,10},{10,2},{3,11},{11,3},{4,12},{12,4},... | collective-permute-start | bytes 835592 | tf_op jit(solution)/shard_map/ppermute | solution.py:538
  57.8 21.7 %all-to-all-start.2 = ((bf16[16,56,512]{2,1,0:T(8,128)(2,1)}), bf16[16,56,512]{2,1,0:T(8,128)(2,1)S(1)}, u32[]{:S(2)}, u32[]{:S(2)}) async-start(bf16[16,56,512]{2,1,0:T(8,128)(2,1)} %bitcast.20), calls=%async_computation.2 | async-start | bytes 1835008 | tf_op jit(solution)/shard_map/all_to_all | solution.py:496
  79.5 17.3 %all-to-all-start.3 = ((bf16[16,232,128]{2,1,0:T(8,128)(2,1)}), bf16[16,232,128]{2,1,0:T(8,128)(2,1)S(1)}, u32[]{:S(2)}, u32[]{:S(2)}) async-start(bf16[16,232,128]{2,1,0:T(8,128)(2,1)} %far_rows.1), calls=%async_computation.3 | async-start | bytes 1900544 | tf_op jit(solution)/shard_map/all_to_all | solution.py:496

commit v7 on v6

--- a/solution.py
+++ b/solution.py
@@ -79,12 +79,20 @@
     return copies
 
 
-def serve_kernel(serve_hbm, memory_hbm, rows_ref, serve, memory, sems):
+def serve_kernel(serve_hbm, memory_hbm, rows_hbm, serve, memory, out, sems):
     copies = fetch([(serve_hbm, serve), (memory_hbm, memory)], sems)
     copies[0].wait()
     picks = one_hot(columns(serve[...].astype(F32)), memory.shape[0])
     copies[1].wait()
-    rows_ref[...] = dot(picks, memory[...]).astype(BF)
+    half = out.shape[0] // 2
+    sends = []
+    for n in range(2):
+        some = slice(n * half, (n + 1) * half)
+        out[some, :] = dot(picks[some, :], memory[...]).astype(BF)
+        sends.append(pltpu.make_async_copy(out.at[some, :], rows_hbm.at[some, :], sems.at[2 + n]))
+        sends[n].start()
+    for send in sends:
+        send.wait()
 
 
 def prepare_kernel(
@@ -576,14 +584,17 @@
 
     shared = cores_share(gru_weight)
     total, half = gru_weight.shape[0], gru_weight.shape[1] // 2
-    rows = call(
+    (rows,) = call(
         serve_kernel,
         "serve_endpoints",
-        sent_shape((slots, width), BF),
+        (sent_shape((slots, width), BF),),
         (),
         (update_serve, memory),
         (),
         fetched=(update_serve, memory),
+        scratch=(pltpu.VMEM((slots, width), BF),),
+        left=(0,),
+        extra_sems=2,
     )
     if shared:
         late_weight = after(gru_weight, rows)

time: 102 us -> 102 us (level)
  no operation moved by 1% of the time
where the time goes in v7:
time: 102 us; the launch traced here: 101 us
  waiting for transfers between devices  49 us (48%)
  starting transfers between devices  26.2 us (26%)
  Pallas kernels  21.3 us (21%)
  local copies, waits for them, and re-layouts  3.26 us (3%)
  between operations  1.42 us (1%)
    pallas_call x7, Pallas kernels, call(): pl.pallas_call(kernel, out_shape=out_shape, in_specs=[SMEM] * len(smem) +...  21.3 us
    ppermute x2, waiting for transfers between devices, other_ev(): return lax.ppermute(x, 'ev', [(0, 1), (1, 0)])  19.2 us
    all_to_all x4, starting transfers between devices, exchange(): return lax.all_to_all(x, axes, split_axis=0, concat_axis=0, tiled=True)  18.4 us
    all_to_all x4, waiting for transfers between devices, exchange(): return lax.all_to_all(x, axes, split_axis=0, concat_axis=0, tiled=True)  18.2 us
    ppermute x1, waiting for transfers between devices, other_half(): return lax.ppermute(x, 'hi', [(0, 1), (1, 0)])  9.34 us
    ppermute x1, starting transfers between devices, other_half(): return lax.ppermute(x, 'hi', [(0, 1), (1, 0)])  3.31 us
    ppermute x2, starting transfers between devices, other_ev(): return lax.ppermute(x, 'ev', [(0, 1), (1, 0)])  2.09 us
  transfers between devices with their start and end apart: 11, of which 9 were waited for; matrix products, arithmetic and copies ran while one was open for 3% of the time, Pallas kernels for 9%

profile of v7, /device:TPU:0, one launch (start us, length us, event | category | flops | bytes accessed | tf_op | source)
XLA Modules:
  0.0 101.2 jit_solution(15596763567205343169)
XLA Ops:
  0.6 2.1 %serve_endpoints.1 = bf16[512,512]{1,0:T(8,128)(2,1)} custom-call(s32[1,512]{1,0:T(1,128)} %serve_hbm.4, bf16[256,512]{1,0:T(8,128)(2,1)} %memory_hbm.3), custom_call_target="tpu_custom_call" | custom-call | tf_op jit(solution)/shard_map/serve_endpoints/pallas_call | solution.py:516
  2.7 7.3 %all-to-all-start = ((bf16[32,16,512]{2,1,0:T(8,128)(2,1)}), bf16[32,16,512]{2,1,0:T(8,128)(2,1)S(1)}, u32[]{:S(2)}, u32[]{:S(2)}) async-start(bf16[32,16,512]{2,1,0:T(8,128)(2,1)} %bitcast.19), calls=%async_computation | async-start | bytes 1048576 | tf_op jit(solution)/shard_map/all_to_all | solution.py:504
  10.0 1.1 %dynamic_slice.6 = bf16[384,384]{1,0:T(8,128)(2,1)S(1)} dynamic-slice(bf16[1684,768]{1,0:T(8,128)(2,1)} %own_weight_hbm.1, s32[]{:T(128)S(6)} %select_n.30, s32[]{:T(128)S(6)} %select_n.31), dynamic_slice_sizes={384,384} | dynamic-slice | bytes 589828 | tf_op jit(solution)/shard_map/dynamic_slice | solution.py:603
  11.2 1.8 %collective-permute-start = (bf16[384,384]{1,0:T(8,128)(2,1)S(1)}, bf16[384,384]{1,0:T(8,128)(2,1)S(1)}, u32[]{:S(2)}, u32[]{:S(2)}) collective-permute-start(bf16[384,384]{1,0:T(8,128)(2,1)S(1)} %dynamic_slice.6), channel_id=1, source_target_pairs={{0,16},{16,0},{1,17},{17,1},{2,18},{18,2},{3,19},{19,3},{4,20},{20... | collective-permute-start | bytes 884744 | tf_op jit(solution)/shard_map/ppermute | solution.py:534
  13.0 2.0 %constant_dynamic-slice_fusion = bf16[916,384]{1,0:T(8,128)(2,1)} fusion(bf16[1684,768]{1,0:T(8,128)(2,1)} %own_weight_hbm.1, s32[]{:T(128)S(6)} %select_n.31), kind=kLoop, calls=%fused_computation | loop fusion | bytes 1406980 | tf_op jit(solution)/shard_map/dynamic_slice | solution.py:666
  15.1 0.3 collective-permute-start.2
  15.3 0.1 stack.27.scalar_ref
  15.4 2.2 %prepare.1 = (f32[528,128]{1,0:T(8,128)S(1)}, bf16[512,512]{1,0:T(8,128)(2,1)S(1)}, bf16[32,8,128]{2,1,0:T(8,128)(2,1)S(1)}, f32[7,128]{1,0:T(8,128)S(1)}, f32[7,128]{1,0:T(8,128)S(1)}) custom-call(s32[6]{0:T(128)S(1)} %stack.27.scalar_ref, s32[1,512]{1,0:T(1,128)} %serve_hbm.4, s32[1,256]{1,0:T(1,128)} %bitcast.29, s32[1,128]{1,0:T(1,128)} %bitcast.31, ...), custom_call_target="tpu_custom_call" | custom-call | tf_op jit(solution)/shard_map/prepare/pallas_call | solution.py:516
  17.6 6.9 %collective-permute-done.refs_0_ = bf16[384,384]{1,0:T(8,128)(2,1)S(1)} collective-permute-done((bf16[384,384]{1,0:T(8,128)(2,1)S(1)}, bf16[384,384]{1,0:T(8,128)(2,1)S(1)}, u32[]{:S(2)}, u32[]{:S(2)}) %collective-permute-start) | collective-permute-done | bytes 294944 | tf_op jit(solution)/shard_map/ppermute | solution.py:534
  24.6 1.4 %all-to-all-done = bf16[32,16,512]{2,1,0:T(8,128)(2,1)S(1)} async-done(((bf16[32,16,512]{2,1,0:T(8,128)(2,1)}), bf16[32,16,512]{2,1,0:T(8,128)(2,1)S(1)}, u32[]{:S(2)}, u32[]{:S(2)}) %all-to-all-start) | async-done | bytes 524320 | tf_op jit(solution)/shard_map/all_to_all | solution.py:504
  25.9 1.3 %partner_rows.1 = bf16[32,72,128]{2,1,0:T(8,128)(2,1)} custom-call(bf16[512,512]{1,0:T(8,128)(2,1)S(1)} %get-tuple-element.24.swap_ref, bf16[32,8,128]{2,1,0:T(8,128)(2,1)S(1)} %get-tuple-element.27.sent_ref, bf16[512,512]{1,0:T(8,128)(2,1)S(1)} %bitcast.18), custom_call_target="tpu_custom_call" | custom-call | tf_op jit(solution)/shard_map/partner_rows/pallas_call | solution.py:516
  27.2 3.5 %all-to-all-start.1 = ((bf16[32,72,128]{2,1,0:T(8,128)(2,1)}), bf16[32,72,128]{2,1,0:T(8,128)(2,1)S(1)}, u32[]{:S(2)}, u32[]{:S(2)}) async-start(bf16[32,72,128]{2,1,0:T(8,128)(2,1)} %partner_rows.1), calls=%async_computation.1 | async-start | bytes 1179648 | tf_op jit(solution)/shard_map/all_to_all | solution.py:504
  30.7 1.8 %collective-permute-start.1 = (bf16[384,384]{1,0:T(8,128)(2,1)S(1)}, bf16[384,384]{1,0:T(8,128)(2,1)S(1)}, u32[]{:S(2)}, u32[]{:S(2)}) collective-permute-start(bf16[384,384]{1,0:T(8,128)(2,1)S(1)} %collective-permute-done.refs_0_), channel_id=1, source_target_pairs={{0,2},{1,3},{2,0},{3,1},{4,6},{5,7},{6,4},{7,5},{8,10},{9,11},{10,... | collective-permute-start | bytes 884744 | tf_op jit(solution)/shard_map/ppermute | solution.py:538
  32.6 12.3 %collective-permute-done.2.refs_2_ = bf16[916,384]{1,0:T(8,128)(2,1)S(1)} collective-permute-done((bf16[916,384]{1,0:T(8,128)(2,1)}, bf16[916,384]{1,0:T(8,128)(2,1)S(1)}, u32[]{:S(2)}, u32[]{:S(2)}) %collective-permute-start.2) | collective-permute-done | bytes 703520 | tf_op jit(solution)/shard_map/ppermute | solution.py:534
  44.8 0.5 collective-permute-done.1.refs_1_
  45.3 0.0 collective-permute-start.5
  45.3 0.5 collective-permute-start.3
  45.8 0.0 collective-permute-start.4
  46.5 1.4 %collective-permute-done.3.refs_3_ = bf16[384,384]{1,0:T(8,128)(2,1)S(1)} collective-permute-done((bf16[384,384]{1,0:T(8,128)(2,1)S(1)}, bf16[384,384]{1,0:T(8,128)(2,1)S(1)}, u32[]{:S(2)}, u32[]{:S(2)}) %collective-permute-start.3) | collective-permute-done | bytes 294944 | tf_op jit(solution)/shard_map/ppermute | solution.py:542
  47.9 0.4 collective-permute-done.4.refs_4_
  48.3 0.0 collective-permute-done.5.refs_5_
  48.3 0.0 all-to-all-done.1.message_ref
  48.3 6.1 %update_memory.1 = (bf16[256,512]{1,0:T(8,128)(2,1)}, bf16[272,512]{1,0:T(8,128)(2,1)}, bf16[896,512]{1,0:T(8,128)(2,1)}) custom-call(s32[6]{0:T(128)S(1)} %stack.27.scalar_ref, s32[1]{0:T(128)S(6)} %copy.20.hub_ref, s32[1,512]{1,0:T(1,128)} %serve_hbm.4, bf16[256,512]{1,0:T(8,128)(2,1)} %memory_hbm.3, f32[2,1536]{1,0:T(2,128)} %bias_hbm.1, ...), custom_call_target="tpu_custom_call" | custom-call | tf_op jit(solution)/shard_map/update_memory/pallas_call | solution.py:516
  54.4 3.3 %collective-permute-start.6 = (bf16[272,512]{1,0:T(8,128)(2,1)}, bf16[272,512]{1,0:T(8,128)(2,1)S(1)}, u32[]{:S(2)}, u32[]{:S(2)}) collective-permute-start(bf16[272,512]{1,0:T(8,128)(2,1)} %get-tuple-element.37.own_hbm), channel_id=1, source_target_pairs={{0,8},{8,0},{1,9},{9,1},{2,10},{10,2},{3,11},{11,3},{4,12},{12,4},... | collective-permute-start | bytes 835592 | tf_op jit(solution)/shard_map/ppermute | solution.py:546
  57.7 3.9 %all-to-all-start.2 = ((bf16[16,56,512]{2,1,0:T(8,128)(2,1)}), bf16[16,56,512]{2,1,0:T(8,128)(2,1)S(1)}, u32[]{:S(2)}, u32[]{:S(2)}) async-start(bf16[16,56,512]{2,1,0:T(8,128)(2,1)} %bitcast.20), calls=%async_computation.2 | async-start | bytes 1835008 | tf_op jit(solution)/shard_map/all_to_all | solution.py:504
  61.6 9.3 %collective-permute-done.6.other_ref = bf16[272,512]{1,0:T(8,128)(2,1)S(1)} collective-permute-done((bf16[272,512]{1,0:T(8,128)(2,1)}, bf16[272,512]{1,0:T(8,128)(2,1)S(1)}, u32[]{:S(2)}, u32[]{:S(2)}) %collective-permute-start.6) | collective-permute-done | bytes 278560 | tf_op jit(solution)/shard_map/ppermute | solution.py:546
  71.0 1.7 %far_rows.1 = bf16[16,232,128]{2,1,0:T(8,128)(2,1)} custom-call(bf16[272,512]{1,0:T(8,128)(2,1)} %get-tuple-element.37.own_hbm, bf16[272,512]{1,0:T(8,128)(2,1)S(1)} %collective-permute-done.6.other_ref), custom_call_target="tpu_custom_call" | custom-call | flops 30000001024 | tf_op jit(solution)/shard_map/far_rows/pallas_call | solution.py:516
  72.7 6.8 %all-to-all-done.2.looked_ref = bf16[16,56,512]{2,1,0:T(8,128)(2,1)S(1)} async-done(((bf16[16,56,512]{2,1,0:T(8,128)(2,1)}), bf16[16,56,512]{2,1,0:T(8,128)(2,1)S(1)}, u32[]{:S(2)}, u32[]{:S(2)}) %all-to-all-start.2) | async-done | bytes 917536 | tf_op jit(solution)/shard_map/all_to_all | solution.py:504
  79.4 3.7 %all-to-all-start.3 = ((bf16[16,232,128]{2,1,0:T(8,128)(2,1)}), bf16[16,232,128]{2,1,0:T(8,128)(2,1)S(1)}, u32[]{:S(2)}, u32[]{:S(2)}) async-start(bf16[16,232,128]{2,1,0:T(8,128)(2,1)} %far_rows.1), calls=%async_computation.3 | async-start | bytes 1900544 | tf_op jit(solution)/shard_map/all_to_all | solution.py:504
  83.2 3.6 %pick_near.1 = (bf16[896,512]{1,0:T(8,128)(2,1)S(1)}, f32[7,128]{1,0:T(8,128)S(1)}, f32[4,128]{1,0:T(4,128)S(1)}, bf16[1280,128]{1,0:T(8,128)(2,1)}, bf16[8,128]{1,0:T(8,128)(2,1)S(1)}) custom-call(s32[6]{0:T(128)S(1)} %stack.27.scalar_ref, s32[7,128]{1,0:T(8,128)} %bitcast.23, s32[4,128]{1,0:T(4,128)} %bitcast.24, s32[10,128]{1,0:T(8,128)} %bitcast.22, ...), custom_call_target="tpu_custom_call" | custom-call | tf_op jit(solution)/shard_map/pick_near/pallas_call | solution.py:516
  86.7 10.0 %all-to-all-done.3.looked_ref = bf16[16,232,128]{2,1,0:T(8,128)(2,1)S(1)} async-done(((bf16[16,232,128]{2,1,0:T(8,128)(2,1)}), bf16[16,232,128]{2,1,0:T(8,128)(2,1)S(1)}, u32[]{:S(2)}, u32[]{:S(2)}) %all-to-all-start.3) | async-done | bytes 950304 | tf_op jit(solution)/shard_map/all_to_all | solution.py:504
  96.7 4.4 %attend.1 = bf16[128,512]{1,0:T(8,128)(2,1)} custom-call(bf16[612,512]{1,0:T(8,128)(2,1)} %keyval_hbm.1, bf16[1280,128]{1,0:T(8,128)(2,1)} %get-tuple-element.32.enc_hbm, bf16[612,256]{1,0:T(8,128)(2,1)} %query_hbm.1, bf16[768,512]{1,0:T(8,128)(2,1)} %output_hbm.1, bf16[896,512]{1,0:T(8,128)(2,1)S(1)} %get-tuple-element.33.picked_ref, ...), custom_call_target="tpu_custom_call" | custom-call | tf_op jit(solution)/shard_map/attend/pallas_call | solution.py:516
Async XLA Ops:
  2.7 23.2 %all-to-all-start = ((bf16[32,16,512]{2,1,0:T(8,128)(2,1)}), bf16[32,16,512]{2,1,0:T(8,128)(2,1)S(1)}, u32[]{:S(2)}, u32[]{:S(2)}) async-start(bf16[32,16,512]{2,1,0:T(8,128)(2,1)} %bitcast.19), calls=%async_computation | async-start | bytes 1048576 | tf_op jit(solution)/shard_map/all_to_all | solution.py:504
  11.2 13.4 %collective-permute-start = (bf16[384,384]{1,0:T(8,128)(2,1)S(1)}, bf16[384,384]{1,0:T(8,128)(2,1)S(1)}, u32[]{:S(2)}, u32[]{:S(2)}) collective-permute-start(bf16[384,384]{1,0:T(8,128)(2,1)S(1)} %dynamic_slice.6), channel_id=1, source_target_pairs={{0,16},{16,0},{1,17},{17,1},{2,18},{18,2},{3,19},{19,3},{4,20},{20... | collective-permute-start | bytes 884744 | tf_op jit(solution)/shard_map/ppermute | solution.py:534
  15.1 29.8 %collective-permute-start.2 = (bf16[916,384]{1,0:T(8,128)(2,1)}, bf16[916,384]{1,0:T(8,128)(2,1)S(1)}, u32[]{:S(2)}, u32[]{:S(2)}) collective-permute-start(bf16[916,384]{1,0:T(8,128)(2,1)} %constant_dynamic-slice_fusion), channel_id=1, source_target_pairs={{0,16},{16,0},{1,17},{17,1},{2,18},{18,2},{3,19},{19,3},{4,20},{20... | collective-permute-start | bytes 2110472 | tf_op jit(solution)/shard_map/ppermute | solution.py:534
  27.2 21.1 %all-to-all-start.1 = ((bf16[32,72,128]{2,1,0:T(8,128)(2,1)}), bf16[32,72,128]{2,1,0:T(8,128)(2,1)S(1)}, u32[]{:S(2)}, u32[]{:S(2)}) async-start(bf16[32,72,128]{2,1,0:T(8,128)(2,1)} %partner_rows.1), calls=%async_computation.1 | async-start | bytes 1179648 | tf_op jit(solution)/shard_map/all_to_all | solution.py:504
  30.7 14.6 %collective-permute-start.1 = (bf16[384,384]{1,0:T(8,128)(2,1)S(1)}, bf16[384,384]{1,0:T(8,128)(2,1)S(1)}, u32[]{:S(2)}, u32[]{:S(2)}) collective-permute-start(bf16[384,384]{1,0:T(8,128)(2,1)S(1)} %collective-permute-done.refs_0_), channel_id=1, source_target_pairs={{0,2},{1,3},{2,0},{3,1},{4,6},{5,7},{6,4},{7,5},{8,10},{9,11},{10,... | collective-permute-start | bytes 884744 | tf_op jit(solution)/shard_map/ppermute | solution.py:538
  45.3 3.0 %collective-permute-start.5 = (bf16[916,384]{1,0:T(8,128)(2,1)S(1)}, bf16[916,384]{1,0:T(8,128)(2,1)S(1)}, u32[]{:S(2)}, u32[]{:S(2)}) collective-permute-start(bf16[916,384]{1,0:T(8,128)(2,1)S(1)} %collective-permute-done.2.refs_2_), channel_id=1, source_target_pairs={{0,1},{1,0},{2,3},{3,2},{4,5},{5,4},{6,7},{7,6},{8,9},{9,8},{10,11... | collective-permute-start | bytes 2110472 | tf_op jit(solution)/shard_map/ppermute | solution.py:542
  45.3 2.6 %collective-permute-start.3 = (bf16[384,384]{1,0:T(8,128)(2,1)S(1)}, bf16[384,384]{1,0:T(8,128)(2,1)S(1)}, u32[]{:S(2)}, u32[]{:S(2)}) collective-permute-start(bf16[384,384]{1,0:T(8,128)(2,1)S(1)} %collective-permute-done.refs_0_), channel_id=1, source_target_pairs={{0,1},{1,0},{2,3},{3,2},{4,5},{5,4},{6,7},{7,6},{8,9},{9,8},{10,11... | collective-permute-start | bytes 884744 | tf_op jit(solution)/shard_map/ppermute | solution.py:542
  45.8 2.5 %collective-permute-start.4 = (bf16[384,384]{1,0:T(8,128)(2,1)S(1)}, bf16[384,384]{1,0:T(8,128)(2,1)S(1)}, u32[]{:S(2)}, u32[]{:S(2)}) collective-permute-start(bf16[384,384]{1,0:T(8,128)(2,1)S(1)} %collective-permute-done.1.refs_1_), channel_id=1, source_target_pairs={{0,1},{1,0},{2,3},{3,2},{4,5},{5,4},{6,7},{7,6},{8,9},{9,8},{10,11... | collective-permute-start | bytes 884744 | tf_op jit(solution)/shard_map/ppermute | solution.py:542
  54.4 16.6 %collective-permute-start.6 = (bf16[272,512]{1,0:T(8,128)(2,1)}, bf16[272,512]{1,0:T(8,128)(2,1)S(1)}, u32[]{:S(2)}, u32[]{:S(2)}) collective-permute-start(bf16[272,512]{1,0:T(8,128)(2,1)} %get-tuple-element.37.own_hbm), channel_id=1, source_target_pairs={{0,8},{8,0},{1,9},{9,1},{2,10},{10,2},{3,11},{11,3},{4,12},{12,4},... | collective-permute-start | bytes 835592 | tf_op jit(solution)/shard_map/ppermute | solution.py:546
  57.7 21.7 %all-to-all-start.2 = ((bf16[16,56,512]{2,1,0:T(8,128)(2,1)}), bf16[16,56,512]{2,1,0:T(8,128)(2,1)S(1)}, u32[]{:S(2)}, u32[]{:S(2)}) async-start(bf16[16,56,512]{2,1,0:T(8,128)(2,1)} %bitcast.20), calls=%async_computation.2 | async-start | bytes 1835008 | tf_op jit(solution)/shard_map/all_to_all | solution.py:504
  79.4 17.3 %all-to-all-start.3 = ((bf16[16,232,128]{2,1,0:T(8,128)(2,1)}), bf16[16,232,128]{2,1,0:T(8,128)(2,1)S(1)}, u32[]{:S(2)}, u32[]{:S(2)}) async-start(bf16[16,232,128]{2,1,0:T(8,128)(2,1)} %far_rows.1), calls=%async_computation.3 | async-start | bytes 1900544 | tf_op jit(solution)/shard_map/all_to_all | solution.py:504
